TPU v7x, 128 devices: a whole 4x4x4 slice. The times are simulated.
128 devices in a mesh: tile: 8 (over x, core), slab: 16 (over y, z).
Axes of the slice: x: 4, y: 4, z: 4, core: 2. Of those that a mesh axis runs over, the one named last changes fastest.
Arguments:
- pre_conv: bfloat16 [256, 32, 32, 512], P(('tile', 'slab')), may hold values from -6 to 6
- conv_weight: bfloat16 [4608, 1024], replicated, may hold values from -0.09375 to 0.09375
- proj_weight: bfloat16 [1024, 1280], replicated, may hold values from -0.1875 to 0.1875
- norm_gain: float32 [1280], replicated, may hold values from 0.25 to 1.75
- slab_cotangent: bfloat16 [131072, 1280], P(('tile', 'slab')), may hold values from -0.079589844 to 0.079589844
- page_tiles: int32 [128], P(('tile', 'slab')), may hold values from 1 to 2
- block_dest: int32 [1024, 1], P(('tile', 'slab')), may hold values from 0 to 15; in each aligned block of 8 rows (0 to 7, 8 to 15, ...) no two rows name the same one
Outputs:
- grad_conv: float32 [4608, 1024], P(('tile', 'slab'))
- grad_proj: float32 [1024, 1280], P(('tile', 'slab'))
- grad_gain: float32 [1280], replicated
Inputs may be any that keep to these rules, and one draw needn't show every extreme that they name: The live tiles of a device are its first page_tiles ones. `block_dest`: the 8 blocks of one device name different slabs, so each slab receives at most one block from each device of its group.
All inputs are finite; a program needn't handle non-finite values.
Results may differ from a plain program's by a relative error of at most 0.0041.
Values may be sent and summed in bfloat16 or wider, within the bound.
No kernel may reach another device: no remote copies, remote signals or barrier semaphores. Data moves between devices by JAX's collectives and lax.ppermute only.
A program may use at most 128 MiB of HBM per device.

v0:
```python
import jax
import jax.numpy as jnp
from jax import lax
from jax.sharding import PartitionSpec as P

epsilon = 1e-06


def patches(tile_input):
    grid_side = tile_input.shape[0]
    padded = jnp.pad(tile_input, ((1, 1), (1, 1), (0, 0)))
    pieces = [
        padded[row_off : row_off + grid_side : 2, col_off : col_off + grid_side : 2, :]
        for row_off in range(3)
        for col_off in range(3)
    ]
    stacked = jnp.concatenate(pieces, axis=-1)
    return stacked.reshape(-1, stacked.shape[-1])


def norm_backward(values, cotangent, norm_gain):
    cot_float = cotangent.astype(jnp.float32)
    mean_square = jnp.mean(values * values, axis=-1, keepdims=True)
    scale_inv = lax.rsqrt(mean_square + epsilon)
    upstream = cot_float * norm_gain
    inner = jnp.mean(upstream * values, axis=-1, keepdims=True)
    grad_values = (scale_inv * upstream - values * scale_inv**3 * inner).astype(jnp.bfloat16)
    gain_terms = jnp.sum(cot_float * values * scale_inv, axis=(0, 1))
    return (grad_values, gain_terms)


def per_device(
    pre_conv, conv_weight, proj_weight, norm_gain, slab_cotangent, page_tiles, block_dest
):
    tiles_here = pre_conv.shape[0]
    out_width = conv_weight.shape[1]
    model_width = proj_weight.shape[1]
    slab_count = lax.axis_size("slab")
    block_rows = slab_cotangent.shape[0] // slab_count
    is_live = jnp.arange(tiles_here) < page_tiles[0]
    patch_rows = jax.vmap(patches)(pre_conv)
    features = jnp.einsum(
        "tpk,kc->tpc", patch_rows, conv_weight, preferred_element_type=jnp.float32
    ).astype(jnp.bfloat16)
    features = jnp.where(is_live[:, None, None], features, jnp.zeros_like(features))
    blocks = features.reshape(-1, block_rows, out_width)
    targets = block_dest[:, 0]
    cotangent = slab_cotangent.reshape(slab_count, block_rows, model_width)
    projected = jnp.einsum("brc,cw->brw", blocks, proj_weight, preferred_element_type=jnp.float32)
    outgoing = (
        jnp.zeros((slab_count, block_rows, model_width), jnp.float32).at[targets].set(projected)
    )
    received = lax.all_to_all(outgoing, "slab", split_axis=0, concat_axis=0, tiled=True)
    grad_slab, gain_terms = norm_backward(received, cotangent, norm_gain)
    returned = lax.all_to_all(grad_slab, "slab", split_axis=0, concat_axis=0, tiled=True)
    grad_own = returned[targets]
    left_rows = blocks.reshape(-1, out_width)
    right_rows = grad_own.reshape(-1, model_width)
    grad_blocks = jnp.einsum(
        "brw,cw->brc", grad_own, proj_weight, preferred_element_type=jnp.float32
    ).astype(jnp.bfloat16)
    column_part = left_rows
    grad_proj = lax.psum_scatter(
        jnp.einsum("rc,rw->cw", column_part, right_rows, preferred_element_type=jnp.float32),
        ("tile", "slab"),
        scatter_dimension=0,
        tiled=True,
    )
    grad_input = grad_blocks.reshape(tiles_here, -1, out_width)
    grad_input = jnp.where(is_live[:, None, None], grad_input, jnp.zeros_like(grad_input))
    column_part = patch_rows
    grad_conv = lax.psum_scatter(
        jnp.einsum("tpk,tpc->kc", column_part, grad_input, preferred_element_type=jnp.float32),
        ("tile", "slab"),
        scatter_dimension=0,
        tiled=True,
    )
    grad_gain = lax.psum(gain_terms, ("tile", "slab"))
    return (grad_conv, grad_proj, grad_gain)


def solution(mesh):
    return jax.shard_map(
        per_device,
        mesh=mesh,
        in_specs=(
            P(("tile", "slab"), None, None, None),
            P(),
            P(),
            P(),
            P(("tile", "slab"), None),
            P(("tile", "slab")),
            P(("tile", "slab"), None),
        ),
        out_specs=(P(("tile", "slab"), None), P(("tile", "slab"), None), P()),
        check_vma=False,
    )
```

profile of v0, /device:TPU:0, one launch (start us, length us, event | category | flops | bytes accessed | tf_op | source)
XLA Modules:
  0.0 966.9 jit_solution(17315604862166485376)
XLA Ops:
  7.2 0.0 copy-start
  7.2 4.7 pad.4
  11.8 16.4 %slice.27 = bf16[2,16,16,512]{3,2,1,0:T(8,128)(2,1)} slice(bf16[2,34,34,512]{3,2,1,0:T(8,128)(2,1)} %pad.4), slice={[0:2:1], [0:32:2], [0:32:2], [0:512:1]} | slice | bytes 1048576 | tf_op jit(solution)/shard_map/vmap()/slice | solution.py:13
  28.2 16.4 %slice.28 = bf16[2,16,16,512]{3,2,1,0:T(8,128)(2,1)} slice(bf16[2,34,34,512]{3,2,1,0:T(8,128)(2,1)} %pad.4), slice={[0:2:1], [0:32:2], [1:33:2], [0:512:1]} | slice | bytes 1048576 | tf_op jit(solution)/shard_map/vmap()/slice | solution.py:13
  44.6 17.1 %slice.29 = bf16[2,16,16,512]{3,2,1,0:T(8,128)(2,1)} slice(bf16[2,34,34,512]{3,2,1,0:T(8,128)(2,1)} %pad.4), slice={[0:2:1], [0:32:2], [2:34:2], [0:512:1]} | slice | bytes 1048576 | tf_op jit(solution)/shard_map/vmap()/slice | solution.py:13
  61.7 16.4 %slice.30 = bf16[2,16,16,512]{3,2,1,0:T(8,128)(2,1)} slice(bf16[2,34,34,512]{3,2,1,0:T(8,128)(2,1)} %pad.4), slice={[0:2:1], [1:33:2], [0:32:2], [0:512:1]} | slice | bytes 1048576 | tf_op jit(solution)/shard_map/vmap()/slice | solution.py:13
  78.1 16.4 %slice.31 = bf16[2,16,16,512]{3,2,1,0:T(8,128)(2,1)} slice(bf16[2,34,34,512]{3,2,1,0:T(8,128)(2,1)} %pad.4), slice={[0:2:1], [1:33:2], [1:33:2], [0:512:1]} | slice | bytes 1048576 | tf_op jit(solution)/shard_map/vmap()/slice | solution.py:13
  94.5 17.1 %slice.32 = bf16[2,16,16,512]{3,2,1,0:T(8,128)(2,1)} slice(bf16[2,34,34,512]{3,2,1,0:T(8,128)(2,1)} %pad.4), slice={[0:2:1], [1:33:2], [2:34:2], [0:512:1]} | slice | bytes 1048576 | tf_op jit(solution)/shard_map/vmap()/slice | solution.py:13
  111.5 16.4 %slice.33 = bf16[2,16,16,512]{3,2,1,0:T(8,128)(2,1)} slice(bf16[2,34,34,512]{3,2,1,0:T(8,128)(2,1)} %pad.4), slice={[0:2:1], [2:34:2], [0:32:2], [0:512:1]} | slice | bytes 1048576 | tf_op jit(solution)/shard_map/vmap()/slice | solution.py:13
  127.9 16.4 %slice.34 = bf16[2,16,16,512]{3,2,1,0:T(8,128)(2,1)} slice(bf16[2,34,34,512]{3,2,1,0:T(8,128)(2,1)} %pad.4), slice={[0:2:1], [2:34:2], [1:33:2], [0:512:1]} | slice | bytes 1048576 | tf_op jit(solution)/shard_map/vmap()/slice | solution.py:13
  144.3 14.9 %slice.35 = bf16[2,16,16,512]{3,2,1,0:T(8,128)(2,1)S(1)} slice(bf16[2,34,34,512]{3,2,1,0:T(8,128)(2,1)} %pad.4), slice={[0:2:1], [2:34:2], [2:34:2], [0:512:1]} | slice | bytes 1048576 | tf_op jit(solution)/shard_map/vmap()/slice | solution.py:13
  159.2 1.2 constant_dynamic-update-slice_fusion.8
  161.1 1.1 constant_dynamic-update-slice_fusion.7
  162.2 1.1 constant_dynamic-update-slice_fusion.6
  163.3 1.1 constant_dynamic-update-slice_fusion.5
  164.3 1.1 constant_dynamic-update-slice_fusion.4
  165.6 9.5 fusion.20
  175.2 3.0 fusion.12
  178.2 2.8 broadcast_in_dim.22
  181.1 4.7 scatter_fusion
  185.8 70.3 %all_to_all.10 = f32[16,64,1280]{2,1,0:T(8,128)S(1)} all-to-all(f32[16,64,1280]{2,1,0:T(8,128)} %scatter_fusion), channel_id=1, replica_groups=mesh['tile'=8,'slab'=16] {'slab'}, dimensions={0} | all-to-all | bytes 10485760 | tf_op jit(solution)/shard_map/all_to_all | solution.py:53
  256.1 0.4 multiply_reduce_fusion
  256.5 1.3 copy-done.1
  257.9 1.6 fusion.9
  259.5 2.3 fusion.6
  261.8 4.5 all-to-all-start.1
  266.2 0.2 reduce-scatter.4.cloned.1.call-start
  266.5 34.1 %all-to-all-done.1 = bf16[16,64,1280]{2,1,0:T(8,128)(2,1)} async-done(((bf16[16,64,1280]{2,1,0:T(8,128)(2,1)}), bf16[16,64,1280]{2,1,0:T(8,128)(2,1)}, u32[]{:S(2)}, u32[]{:S(2)}) %all-to-all-start.1) | async-done | bytes 2621472 | tf_op jit(solution)/shard_map/all_to_all | solution.py:55
  300.6 3.4 gather_fusion
  304.0 5.5 fusion.24
  309.5 0.0 reduce-scatter.4.cloned.1.call-update
  309.6 0.0 slice-start.1
  309.6 3.0 fusion.17
  312.6 0.1 bitcast_select_fusion
  312.8 9.2 convolution_bitcast_fusion
  321.9 367.5 %fusion = f32[40,1024]{1,0:T(8,128)S(1)} fusion(f32[4608,1024]{1,0:T(8,128)} %convolution_bitcast_fusion), kind=kCustom, calls=%all-reduce-scatter | all-reduce-scatter fusion | flops 5242881 | bytes 19038208
  689.4 3.0 collective-permute-start
  692.4 1.3 collective-permute-start.1
  693.7 2.0 collective-permute-start.12
  695.7 1.3 collective-permute-start.10
  697.0 1.3 collective-permute-start.11
  698.3 0.0 collective-permute-done.12
  698.3 1.3 collective-permute-start.2
  699.6 0.0 collective-permute-done
  699.6 1.3 collective-permute-start.3
  700.9 0.0 collective-permute-done.1
  701.0 1.3 collective-permute-start.4
  702.3 0.0 collective-permute-done.10
  702.3 11.5 %collective-permute-start.5 = (f32[40,1024]{1,0:T(8,128)S(1)}, f32[40,1024]{1,0:T(8,128)}, u32[]{:S(2)}, u32[]{:S(2)}) collective-permute-start(f32[40,1024]{1,0:T(8,128)S(1)} %fusion), channel_id=1, source_target_pairs={{0,6},{1,7},{2,8},{3,9},{4,10},{5,11},{6,12},{7,13},{8,14},{9,15},... | collective-permute-start | bytes 491528
  713.8 0.0 collective-permute-done.11
  713.8 2.0 collective-permute-start.6
  715.8 0.0 collective-permute-done.2
  715.8 1.9 collective-permute-start.7
  717.8 0.0 collective-permute-done.3
  717.8 2.0 collective-permute-start.8
  719.7 2.7 collective-permute-start.9
  722.4 79.7 %psum.7 = f32[1280]{0:T(1024)} all-reduce(f32[1280]{0:T(1024)S(1)} %get-tuple-element.3), channel_id=1, replica_groups=mesh['tile'=8,'slab'=16] {'tile','slab'}, use_global_device_ids=true, to_apply=%region_6.7 | all-reduce | flops 1280 | bytes 10240 | tf_op jit(solution)/shard_map/psum | solution.py:78
  802.2 0.0 collective-permute-done.5
  802.2 0.0 collective-permute-done.6
  802.2 0.0 collective-permute-done.7
  802.2 0.0 collective-permute-done.8
  802.2 22.1 %concatenate.4 = f32[548,1024]{1,0:T(8,128)} concatenate(f32[28,1024]{1,0:T(8,128)} %collective-permute-done.12, f32[40,1024]{1,0:T(8,128)S(1)} %collective-permute-done.11, f32[40,1024]{1,0:T(8,128)S(1)} %collective-permute-done.10, f32[40,1024]{1,0:T(8,128)} %collective-permute-done.9, f32[40,1024]{1,0:T(8,128)} %collective-permute-done.8, f32[40,1024]{1,0:T(8,128)} %collective-permute-done.7, ...), dimensions={0} | concatenate | bytes 4489216
  824.3 1.6 constant_dynamic-slice_fusion
  826.0 134.1 %reduce-scatter.4.cloned.1.call-done = f32[8,1280]{1,0:T(8,128)} async-done(((f32[1024,1280]{1,0:T(8,128)}), f32[8,1280]{1,0:T(8,128)}) %reduce-scatter.4.cloned.1.call-update) | async-done | bytes 40976 | tf_op jit(solution)/shard_map/reduce_scatter | solution.py:63
  (38 shorter events, 0.2 us)
Async XLA Ops:
  7.2 168.0 %copy-start = (bf16[1024,1280]{1,0:T(8,128)(2,1)S(1)}, bf16[1024,1280]{1,0:T(8,128)(2,1)}, u32[]{:S(2)}) copy-start(bf16[1024,1280]{1,0:T(8,128)(2,1)} %param.9) | copy-start | bytes 7864324
  28.2 132.9 %copy-start.11 = (s32[8,1]{0,1:T(1,128)S(1)}, s32[8,1]{0,1:T(1,128)}, u32[]{:S(2)}) copy-start(s32[8,1]{0,1:T(1,128)} %param.13) | copy-start | bytes 100
  159.2 6.2 copy-start.4
  159.2 6.3 copy-start.3
  159.2 6.3 copy-start.2
  165.6 9.5 copy-start.9
  175.2 3.0 copy-start.5
  256.1 1.7 copy-start.1
  256.1 1.7 copy-start.10
  261.8 38.8 %all-to-all-start.1 = ((bf16[16,64,1280]{2,1,0:T(8,128)(2,1)}), bf16[16,64,1280]{2,1,0:T(8,128)(2,1)}, u32[]{:S(2)}, u32[]{:S(2)}) async-start(bf16[16,64,1280]{2,1,0:T(8,128)(2,1)} %fusion.6), calls=%async_computation.1 | async-start | bytes 5242880 | tf_op jit(solution)/shard_map/all_to_all | solution.py:55
  266.2 693.8 %reduce-scatter.4.cloned.1.call-start = ((), (), s32[]{:S(2)}) async-start(), calls=%async_computation.3 | async-start | bytes 5283840 | tf_op jit(solution)/shard_map/reduce_scatter | solution.py:63
  309.5 3.2 slice-start
  309.6 3.2 slice-start.1
  689.4 10.2 %collective-permute-start = (f32[40,1024]{1,0:T(8,128)S(1)}, f32[40,1024]{1,0:T(8,128)S(1)}, u32[]{:S(2)}, u32[]{:S(2)}) collective-permute-start(f32[40,1024]{1,0:T(8,128)S(1)} %fusion), channel_id=1, source_target_pairs={{0,1},{1,2},{2,3},{3,4},{4,5},{5,6},{6,7},{7,8},{8,9},{9,10},{10,1... | collective-permute-start | bytes 491528
  692.4 8.5 collective-permute-start.1
  693.7 4.6 collective-permute-start.12
  695.7 6.6 collective-permute-start.10
  697.0 16.8 %collective-permute-start.11 = (f32[40,1024]{1,0:T(8,128)S(1)}, f32[40,1024]{1,0:T(8,128)S(1)}, u32[]{:S(2)}, u32[]{:S(2)}) collective-permute-start(f32[40,1024]{1,0:T(8,128)S(1)} %fusion), channel_id=1, source_target_pairs={{0,12},{1,13},{2,14},{3,15},{4,16},{5,17},{6,18},{7,19},{8,20},{9,... | collective-permute-start | bytes 491528
  698.3 17.5 %collective-permute-start.2 = (f32[40,1024]{1,0:T(8,128)S(1)}, f32[40,1024]{1,0:T(8,128)S(1)}, u32[]{:S(2)}, u32[]{:S(2)}) collective-permute-start(f32[40,1024]{1,0:T(8,128)S(1)} %fusion), channel_id=1, source_target_pairs={{0,3},{1,4},{2,5},{3,6},{4,7},{5,8},{6,9},{7,10},{8,11},{9,12},{10... | collective-permute-start | bytes 491528
  699.6 18.1 %collective-permute-start.3 = (f32[40,1024]{1,0:T(8,128)S(1)}, f32[40,1024]{1,0:T(8,128)S(1)}, u32[]{:S(2)}, u32[]{:S(2)}) collective-permute-start(f32[40,1024]{1,0:T(8,128)S(1)} %fusion), channel_id=1, source_target_pairs={{0,4},{1,5},{2,6},{3,7},{4,8},{5,9},{6,10},{7,11},{8,12},{9,13},{1... | collective-permute-start | bytes 491528
  701.0 18.8 %collective-permute-start.4 = (f32[40,1024]{1,0:T(8,128)S(1)}, f32[40,1024]{1,0:T(8,128)S(1)}, u32[]{:S(2)}, u32[]{:S(2)}) collective-permute-start(f32[40,1024]{1,0:T(8,128)S(1)} %fusion), channel_id=1, source_target_pairs={{0,5},{1,6},{2,7},{3,8},{4,9},{5,10},{6,11},{7,12},{8,13},{9,14},{... | collective-permute-start | bytes 491528
  702.3 99.9 %collective-permute-start.5 = (f32[40,1024]{1,0:T(8,128)S(1)}, f32[40,1024]{1,0:T(8,128)}, u32[]{:S(2)}, u32[]{:S(2)}) collective-permute-start(f32[40,1024]{1,0:T(8,128)S(1)} %fusion), channel_id=1, source_target_pairs={{0,6},{1,7},{2,8},{3,9},{4,10},{5,11},{6,12},{7,13},{8,14},{9,15},... | collective-permute-start | bytes 491528
  713.8 88.3 %collective-permute-start.6 = (f32[40,1024]{1,0:T(8,128)S(1)}, f32[40,1024]{1,0:T(8,128)}, u32[]{:S(2)}, u32[]{:S(2)}) collective-permute-start(f32[40,1024]{1,0:T(8,128)S(1)} %fusion), channel_id=1, source_target_pairs={{0,7},{1,8},{2,9},{3,10},{4,11},{5,12},{6,13},{7,14},{8,15},{9,16}... | collective-permute-start | bytes 491528
  715.8 3.9 copy-start.6
  715.8 86.4 %collective-permute-start.7 = (f32[40,1024]{1,0:T(8,128)S(1)}, f32[40,1024]{1,0:T(8,128)}, u32[]{:S(2)}, u32[]{:S(2)}) collective-permute-start(f32[40,1024]{1,0:T(8,128)S(1)} %fusion), channel_id=1, source_target_pairs={{0,8},{1,9},{2,10},{3,11},{4,12},{5,13},{6,14},{7,15},{8,16},{9,17... | collective-permute-start | bytes 491528
  717.8 4.7 copy-start.7
  717.8 84.4 %collective-permute-start.8 = (f32[40,1024]{1,0:T(8,128)S(1)}, f32[40,1024]{1,0:T(8,128)}, u32[]{:S(2)}, u32[]{:S(2)}) collective-permute-start(f32[40,1024]{1,0:T(8,128)S(1)} %fusion), channel_id=1, source_target_pairs={{0,9},{1,10},{2,11},{3,12},{4,13},{5,14},{6,15},{7,16},{8,17},{9,1... | collective-permute-start | bytes 491528
  719.7 2.7 copy-start.8
  719.7 82.5 %collective-permute-start.9 = (f32[40,1024]{1,0:T(8,128)S(1)}, f32[40,1024]{1,0:T(8,128)}, u32[]{:S(2)}, u32[]{:S(2)}) collective-permute-start(f32[40,1024]{1,0:T(8,128)S(1)} %fusion), channel_id=1, source_target_pairs={{0,10},{1,11},{2,12},{3,13},{4,14},{5,15},{6,16},{7,17},{8,18},{9,... | collective-permute-start | bytes 491528
Sparse Core Ops, SparseCore 0:
  309.7 650.3 reduce-scatter.3
where the time goes:
time: 978 us; the launch traced here: 967 us
  blocking collectives  518 us (53%)
  local copies, waits for them, and re-layouts  194 us (20%)
  waiting for transfers between devices  168 us (17%)
  starting transfers between devices  37.6 us (4%)
  matrix products  30.2 us (3%)
  between operations  15.1 us (2%)
    unnamed x1, blocking collectives  367 us
    slice x9, local copies, waits for them, and re-layouts, patches(): padded[row_off:row_off + grid_side:2, col_off:col_off + grid_side:2, :]  147 us
    reduce_scatter x1, waiting for transfers between devices, per_device(): lax.psum_scatter(jnp.einsum('rc,rw->cw', column_part, right_rows, preferr...  134 us
    psum x1, blocking collectives, per_device(): grad_gain = lax.psum(gain_terms, ('tile', 'slab'))  79.7 us
    all_to_all x1, blocking collectives, per_device(): lax.all_to_all(outgoing, 'slab', split_axis=0, concat_axis=0, tiled=True)  70.3 us
    all_to_all x1, waiting for transfers between devices, per_device(): lax.all_to_all(grad_slab, 'slab', split_axis=0, concat_axis=0, tiled=True)  34.1 us
    unnamed x13, starting transfers between devices  32.9 us
    unnamed x39, local copies, waits for them, and re-layouts  30.7 us
  transfers between devices with their start and end apart: 15, of which 2 were waited for; matrix products, arithmetic and copies ran while one was open for 42% of the time, Pallas kernels for 0%

commit v1 on v0

v1 whole, which is shorter than its diff:
```python
import functools

import jax
import jax.numpy as jnp
from jax import lax
from jax.experimental import pallas as pl
from jax.experimental.pallas import tpu as pltpu
from jax.sharding import Mesh
from jax.sharding import PartitionSpec as P

EPS = 1e-6
BF = jnp.bfloat16
F32 = jnp.float32
ALL = ("x", "core", "y", "z")
CHIPS = ("x", "y", "z")

CIN = 512
COUT = 1024
DM = 1280
TOK = 256
SIDE = 16
NX = 4
NYZ = 16
CONV_ROWS = 36
PROJ_ROWS = 8
XCONV = CONV_ROWS * NYZ
XPROJ = PROJ_ROWS * NYZ
XROWS = XCONV + XPROJ
CHUNK = 48


def dot(a, b, dims):
    return lax.dot_general(a, b, (dims, ((), ())), preferred_element_type=F32)


def selection():
    row = lax.broadcasted_iota(jnp.int32, (384, 256), 0)
    col = lax.broadcasted_iota(jnp.int32, (384, 256), 1)
    tap = lax.shift_right_logical(row, 7)
    parity = lax.shift_right_logical(row, 6) & 1
    y = lax.shift_right_logical(row, 4) & 3
    x = 2 * (row & 15) + tap - 1
    hit = (col == (2 * y + parity) * 32 + x) & (x >= 0)
    return jnp.where(hit, 1.0, 0.0)


def forward_kernel(
    core_ref, pages_ref, pre_ref, w_ref, proj_ref, own_ref, other_ref, values_ref, patch, patch_t, acc
):
    step = pl.program_id(0)

    @pl.when(step == 0)
    def _():
        select = selection()
        for t in range(2):
            live = jnp.where(t < pages_ref[0], 1.0, 0.0)
            chosen = (select * live).astype(BF)
            for c in range(3):
                patch[t * TOK : t * TOK + SIDE, c * CIN : (c + 1) * CIN] = jnp.zeros((SIDE, CIN), BF)
            for q in range(4):
                rows = pre_ref[t * 1024 + q * 256 : t * 1024 + (q + 1) * 256, :]
                got = dot(chosen, rows, ((1,), (0,))).astype(BF)
                at = t * TOK + q * 64
                for c in range(3):
                    even = got[c * 128 : c * 128 + 64]
                    odd = got[c * 128 + 64 : c * 128 + 128]
                    patch[at : at + 64, (3 + c) * CIN : (4 + c) * CIN] = even
                    patch[at : at + 64, (6 + c) * CIN : (7 + c) * CIN] = odd
                    if q < 3:
                        patch[at + 16 : at + 80, c * CIN : (c + 1) * CIN] = odd
                    else:
                        patch[at + 16 : at + 64, c * CIN : (c + 1) * CIN] = odd[:48]

    for k in range(9):

        @pl.when(step == k)
        def _(k=k):
            taps = patch[:, k * CIN : (k + 1) * CIN]
            part = dot(taps, w_ref[...], ((1,), (0,)))
            if k == 0:
                acc[...] = part
            else:
                acc[...] += part
            patch_t[k * CIN : (k + 1) * CIN, :] = taps.T

    @pl.when(step == 8)
    def _():
        tokens = acc[...].astype(BF)
        values_ref[...] = dot(tokens, proj_ref[...], ((1,), (0,)))
        patch_t[9 * CIN : 9 * CIN + COUT, :] = tokens.T
        core = core_ref[0]
        for x in range(NX):
            for who, ref in ((core, own_ref), (1 - core, other_ref)):
                a = 2 * x + who
                conv_at = pl.multiple_of(a * XCONV, 64)
                proj_at = pl.multiple_of(9 * CIN + a * XPROJ, 128)
                ref[x * XROWS : x * XROWS + XCONV, :] = patch_t[pl.ds(conv_at, XCONV), :]
                ref[x * XROWS + XCONV : (x + 1) * XROWS, :] = patch_t[pl.ds(proj_at, XPROJ), :]


def forward(core, pages, pre, w, proj):
    n = 2 * TOK
    smem = pl.BlockSpec(memory_space=pltpu.SMEM)
    return pl.pallas_call(
        forward_kernel,
        grid=(9,),
        in_specs=[
            smem,
            smem,
            pl.BlockSpec((2048, CIN), lambda k: (0, 0)),
            pl.BlockSpec((CIN, COUT), lambda k: (k, 0)),
            pl.BlockSpec((COUT, DM), lambda k: (0, 0)),
        ],
        out_specs=[
            pl.BlockSpec((NX * XROWS, n), lambda k: (0, 0)),
            pl.BlockSpec((NX * XROWS, n), lambda k: (0, 0)),
            pl.BlockSpec((n, DM), lambda k: (0, 0)),
        ],
        out_shape=[
            jax.ShapeDtypeStruct((NX * XROWS, n), BF),
            jax.ShapeDtypeStruct((NX * XROWS, n), BF),
            jax.ShapeDtypeStruct((n, DM), F32),
        ],
        scratch_shapes=[
            pltpu.VMEM((n, 9 * CIN), BF),
            pltpu.VMEM((9 * CIN + COUT, n), BF),
            pltpu.VMEM((n, COUT), F32),
        ],
        compiler_params=pltpu.CompilerParams(vmem_limit_bytes=56 << 20),
        cost_estimate=pl.CostEstimate(flops=6_200_000_000, bytes_accessed=24_000_000, transcendentals=0),
        name="forward",
    )(core, pages, pre, w, proj)


def norm_kernel(dest_ref, cot_ref, values_ref, gain_ref, grad_ref, gain_out_ref):
    step = pl.program_id(0)
    values = values_ref[...]
    cot = cot_ref[0].astype(F32)
    scale = lax.rsqrt(jnp.mean(values * values, axis=-1, keepdims=True) + EPS)
    up = cot * gain_ref[...]
    inner = jnp.mean(up * values, axis=-1, keepdims=True)
    grad_ref[...] = (scale * up - values * (scale * scale * scale * inner)).astype(BF)
    terms = jnp.sum(cot * values * scale, axis=0, keepdims=True)

    @pl.when(step == 0)
    def _():
        gain_out_ref[...] = jnp.zeros_like(gain_out_ref)

    gain_out_ref[...] += jnp.broadcast_to(terms, gain_out_ref.shape)


def norm(dest, cot, values, gain):
    return pl.pallas_call(
        norm_kernel,
        grid_spec=pltpu.PrefetchScalarGridSpec(
            num_scalar_prefetch=1,
            grid=(8,),
            in_specs=[
                pl.BlockSpec((1, 64, DM), lambda k, d: (d[k], 0, 0)),
                pl.BlockSpec((64, DM), lambda k, d: (k, 0)),
                pl.BlockSpec((1, DM), lambda k, d: (0, 0)),
            ],
            out_specs=[
                pl.BlockSpec((64, DM), lambda k, d: (k, 0)),
                pl.BlockSpec((8, DM), lambda k, d: (0, 0)),
            ],
        ),
        out_shape=[jax.ShapeDtypeStruct((512, DM), BF), jax.ShapeDtypeStruct((8, DM), F32)],
        compiler_params=pltpu.CompilerParams(vmem_limit_bytes=32 << 20),
        cost_estimate=pl.CostEstimate(flops=8_000_000, bytes_accessed=6_000_000, transcendentals=512),
        name="norm_backward",
    )(dest, cot, values, gain)


def backward_kernel(
    own_ref, other_ref, gown_ref, gother_ref, proj_ref, gain_own_ref, gain_other_ref, out_ref, gtok, conv, stage
):
    step = pl.program_id(0)

    @pl.when(step == 0)
    def _():
        gtok[:512] = dot(gown_ref[...], proj_ref[...], ((1,), (1,))).astype(BF)
        gtok[512:] = dot(gother_ref[...], proj_ref[...], ((1,), (1,))).astype(BF)

    conv[...] = dot(own_ref[:XCONV], gtok[:512], ((1,), (0,))) + dot(
        other_ref[:XCONV], gtok[512:], ((1,), (0,))
    )
    proj = dot(own_ref[XCONV:], gown_ref[...], ((1,), (0,))) + dot(
        other_ref[XCONV:], gother_ref[...], ((1,), (0,))
    )
    gain = gain_own_ref[0:1] + gain_other_ref[0:1]
    for k in range(NYZ):
        stage[0:8, :] = proj[8 * k : 8 * k + 8, :COUT]
        stage[8:44, :] = conv[36 * k : 36 * k + 36, :]
        for r in range(8):
            stage[44 + r // 4 : 45 + r // 4, (r % 4) * 256 : (r % 4 + 1) * 256] = proj[
                8 * k + r : 8 * k + r + 1, COUT:
            ]
        stage[46:47, :] = gain[:, :COUT]
        stage[47:48, :256] = gain[:, COUT:]
        stage[47:48, 256:] = jnp.zeros((1, COUT - 256), F32)
        out_ref[k] = stage[...].astype(BF)


def backward(own, other, gown, gother, proj, gain_own, gain_other):
    whole = lambda *s: pl.BlockSpec(s, lambda x: (0, 0))
    return pl.pallas_call(
        backward_kernel,
        grid=(NX,),
        in_specs=[
            pl.BlockSpec((XROWS, 512), lambda x: (x, 0)),
            pl.BlockSpec((XROWS, 512), lambda x: (x, 0)),
            whole(512, DM),
            whole(512, DM),
            whole(COUT, DM),
            whole(8, DM),
            whole(8, DM),
        ],
        out_specs=pl.BlockSpec((NYZ, CHUNK, COUT), lambda x: (x, 0, 0)),
        out_shape=jax.ShapeDtypeStruct((NX * NYZ, CHUNK, COUT), BF),
        scratch_shapes=[
            pltpu.VMEM((1024, COUT), BF),
            pltpu.VMEM((XCONV, COUT), F32),
            pltpu.VMEM((CHUNK, COUT), F32),
        ],
        compiler_params=pltpu.CompilerParams(vmem_limit_bytes=56 << 20),
        cost_estimate=pl.CostEstimate(flops=9_000_000_000, bytes_accessed=20_000_000, transcendentals=0),
        name="backward",
    )(own, other, gown, gother, proj, gain_own, gain_other)


def sum_kernel(got_ref, conv_ref, proj_ref, gain_ref, acc):
    step = pl.program_id(0)
    part = got_ref[0].astype(F32)
    for i in range(1, 8):
        part = part + got_ref[i].astype(F32)

    @pl.when(step == 0)
    def _():
        acc[...] = part

    @pl.when(step > 0)
    def _():
        acc[...] += part

    @pl.when(step == 7)
    def _():
        proj_ref[:, :COUT] = acc[0:8, :]
        conv_ref[...] = acc[8:44, :]
        for r in range(8):
            proj_ref[r : r + 1, COUT:] = acc[44 + r // 4 : 45 + r // 4, (r % 4) * 256 : (r % 4 + 1) * 256]
        gain_ref[:, :COUT] = acc[46:47, :]
        gain_ref[:, COUT:] = acc[47:48, :256]


def total(got):
    return pl.pallas_call(
        sum_kernel,
        grid=(8,),
        in_specs=[pl.BlockSpec((8, CHUNK, COUT), lambda k: (k, 0, 0))],
        out_specs=[
            pl.BlockSpec((CONV_ROWS, COUT), lambda k: (0, 0)),
            pl.BlockSpec((PROJ_ROWS, DM), lambda k: (0, 0)),
            pl.BlockSpec((1, DM), lambda k: (0, 0)),
        ],
        out_shape=[
            jax.ShapeDtypeStruct((CONV_ROWS, COUT), F32),
            jax.ShapeDtypeStruct((PROJ_ROWS, DM), F32),
            jax.ShapeDtypeStruct((1, DM), F32),
        ],
        scratch_shapes=[pltpu.VMEM((CHUNK, COUT), F32)],
        compiler_params=pltpu.CompilerParams(vmem_limit_bytes=32 << 20),
        cost_estimate=pl.CostEstimate(flops=3_000_000, bytes_accessed=6_500_000, transcendentals=0),
        name="total",
    )(got)


def per_device(pre_conv, conv_weight, proj_weight, norm_gain, slab_cotangent, page_tiles, block_dest):
    core = lax.axis_index("core").astype(jnp.int32).reshape(1)
    swap = functools.partial(lax.ppermute, axis_name="core", perm=[(0, 1), (1, 0)])
    cot = lax.all_to_all(slab_cotangent.reshape(16, 64, DM), ("y", "z"), 0, 0, tiled=True)
    own, other, values = forward(core, page_tiles, pre_conv.reshape(2048, CIN), conv_weight, proj_weight)
    other = swap(other)
    grads, gain = norm(block_dest[:, 0], cot, values, norm_gain.reshape(1, DM))
    chunks = backward(own, other, grads, swap(grads), proj_weight, gain, swap(gain))
    got = lax.all_to_all(chunks, CHIPS, 0, 0, tiled=True)
    grad_conv, grad_proj, grad_gain = total(got)
    return grad_conv, grad_proj, grad_gain.reshape(DM)


def solution(mesh):
    split = Mesh(mesh.devices.reshape(4, 2, 4, 4), ALL)
    return jax.shard_map(
        per_device,
        mesh=split,
        in_specs=(P(ALL), P(), P(), P(), P(ALL), P(ALL), P(ALL)),
        out_specs=(P(ALL), P(ALL), P()),
        check_vma=False,
    )
```

time: 978 us -> 154 us (0.16); the launches traced: 967 us -> 153 us
  blocking collectives: 518 us -> 81.8 us
  local copies, waits for them, and re-layouts: 194 us -> 2.8 us
  waiting for transfers between devices: 168 us -> 21.4 us
  Pallas kernels: 0 us -> 36.5 us
  matrix products: 30.2 us -> 0 us
  starting transfers between devices: 37.6 us -> 8.73 us
  between operations: 15.1 us -> 1.38 us
    unnamed x1 -> x0, blocking collectives: 367 us -> none
    slice x9 -> x0, local copies, waits for them, and re-layouts: 147 us -> none  [patches(): padded[row_off:row_off + grid_side:2, col_off:col_off + grid_side:2, :]]
    reduce_scatter x1 -> x0, waiting for transfers between devices: 134 us -> none  [per_device(): lax.psum_scatter(jnp.einsum('rc,rw->cw', column_part, right_rows, preferr...]
    psum x1 -> x0, blocking collectives: 79.7 us -> none  [per_device(): grad_gain = lax.psum(gain_terms, ('tile', 'slab'))]
    pallas_call x0 -> x4, Pallas kernels: none -> 36.5 us  [the longest x1 17.6 us: forward(): pl.pallas_call(forward_kernel, grid=(9,), in_specs=[smem, smem, pl.BlockS...]
    unnamed x13 -> x0, starting transfers between devices: 32.9 us -> none
    dot_general x5 -> x0, matrix products: 30.2 us -> none  [the longest x1 9.53 us: per_device(): jnp.einsum('tpk,kc->tpc', patch_rows, conv_weight, preferred_element_type...]
    unnamed x39 -> x14, local copies, waits for them, and re-layouts: 30.7 us -> 2.79 us
  transfers between devices with their start and end apart: 15 -> 4, of which waited for: 2 -> 2; matrix products, arithmetic and copies ran while one was open for 42% -> 0% of each run, Pallas kernels for 0% -> 13%
where the time goes in v1:
time: 154 us; the launch traced here: 153 us
  blocking collectives  81.8 us (53%)
  Pallas kernels  36.5 us (24%)
  waiting for transfers between devices  21.4 us (14%)
  starting transfers between devices  8.73 us (6%)
  local copies, waits for them, and re-layouts  2.8 us (2%)
    all_to_all x1, blocking collectives, per_device(): got = lax.all_to_all(chunks, CHIPS, 0, 0, tiled=True)  81.8 us
    all_to_all x1, waiting for transfers between devices, per_device(): lax.all_to_all(slab_cotangent.reshape(16, 64, DM), ('y', 'z'), 0, 0, tile...  18.8 us
    pallas_call x1, Pallas kernels, forward(): pl.pallas_call(forward_kernel, grid=(9,), in_specs=[smem, smem, pl.BlockS...  17.6 us
    pallas_call x1, Pallas kernels, backward(): pl.pallas_call(backward_kernel, grid=(NX,), in_specs=[pl.BlockSpec((XROWS...  14.8 us
    all_to_all x1, starting transfers between devices, per_device(): lax.all_to_all(slab_cotangent.reshape(16, 64, DM), ('y', 'z'), 0, 0, tile...  8.14 us
  transfers between devices with their start and end apart: 4, of which 2 were waited for; matrix products, arithmetic and copies ran while one was open for 0% of the time, Pallas kernels for 13%

profile of v1, /device:TPU:0, one launch (start us, length us, event | category | flops | bytes accessed | tf_op | source)
XLA Modules:
  0.0 153.2 jit_solution(149893698939563844)
XLA Ops:
  0.6 8.1 %all-to-all-start = ((bf16[16,64,1280]{2,1,0:T(8,128)(2,1)}), bf16[16,64,1280]{2,1,0:T(8,128)(2,1)S(1)}, u32[]{:S(2)}, u32[]{:S(2)}) async-start(bf16[16,64,1280]{2,1,0:T(8,128)(2,1)} %bitcast.5), calls=%async_computation | async-start | bytes 5242880 | tf_op jit(solution)/shard_map/all_to_all | solution.py:281
  9.4 0.0 copy-start.4
  9.4 0.0 copy-start.1
  9.5 17.6 %forward.1 = (bf16[2816,512]{1,0:T(8,128)(2,1)}, bf16[2816,512]{1,0:T(8,128)(2,1)}, f32[512,1280]{1,0:T(8,128)}) custom-call(s32[1]{0:T(128)} %bitcast.core_ref, s32[1]{0:T(128)S(6)} %copy.10.pages_ref, bf16[2048,512]{1,0:T(8,128)(2,1)} %bitcast.6, bf16[4608,1024]{1,0:T(8,128)(2,1)} %w_ref.1, bf16[1024,1280]{1,0:T(8,128)(2,1)} %proj_ref.3), custom_call_target="tpu_custom_call" | custom-call | flops 6200000000 | bytes 24000000 | tf_op jit(solution)/shard_map/forward/pallas_call | solution.py:104
  27.0 0.0 collective-permute-start
  27.0 0.0 copy-done.4
  27.0 18.8 %all-to-all-done.cot_ref = bf16[16,64,1280]{2,1,0:T(8,128)(2,1)S(1)} async-done(((bf16[16,64,1280]{2,1,0:T(8,128)(2,1)}), bf16[16,64,1280]{2,1,0:T(8,128)(2,1)S(1)}, u32[]{:S(2)}, u32[]{:S(2)}) %all-to-all-start) | async-done | bytes 2621472 | tf_op jit(solution)/shard_map/all_to_all | solution.py:281
  45.9 0.0 copy-done.1
  45.9 0.0 copy-start
  45.9 1.7 %copy-done = f32[512,1280]{1,0:T(8,128)S(1)} copy-done((f32[512,1280]{1,0:T(8,128)S(1)}, f32[512,1280]{1,0:T(8,128)}, u32[]{:S(2)}) %copy-start) | copy-done | bytes 2621464
  47.6 2.2 %norm_backward.1 = (bf16[512,1280]{1,0:T(8,128)(2,1)S(1)}, f32[8,1280]{1,0:T(8,128)S(1)}) custom-call(s32[8]{0:T(128)S(1)} %bitcast.4, bf16[16,64,1280]{2,1,0:T(8,128)(2,1)S(1)} %all-to-all-done.cot_ref, f32[512,1280]{1,0:T(8,128)S(1)} %copy-done, f32[1,1280]{1,0:T(1,128)S(1)} %reshape.24.gain_ref), custom_call_target="tpu_custom_call" | custom-call | flops 8000000 | bytes 6000000 | tf_op jit(solution)/shard_map/norm_backward/pallas_call | solution.py:153
  49.8 0.0 copy-start.2
  49.8 0.0 copy-start.3
  49.8 0.1 collective-permute-start.1
  49.9 0.5 collective-permute-start.2
  50.4 2.6 %collective-permute-done.2.gain_other_ref = f32[8,1280]{1,0:T(8,128)S(1)} collective-permute-done((f32[8,1280]{1,0:T(8,128)S(1)}, f32[8,1280]{1,0:T(8,128)S(1)}, u32[]{:S(2)}, u32[]{:S(2)}) %collective-permute-start.2) | collective-permute-done | bytes 40992 | tf_op jit(solution)/shard_map/ppermute | solution.py:285
  53.0 0.0 copy-start.6
  53.0 0.0 collective-permute-done.other_ref
  53.0 0.0 collective-permute-done.1.gother_ref
  53.0 0.0 copy-start.5
  53.0 0.0 copy-done.2
  53.0 0.0 copy-done.3
  53.0 0.6 copy-done.6
  53.6 0.4 copy-done.5
  54.0 14.8 %backward.1 = bf16[64,48,1024]{2,1,0:T(8,128)(2,1)} custom-call(bf16[2816,512]{1,0:T(8,128)(2,1)} %get-tuple-element.11.own_ref, bf16[2816,512]{1,0:T(8,128)(2,1)} %collective-permute-done.other_ref, bf16[512,1280]{1,0:T(8,128)(2,1)} %copy-done.2, bf16[512,1280]{1,0:T(8,128)(2,1)} %copy-done.5, bf16[1024,1280]{1,0:T(8,128)(2,1)} %proj_ref.3, ...), custom_call_target="tpu_custom_call" | custom-call | flops 8999999488 | bytes 20000000 | tf_op jit(solution)/shard_map/backward/pallas_call | solution.py:207
  68.9 81.8 %all_to_all.10.got_ref = bf16[64,48,1024]{2,1,0:T(8,128)(2,1)S(1)} all-to-all(bf16[64,48,1024]{2,1,0:T(8,128)(2,1)} %backward.1), channel_id=1, replica_groups=mesh['x'=4,'core'=2,'y'=4,'z'=4] {'x','y','z'}, dimensions={0} | all-to-all | bytes 12582912 | tf_op jit(solution)/shard_map/all_to_all | solution.py:286
  150.6 1.9 %total.1 = (f32[36,1024]{1,0:T(8,128)}, f32[8,1280]{1,0:T(8,128)}, f32[1,1280]{1,0:T(1,128)S(1)}) custom-call(bf16[64,48,1024]{2,1,0:T(8,128)(2,1)S(1)} %all_to_all.10.got_ref), custom_call_target="tpu_custom_call" | custom-call | flops 3000000 | bytes 6500000 | tf_op jit(solution)/shard_map/total/pallas_call | solution.py:257
  152.6 0.6 reduce
  (1 shorter events, 0.0 us)
Async XLA Ops:
  0.6 45.2 %all-to-all-start = ((bf16[16,64,1280]{2,1,0:T(8,128)(2,1)}), bf16[16,64,1280]{2,1,0:T(8,128)(2,1)S(1)}, u32[]{:S(2)}, u32[]{:S(2)}) async-start(bf16[16,64,1280]{2,1,0:T(8,128)(2,1)} %bitcast.5), calls=%async_computation | async-start | bytes 5242880 | tf_op jit(solution)/shard_map/all_to_all | solution.py:281
  9.4 17.6 %copy-start.4 = (f32[1280]{0:T(1024)S(1)}, f32[1280]{0:T(1024)}, u32[]{:S(2)}) copy-start(f32[1280]{0:T(1024)} %param.10) | copy-start | bytes 15364
  9.4 36.4 %copy-start.1 = (s32[8,1]{0,1:T(1,128)S(1)}, s32[8,1]{0,1:T(1,128)}, u32[]{:S(2)}) copy-start(s32[8,1]{0,1:T(1,128)} %param.13) | copy-start | bytes 100
  27.0 26.0 %collective-permute-start = (bf16[2816,512]{1,0:T(8,128)(2,1)}, bf16[2816,512]{1,0:T(8,128)(2,1)}, u32[]{:S(2)}, u32[]{:S(2)}) collective-permute-start(bf16[2816,512]{1,0:T(8,128)(2,1)} %get-tuple-element.12), channel_id=1, source_target_pairs={{0,16},{16,0},{1,17},{17,1},{2,18},{18,2},{3,19},{19,3},{4,20},{20... | collective-permute-start | bytes 8650760 | tf_op jit(solution)/shard_map/ppermute | solution.py:283
  45.9 1.7 %copy-start = (f32[512,1280]{1,0:T(8,128)S(1)}, f32[512,1280]{1,0:T(8,128)}, u32[]{:S(2)}) copy-start(f32[512,1280]{1,0:T(8,128)} %get-tuple-element.13.values_ref) | copy-start | bytes 7864324
  49.8 3.2 %copy-start.2 = (bf16[512,1280]{1,0:T(8,128)(2,1)}, bf16[512,1280]{1,0:T(8,128)(2,1)S(1)}, u32[]{:S(2)}) copy-start(bf16[512,1280]{1,0:T(8,128)(2,1)S(1)} %get-tuple-element.14.gown_ref) | copy-start | bytes 3932164
  49.8 3.2 %copy-start.3 = (f32[8,1280]{1,0:T(8,128)}, f32[8,1280]{1,0:T(8,128)S(1)}, u32[]{:S(2)}) copy-start(f32[8,1280]{1,0:T(8,128)S(1)} %get-tuple-element.15.gain_own_ref) | copy-start | bytes 122884
  49.8 3.2 %collective-permute-start.1 = (bf16[512,1280]{1,0:T(8,128)(2,1)S(1)}, bf16[512,1280]{1,0:T(8,128)(2,1)S(1)}, u32[]{:S(2)}, u32[]{:S(2)}) collective-permute-start(bf16[512,1280]{1,0:T(8,128)(2,1)S(1)} %get-tuple-element.14.gown_ref), channel_id=1, source_target_pairs={{0,16},{16,0},{1,17},{17,1},{2,18},{18,2},{3,19},{19,3},{4,20},{20... | collective-permute-start | bytes 3932168 | tf_op jit(solution)/shard_map/ppermute | solution.py:285
  49.9 3.1 %collective-permute-start.2 = (f32[8,1280]{1,0:T(8,128)S(1)}, f32[8,1280]{1,0:T(8,128)S(1)}, u32[]{:S(2)}, u32[]{:S(2)}) collective-permute-start(f32[8,1280]{1,0:T(8,128)S(1)} %get-tuple-element.15.gain_own_ref), channel_id=1, source_target_pairs={{0,16},{16,0},{1,17},{17,1},{2,18},{18,2},{3,19},{19,3},{4,20},{20... | collective-permute-start | bytes 122888 | tf_op jit(solution)/shard_map/ppermute | solution.py:285
  53.0 0.6 copy-start.6
  53.0 1.1 copy-start.5

commit v2 on v1

v2 whole, which is shorter than its diff:
```python
import functools

import jax
import jax.numpy as jnp
from jax import lax
from jax.experimental import pallas as pl
from jax.experimental.pallas import tpu as pltpu
from jax.sharding import Mesh
from jax.sharding import PartitionSpec as P

EPS = 1e-6
BF = jnp.bfloat16
F32 = jnp.float32
ALL = ("x", "core", "y", "z")
CHIPS = ("x", "y", "z")

CIN = 512
COUT = 1024
DM = 1280
TOK = 256
SIDE = 16
NX = 4
NYZ = 16
CONV_ROWS = 36
PROJ_ROWS = 8
XCONV = CONV_ROWS * NYZ
XPROJ = PROJ_ROWS * NYZ
XROWS = XCONV + XPROJ
YROWS = XCONV // 4
HROWS = XCONV // 2
HALF = COUT // 2
LONG = 20_000_000_000


def dot(a, b, dims):
    return lax.dot_general(a, b, (dims, ((), ())), preferred_element_type=F32)


def selection():
    row = lax.broadcasted_iota(jnp.int32, (384, 256), 0)
    col = lax.broadcasted_iota(jnp.int32, (384, 256), 1)
    tap = lax.shift_right_logical(row, 7)
    parity = lax.shift_right_logical(row, 6) & 1
    y = lax.shift_right_logical(row, 4) & 3
    x = 2 * (row & 15) + tap - 1
    hit = (col == (2 * y + parity) * 32 + x) & (x >= 0)
    return jnp.where(hit, 1.0, 0.0)


def forward_kernel(
    core_ref, pages_ref, pre_ref, w_ref, proj_ref, own_ref, other_ref, values_ref, proj_t_ref, patch, patch_t, acc
):
    step = pl.program_id(0)

    @pl.when(step == 0)
    def _():
        select = selection()
        for t in range(2):
            live = jnp.where(t < pages_ref[0], 1.0, 0.0)
            chosen = (select * live).astype(BF)
            for c in range(3):
                patch[t * TOK : t * TOK + SIDE, c * CIN : (c + 1) * CIN] = jnp.zeros((SIDE, CIN), BF)
            for q in range(4):
                rows = pre_ref[t * 1024 + q * 256 : t * 1024 + (q + 1) * 256, :]
                got = dot(chosen, rows, ((1,), (0,))).astype(BF)
                at = t * TOK + q * 64
                for c in range(3):
                    even = got[c * 128 : c * 128 + 64]
                    odd = got[c * 128 + 64 : c * 128 + 128]
                    patch[at : at + 64, (3 + c) * CIN : (4 + c) * CIN] = even
                    patch[at : at + 64, (6 + c) * CIN : (7 + c) * CIN] = odd
                    if q < 3:
                        patch[at + 16 : at + 80, c * CIN : (c + 1) * CIN] = odd
                    else:
                        patch[at + 16 : at + 64, c * CIN : (c + 1) * CIN] = odd[:48]

    for k in range(9):

        @pl.when(step == k)
        def _(k=k):
            taps = patch[:, k * CIN : (k + 1) * CIN]
            part = dot(taps, w_ref[...], ((1,), (0,)))
            if k == 0:
                acc[...] = part
            else:
                acc[...] += part
            patch_t[k * CIN : (k + 1) * CIN, :] = taps.T

    @pl.when(step == 8)
    def _():
        tokens = acc[...].astype(BF)
        values_ref[...] = dot(tokens, proj_ref[...], ((1,), (0,)))
        proj_t_ref[...] = proj_ref[...].T
        patch_t[9 * CIN : 9 * CIN + COUT, :] = tokens.T
        core = core_ref[1]
        for x in range(NX):
            for who, ref in ((core, own_ref), (1 - core, other_ref)):
                a = 2 * x + who
                conv_at = pl.multiple_of(a * XCONV, 64)
                proj_at = pl.multiple_of(9 * CIN + a * XPROJ, 128)
                ref[x * XCONV : (x + 1) * XCONV, :] = patch_t[pl.ds(conv_at, XCONV), :]
                to = NX * XCONV + x * XPROJ
                ref[to : to + XPROJ, :] = patch_t[pl.ds(proj_at, XPROJ), :]


def forward(core, pages, pre, w, proj):
    n = 2 * TOK
    smem = pl.BlockSpec(memory_space=pltpu.SMEM)
    return pl.pallas_call(
        forward_kernel,
        grid=(9,),
        in_specs=[
            smem,
            smem,
            pl.BlockSpec((2048, CIN), lambda k: (0, 0)),
            pl.BlockSpec((CIN, COUT), lambda k: (k, 0)),
            pl.BlockSpec((COUT, DM), lambda k: (0, 0)),
        ],
        out_specs=[
            pl.BlockSpec((NX * XROWS, n), lambda k: (0, 0)),
            pl.BlockSpec((NX * XROWS, n), lambda k: (0, 0)),
            pl.BlockSpec((n, DM), lambda k: (0, 0)),
            pl.BlockSpec((DM, COUT), lambda k: (0, 0)),
        ],
        out_shape=[
            jax.ShapeDtypeStruct((NX * XROWS, n), BF),
            jax.ShapeDtypeStruct((NX * XROWS, n), BF),
            jax.ShapeDtypeStruct((n, DM), F32),
            jax.ShapeDtypeStruct((DM, COUT), BF),
        ],
        scratch_shapes=[
            pltpu.VMEM((n, 9 * CIN), BF),
            pltpu.VMEM((9 * CIN + COUT, n), BF),
            pltpu.VMEM((n, COUT), F32),
        ],
        compiler_params=pltpu.CompilerParams(vmem_limit_bytes=60 << 20),
        cost_estimate=pl.CostEstimate(flops=6_200_000_000, bytes_accessed=24_000_000, transcendentals=0),
        name="forward",
    )(core, pages, pre, w, proj)


def norm_kernel(
    dest_ref, cot_ref, values_hbm, gain_ref, proj_t_hbm, grad_ref, gain_out_ref, proj_t_ref, values, sems
):
    copies = [pltpu.make_async_copy(values_hbm.at[k], values.at[k], sems.at[k]) for k in range(8)]
    copies.append(pltpu.make_async_copy(proj_t_hbm, proj_t_ref, sems.at[8]))
    for copy in copies:
        copy.start()
    total = jnp.zeros((8, DM), F32)
    for k in range(8):
        c = cot_ref[dest_ref[k]].astype(F32)
        copies[k].wait()
        v = values[k]
        scale = lax.rsqrt(jnp.mean(v * v, axis=-1, keepdims=True) + EPS)
        up = c * gain_ref[...]
        inner = jnp.mean(up * v, axis=-1, keepdims=True)
        grad_ref[64 * k : 64 * k + 64, :] = (scale * up - v * (scale * scale * scale * inner)).astype(BF)
        total = total + jnp.sum((c * v * scale).reshape(8, 8, DM), axis=0)
    gain_out_ref[...] = jnp.broadcast_to(jnp.sum(total, axis=0, keepdims=True), (8, DM))
    copies[8].wait()


SMEM_SPEC = pl.BlockSpec(memory_space=pltpu.SMEM)
VMEM_SPEC = pl.BlockSpec(memory_space=pltpu.VMEM)
HBM_SPEC = pl.BlockSpec(memory_space=pltpu.HBM)
ANY_SPEC = pl.BlockSpec(memory_space=pl.ANY)


def in_hbm(array):
    return pltpu.with_memory_space_constraint(array, pltpu.HBM)


def norm(dest, cot, values, gain, proj_t):
    return pl.pallas_call(
        norm_kernel,
        in_specs=[SMEM_SPEC, VMEM_SPEC, HBM_SPEC, VMEM_SPEC, HBM_SPEC],
        out_specs=[VMEM_SPEC] * 3,
        out_shape=[
            jax.ShapeDtypeStruct((512, DM), BF),
            jax.ShapeDtypeStruct((8, DM), F32),
            pltpu.VMEM((DM, COUT), BF),
        ],
        scratch_shapes=[pltpu.VMEM((8, 64, DM), F32), pltpu.SemaphoreType.DMA((9,))],
        compiler_params=pltpu.CompilerParams(vmem_limit_bytes=16 << 20),
        cost_estimate=pl.CostEstimate(flops=8_000_000, bytes_accessed=8_000_000, transcendentals=512),
        name="norm_backward",
    )(dest, cot, in_hbm(values.reshape(8, 64, DM)), gain, in_hbm(proj_t))


def token_kernel(
    grad_ref, proj_t_ref, own_hbm, other_hbm, out_ref, own_ref, other_ref, own_tok_ref, other_tok_ref, sems
):
    copies = []
    for x in range(4):
        rows = pl.ds(x * XCONV, XCONV)
        copies.append(pltpu.make_async_copy(own_hbm.at[rows], own_ref.at[x], sems.at[0, x]))
        copies.append(pltpu.make_async_copy(other_hbm.at[rows], other_ref.at[x], sems.at[1, x]))
    rows = pl.ds(NX * XCONV, NX * XPROJ)
    copies.append(pltpu.make_async_copy(own_hbm.at[rows], own_tok_ref, sems.at[0, 4]))
    copies.append(pltpu.make_async_copy(other_hbm.at[rows], other_tok_ref, sems.at[1, 4]))
    for copy in copies:
        copy.start()
    out_ref[...] = dot(grad_ref[...], proj_t_ref[...], ((1,), (0,))).astype(BF)
    for copy in copies:
        copy.wait()


def token_grad(grads, proj_t, own, other):
    return pl.pallas_call(
        token_kernel,
        in_specs=[VMEM_SPEC, VMEM_SPEC, HBM_SPEC, HBM_SPEC],
        out_specs=[VMEM_SPEC] * 5,
        out_shape=[jax.ShapeDtypeStruct((512, COUT), BF)]
        + [pltpu.VMEM((NX, XCONV, 512), BF)] * 2
        + [pltpu.VMEM((NX * XPROJ, 512), BF)] * 2,
        scratch_shapes=[pltpu.SemaphoreType.DMA((2, 5))],
        compiler_params=pltpu.CompilerParams(vmem_limit_bytes=16 << 20),
        cost_estimate=pl.CostEstimate(flops=1_340_000_000, bytes_accessed=8_000_000, transcendentals=0),
        name="token_grad",
    )(grads, proj_t, in_hbm(own), in_hbm(other))


def by_turn(axis, pos_ref, s, rows_ref):
    if axis == 0:
        return rows_ref[(pos_ref[0] + s) & 3]
    rows = pl.ds(pl.multiple_of(((pos_ref[2] + s) & 3) * YROWS, 16), YROWS)
    return jnp.concatenate([rows_ref[x, rows, :] for x in range(NX)], axis=0)


def conv_block(axis, pos_ref, s, own, other, gtok, gtok_other):
    at = pl.ds(axis * HALF // 2, HALF)
    return (
        dot(by_turn(axis, pos_ref, s, own), gtok[:, at], ((1,), (0,)))
        + dot(by_turn(axis, pos_ref, s, other), gtok_other[:, at], ((1,), (0,)))
    ).astype(BF)


def conv_first_kernel(pos_ref, own, other, gtok, gother, proj_t, after, *rest):
    outs, gtok_other, part, sems = rest[:4], rest[4], rest[5], rest[6]
    gtok_other[...] = dot(gother[...], proj_t[...], ((1,), (0,))).astype(BF)
    sends = []
    for slot, axis in enumerate((0, 2)):
        part[slot] = conv_block(axis, pos_ref, 2, own, other, gtok, gtok_other)
        for half in range(2):
            rows = part.at[slot, pl.ds(half * HROWS, HROWS)]
            sends.append(pltpu.make_async_copy(rows, outs[2 * slot + half], sems.at[slot, half]))
            sends[-1].start()
    for copy in sends:
        copy.wait()


def conv_first(pos, own, other, gtok, gother, proj_t, after):
    return pl.pallas_call(
        conv_first_kernel,
        in_specs=[SMEM_SPEC] + [VMEM_SPEC] * 5 + [ANY_SPEC],
        out_specs=[HBM_SPEC] * 4 + [VMEM_SPEC],
        out_shape=[pltpu.HBM((HROWS, HALF), BF)] * 4 + [jax.ShapeDtypeStruct((512, COUT), BF)],
        scratch_shapes=[pltpu.VMEM((2, XCONV, HALF), BF), pltpu.SemaphoreType.DMA((2, 2))],
        compiler_params=pltpu.CompilerParams(vmem_limit_bytes=16 << 20),
        cost_estimate=pl.CostEstimate(flops=2_500_000_000, bytes_accessed=2_000_000, transcendentals=0),
        name="conv_first",
    )(pos, own, other, gtok, gother, proj_t, after)


def conv_second_kernel(pos_ref, own, other, gtok, gtok_other, through_in, *rest):
    outs, through_out, part, sems = rest[:6], rest[6], rest[7], rest[8]
    sends = []
    for axis in (0, 2):
        for s in (1, 3, 0):
            slot = len(sends)
            part[slot] = conv_block(axis, pos_ref, s, own, other, gtok, gtok_other)
            sends.append(pltpu.make_async_copy(part.at[slot], outs[slot], sems.at[slot]))
            sends[-1].start()
    for copy in sends:
        copy.wait()


def conv_second(pos, own, other, gtok, gtok_other, through):
    return pl.pallas_call(
        conv_second_kernel,
        in_specs=[SMEM_SPEC] + [VMEM_SPEC] * 4 + [HBM_SPEC],
        out_specs=[HBM_SPEC] * 7,
        out_shape=[pltpu.HBM((XCONV, HALF), BF)] * 6 + [pltpu.HBM(through.shape, through.dtype)],
        input_output_aliases={5: 6},
        scratch_shapes=[pltpu.VMEM((6, XCONV, HALF), BF), pltpu.SemaphoreType.DMA((6,))],
        compiler_params=pltpu.CompilerParams(vmem_limit_bytes=16 << 20),
        cost_estimate=pl.CostEstimate(flops=3_700_000_000, bytes_accessed=3_000_000, transcendentals=0),
        name="conv_second",
    )(pos, own, other, gtok, gtok_other, in_hbm(through))


def add_kernel(ahead_in, behind_in, from_behind, from_ahead, ahead, behind, part, sems):
    halves = (
        (ahead_in, ahead, pl.ds(0, HROWS), from_behind),
        (behind_in, behind, pl.ds(HROWS, HROWS), from_ahead),
    )
    loads = [
        pltpu.make_async_copy(old.at[rows], part.at[i], sems.at[0, i]) for i, (old, _, rows, _) in enumerate(halves)
    ]
    stores = [
        pltpu.make_async_copy(part.at[i], new.at[rows], sems.at[1, i]) for i, (_, new, rows, _) in enumerate(halves)
    ]
    for copy in loads:
        copy.start()
    for i in range(2):
        loads[i].wait()
        part[i] = (part[i].astype(F32) + halves[i][3][...].astype(F32)).astype(BF)
        stores[i].start()
    for copy in stores:
        copy.wait()


def relay(axis, halves, ahead, behind, here):
    forward, back = [(i, (i + 1) % 4) for i in range(4)], [(i, (i + 3) % 4) for i in range(4)]
    from_behind = lax.ppermute(halves[0], axis, forward)
    from_ahead = lax.ppermute(halves[1], axis, back)

    def finish():
        one, other = pl.pallas_call(
            add_kernel,
            in_specs=[HBM_SPEC, HBM_SPEC, VMEM_SPEC, VMEM_SPEC],
            out_specs=[HBM_SPEC] * 2,
            out_shape=[pltpu.HBM((XCONV, HALF), BF)] * 2,
            input_output_aliases={0: 0, 1: 1},
            scratch_shapes=[pltpu.VMEM((2, HROWS, HALF), BF), pltpu.SemaphoreType.DMA((2, 2))],
            compiler_params=pltpu.CompilerParams(vmem_limit_bytes=16 << 20),
            cost_estimate=pl.CostEstimate(flops=LONG, bytes_accessed=3_000_000, transcendentals=0),
            name="add_" + axis,
        )(in_hbm(ahead), in_hbm(behind), from_behind, from_ahead)
        return [here, lax.ppermute(one, axis, forward), lax.ppermute(other, axis, back)]

    return finish()


def split_gain(gain):
    high = gain.astype(BF).astype(F32)
    rest = gain - high
    low = rest.astype(BF).astype(F32)
    return jnp.concatenate(
        [
            jnp.broadcast_to(high, (8, DM)),
            jnp.broadcast_to(low, (8, DM)),
        ],
        axis=0,
    )


def proj_kernel(own, other, gown, gother, gain_own, gain_other, after, out_hbm, part, out, sem):
    gain = split_gain(gain_own[0:1] + gain_other[0:1]).astype(BF)
    for z in range(4):
        out[z, 128:144, :] = gain
    for x in range(4):
        rows = slice(x * XPROJ, (x + 1) * XPROJ)
        part[...] = dot(own[rows, :], gown[...], ((1,), (0,))) + dot(other[rows, :], gother[...], ((1,), (0,)))
        for z in range(4):
            pick = [part[y * 32 + z * 8 : y * 32 + z * 8 + 8, :] for y in range(4)]
            out[z, x * 32 : x * 32 + 32, :] = jnp.concatenate(pick, axis=0).astype(BF)
    copy = pltpu.make_async_copy(out, out_hbm, sem)
    copy.start()
    copy.wait()


def proj_grad(own, other, gown, gother, gain_own, gain_other, after):
    return pl.pallas_call(
        proj_kernel,
        in_specs=[VMEM_SPEC] * 6 + [ANY_SPEC],
        out_specs=HBM_SPEC,
        out_shape=pltpu.HBM((4, 144, DM), BF),
        scratch_shapes=[
            pltpu.VMEM((XPROJ, DM), F32),
            pltpu.VMEM((4, 144, DM), BF),
            pltpu.SemaphoreType.DMA,
        ],
        compiler_params=pltpu.CompilerParams(vmem_limit_bytes=16 << 20),
        cost_estimate=pl.CostEstimate(flops=1_400_000_000, bytes_accessed=2_000_000, transcendentals=0),
        name="proj_grad",
    )(own, other, gown, gother, gain_own, gain_other, after)


def small(kernel, name, outs, args, scratch=(), mib=16, flops=1_000_000, after=()):
    bytes_in = sum(a.size * a.dtype.itemsize for a in args)
    return pl.pallas_call(
        kernel,
        in_specs=[SMEM_SPEC] + [VMEM_SPEC] * (len(args) - 1) + [ANY_SPEC] * len(after),
        out_specs=[VMEM_SPEC] * len(outs),
        out_shape=[jax.ShapeDtypeStruct(*o) for o in outs],
        scratch_shapes=list(scratch),
        compiler_params=pltpu.CompilerParams(vmem_limit_bytes=mib << 20),
        cost_estimate=pl.CostEstimate(flops=flops, bytes_accessed=bytes_in, transcendentals=0),
        name=name,
    )(*args, *after)


def first_sum_kernel(pos_ref, a, b, c, *outs):
    for s, ref in enumerate(outs):
        at = pl.ds(pl.multiple_of(((pos_ref[2] + s) & 3) * YROWS, 16), YROWS)
        ref[...] = (a[at, :].astype(F32) + (b[at, :].astype(F32) + c[at, :].astype(F32))).astype(BF)


def second_sum_kernel(pos_ref, a, b, c, proj_ref, *outs):
    gains = [proj_ref[i, 128:136, :].astype(F32) + proj_ref[i, 136:144, :].astype(F32) for i in range(4)]
    gain = split_gain(((gains[0] + gains[1]) + (gains[2] + gains[3]))[0:1])
    for s, ref in enumerate(outs):
        x = (pos_ref[0] + s) & 3
        at = pl.ds(pl.multiple_of(x * YROWS, 16), YROWS)
        ref[0:YROWS, :] = (a[at, :].astype(F32) + (b[at, :].astype(F32) + c[at, :].astype(F32))).astype(BF)
        at = pl.ds(pl.multiple_of(x * 32, 32), 32)
        rows = [proj_ref[i, at, :].astype(F32) for i in range(4)]
        rows = (rows[0] + rows[1]) + (rows[2] + rows[3])
        rows = jnp.concatenate([rows, gain], axis=0).astype(BF)
        ref[144:192, :] = rows[:, :512]
        ref[192:240, :] = rows[:, 512:1024]
        ref[240:288, 0:256] = rows[:, 1024:]
        ref[240:288, 256:512] = jnp.zeros((48, 256), BF)


def plane_sum_kernel(pos_ref, a0, a1, a2, a3, b0, b1, b2, b3, o0, o1, o2, o3, part, by_z):
    for at, refs in ((0, (a0, a1, a2, a3)), (HALF, (b0, b1, b2, b3))):
        p, q, r, t = [ref[0:YROWS, :].astype(F32) for ref in refs]
        part[:, at : at + HALF] = (p + q) + (r + t)
    for z in range(4):
        by_z[z, 0:36, :] = part[36 * z : 36 * z + 36, :]
    for s, ref in enumerate((o0, o1, o2, o3)):
        ref[...] = by_z[(pos_ref[3] + s) & 3, 0:36, :].astype(BF)


def conv_total_kernel(pos_ref, a, b, c, d, out_ref):
    out_ref[...] = (a[...].astype(F32) + b[...].astype(F32)) + (c[...].astype(F32) + d[...].astype(F32))


def proj_plane_kernel(pos_ref, a, b, c, d, out_ref, gains, part):
    rows = []
    for s, ref in enumerate((a, b, c, d)):
        got = jnp.concatenate(
            [ref[144:192, :], ref[192:240, :], ref[240:288, 0:256]], axis=1
        ).astype(F32)
        rows.append(got[0:32])
        gains[(pos_ref[0] - s) & 3] = got[32:40] + got[40:48]
    part[...] = (rows[0] + rows[1]) + (rows[2] + rows[3])
    gain = split_gain(((gains[0] + gains[1]) + (gains[2] + gains[3]))[0:1])
    gain = jnp.concatenate([gain[0:4], gain[8:12]], axis=0)
    for y in range(4):
        out_ref[y] = jnp.concatenate([part[8 * y : 8 * y + 8, :], gain], axis=0).astype(BF)


def proj_total_kernel(pos_ref, got_ref, out_ref, gain_ref):
    got = [got_ref[i].astype(F32) for i in range(4)]
    total = (got[0] + got[1]) + (got[2] + got[3])
    out_ref[...] = total[0:8]
    gain_ref[...] = total[8:9] + total[12:13]


def turn(axis, parts):
    return [parts[0]] + [
        lax.ppermute(parts[s], axis, [(i, (i + s) % 4) for i in range(4)]) for s in (1, 2, 3)
    ]


def per_device(pre_conv, conv_weight, proj_weight, norm_gain, slab_cotangent, page_tiles, block_dest):
    pos = jnp.stack([lax.axis_index(axis) for axis in ALL]).astype(jnp.int32)
    swap = functools.partial(lax.ppermute, axis_name="core", perm=[(0, 1), (1, 0)])
    cot = lax.all_to_all(slab_cotangent.reshape(16, 64, DM), ("y", "z"), 0, 0, tiled=True)
    own, other, values, proj_t = forward(
        pos, page_tiles, pre_conv.reshape(2048, CIN), conv_weight, proj_weight
    )
    other = swap(other)
    grads, gain, proj_t = norm(block_dest[:, 0], cot, values, norm_gain.reshape(1, DM), proj_t)
    gother, gain_other = swap(grads), swap(gain)

    gtok, mine, theirs, my_tokens, their_tokens = token_grad(grads, proj_t, own, other)
    *halves, gtok_other = conv_first(pos, mine, theirs, gtok, gother, proj_t, gain_other)
    proj = proj_grad(my_tokens, their_tokens, grads, gother, gain, gain_other, gtok_other)
    *shares, proj = conv_second(pos, mine, theirs, gtok, gtok_other, proj)
    proj = lax.all_to_all(proj, "z", 0, 0, tiled=True)
    first = relay("x", halves[:2], *shares[:3])
    second = relay("y", halves[2:], *shares[3:])

    plane = ((YROWS, HALF), BF)
    wide = ((2 * YROWS, HALF), BF)
    first = turn("y", small(first_sum_kernel, "first_sum", [plane] * 4, [pos, *first], flops=LONG))
    second = turn("x", small(second_sum_kernel, "second_sum", [wide] * 4, [pos, *second, proj], flops=LONG))
    (proj,) = small(
        proj_plane_kernel,
        "proj_plane",
        [((4, 16, DM), BF)],
        [pos, *second],
        [pltpu.VMEM((4, 8, DM), F32), pltpu.VMEM((32, DM), F32)],
    )
    proj = lax.all_to_all(proj, "y", 0, 0, tiled=True)
    grad_proj, grad_gain = small(
        proj_total_kernel, "proj_total", [((PROJ_ROWS, DM), F32), ((1, DM), F32)], [pos, proj]
    )
    both = small(
        plane_sum_kernel,
        "plane_sum",
        [((CONV_ROWS, COUT), BF)] * 4,
        [pos, *first, *second],
        [pltpu.VMEM((YROWS, COUT), F32), pltpu.VMEM((4, 40, COUT), F32)],
        flops=LONG,
    )
    (grad_conv,) = small(
        conv_total_kernel,
        "conv_total",
        [((CONV_ROWS, COUT), F32)],
        [pos, *turn("z", both)],
        flops=LONG,
    )
    return grad_conv, grad_proj, grad_gain.reshape(DM)


def solution(mesh):
    split = Mesh(mesh.devices.reshape(4, 2, 4, 4), ALL)
    return jax.shard_map(
        per_device,
        mesh=split,
        in_specs=(P(ALL), P(), P(), P(), P(ALL), P(ALL), P(ALL)),
        out_specs=(P(ALL), P(ALL), P()),
        check_vma=False,
    )
```

time: 154 us -> 135 us (0.88)
  blocking collectives: 81.8 us -> 0 us
  starting transfers between devices: 8.73 us -> 40.1 us
  waiting for transfers between devices: 21.4 us -> 43 us
  Pallas kernels: 36.5 us -> 47.8 us
  local copies, waits for them, and re-layouts: 2.8 us -> 1.08 us
    all_to_all x1 -> x0, blocking collectives: 81.8 us -> none  [per_device(): got = lax.all_to_all(chunks, CHIPS, 0, 0, tiled=True)]
    ppermute x2 -> x19, starting transfers between devices: 0.58 us -> 24.5 us  [the longest x9 10.7 us: turn(): lax.ppermute(parts[s], axis, [(i, (i + s) % 4) for i in range(4)])]
    ppermute x2 -> x19, waiting for transfers between devices: 2.59 us -> 21 us  [the longest x2 12.7 us: finish(): lax.ppermute(one, axis, forward)]
    pallas_call x3 -> x13, Pallas kernels: 18.9 us -> 29.2 us  [the longest x6 6.31 us: small(): pl.pallas_call(kernel, in_specs=[SMEM_SPEC] + [VMEM_SPEC] * (len(args) -...]
    all_to_all x0 -> x2, starting transfers between devices: none -> 7.46 us  [the longest x1 3.9 us: per_device(): proj = lax.all_to_all(proj, 'y', 0, 0, tiled=True)]
    all_to_all x0 -> x2, waiting for transfers between devices: none -> 4.89 us  [the longest x1 4.88 us: per_device(): proj = lax.all_to_all(proj, 'y', 0, 0, tiled=True)]
    unnamed x14 -> x10, local copies, waits for them, and re-layouts: 2.79 us -> 1.08 us
    all_to_all x1, waiting for transfers between devices: 18.8 us -> 17.2 us  [per_device(): lax.all_to_all(slab_cotangent.reshape(16, 64, DM), ('y', 'z'), 0, 0, tile...]
  transfers between devices with their start and end apart: 4 -> 23, of which waited for: 2 -> 8; matrix products, arithmetic and copies ran while one was open for 0% -> 0% of each run, Pallas kernels for 13% -> 31%
where the time goes in v2:
time: 135 us
  Pallas kernels  47.8 us (35%)
  waiting for transfers between devices  43 us (32%)
  starting transfers between devices  40.1 us (30%)
  between operations  1.5 us (1%)
    pallas_call x1, Pallas kernels, forward(): pl.pallas_call(forward_kernel, grid=(9,), in_specs=[smem, smem, pl.BlockS...  18.6 us
    all_to_all x1, waiting for transfers between devices, per_device(): lax.all_to_all(slab_cotangent.reshape(16, 64, DM), ('y', 'z'), 0, 0, tile...  17.2 us
    ppermute x2, waiting for transfers between devices, finish(): lax.ppermute(one, axis, forward)  12.7 us
    ppermute x9, starting transfers between devices, turn(): lax.ppermute(parts[s], axis, [(i, (i + s) % 4) for i in range(4)])  10.7 us
    ppermute x9, waiting for transfers between devices, turn(): lax.ppermute(parts[s], axis, [(i, (i + s) % 4) for i in range(4)])  8.21 us
    all_to_all x1, starting transfers between devices, per_device(): lax.all_to_all(slab_cotangent.reshape(16, 64, DM), ('y', 'z'), 0, 0, tile...  8.14 us
    pallas_call x6, Pallas kernels, small(): pl.pallas_call(kernel, in_specs=[SMEM_SPEC] + [VMEM_SPEC] * (len(args) -...  6.31 us
    ppermute x2, starting transfers between devices, finish(): lax.ppermute(other, axis, back)  6.18 us
  transfers between devices with their start and end apart: 23, of which 8 were waited for; matrix products, arithmetic and copies ran while one was open for 0% of the time, Pallas kernels for 31%

profile of v2, /device:TPU:0, one launch (start us, length us, event | category | flops | bytes accessed | tf_op | source)
XLA Modules:
  0.0 134.7 jit_solution(4849079681879081446)
XLA Ops:
  0.6 8.1 %all-to-all-start = ((bf16[16,64,1280]{2,1,0:T(8,128)(2,1)}), bf16[16,64,1280]{2,1,0:T(8,128)(2,1)S(1)}, u32[]{:S(2)}, u32[]{:S(2)}) async-start(bf16[16,64,1280]{2,1,0:T(8,128)(2,1)} %bitcast.9), calls=%async_computation | async-start | bytes 5242880 | tf_op jit(solution)/shard_map/all_to_all | solution.py:462
  9.4 0.6 pad_add_fusion.core_ref.pos_ref
  10.1 18.6 %forward.1 = (bf16[2816,512]{1,0:T(8,128)(2,1)}, bf16[2816,512]{1,0:T(8,128)(2,1)}, f32[512,1280]{1,0:T(8,128)}, bf16[1280,1024]{1,0:T(8,128)(2,1)}) custom-call(s32[4]{0:T(128)} %pad_add_fusion.core_ref.pos_ref, s32[1]{0:T(128)S(6)} %copy.20.pages_ref, bf16[2048,512]{1,0:T(8,128)(2,1)} %bitcast.11, bf16[4608,1024]{1,0:T(8,128)(2,1)} %w_ref.1, ...), custom_call_target="tpu_custom_call" | custom-call | flops 6200000000 | bytes 24000000 | tf_op jit(solution)/shard_map/forward/pallas_call | solution.py:109
  28.7 0.0 collective-permute-start
  28.7 17.2 %all-to-all-done.cot_ref = bf16[16,64,1280]{2,1,0:T(8,128)(2,1)S(1)} async-done(((bf16[16,64,1280]{2,1,0:T(8,128)(2,1)}), bf16[16,64,1280]{2,1,0:T(8,128)(2,1)S(1)}, u32[]{:S(2)}, u32[]{:S(2)}) %all-to-all-start) | async-done | bytes 2621472 | tf_op jit(solution)/shard_map/all_to_all | solution.py:462
  45.9 3.2 %norm_backward.1 = (bf16[512,1280]{1,0:T(8,128)(2,1)S(1)}, f32[8,1280]{1,0:T(8,128)S(1)}, bf16[1280,1024]{1,0:T(8,128)(2,1)S(1)}) custom-call(s32[8]{0:T(128)S(1)} %bitcast.8, bf16[16,64,1280]{2,1,0:T(8,128)(2,1)S(1)} %all-to-all-done.cot_ref, f32[8,64,1280]{2,1,0:T(8,128)} %bitcast.10, f32[1,1280]{1,0:T(1,128)S(1)} %reshape.24.gain_ref, ...), custom_call_target="tpu_custom_call" | custom-call | flops 8000000 | bytes 8000000 | tf_op jit(solution)/shard_map/norm_backward/pallas_call | solution.py:174
  49.0 0.1 collective-permute-start.1
  49.1 0.5 collective-permute-start.2
  49.6 0.0 collective-permute-done.other_hbm
  49.6 3.8 %token_grad.1 = (bf16[512,1024]{1,0:T(8,128)(2,1)S(1)}, bf16[4,576,512]{2,1,0:T(8,128)(2,1)S(1)}, bf16[4,576,512]{2,1,0:T(8,128)(2,1)S(1)}, bf16[512,512]{1,0:T(8,128)(2,1)S(1)}, bf16[512,512]{1,0:T(8,128)(2,1)S(1)}) custom-call(bf16[512,1280]{1,0:T(8,128)(2,1)S(1)} %get-tuple-element.47.grad_ref.gown, ...), custom_call_target="tpu_custom_call" | custom-call | flops 1340000000 | bytes 8000000 | tf_op jit(solution)/shard_map/token_grad/pallas_call | solution.py:209
  53.4 0.0 collective-permute-done.2.after.gain_other
  53.4 0.0 collective-permute-done.1.gother
  53.4 4.2 %conv_first.1 = (bf16[288,512]{1,0:T(8,128)(2,1)}, bf16[288,512]{1,0:T(8,128)(2,1)}, bf16[288,512]{1,0:T(8,128)(2,1)}, bf16[288,512]{1,0:T(8,128)(2,1)}, bf16[512,1024]{1,0:T(8,128)(2,1)S(1)}) custom-call(s32[4]{0:T(128)S(1)} %copy-done, bf16[4,576,512]{2,1,0:T(8,128)(2,1)S(1)} %get-tuple-element.51.own, bf16[4,576,512]{2,1,0:T(8,128)(2,1)S(1)} %get-tuple-element.52.other, ...), custom_call_target="tpu_custom_call" | custom-call | flops 2500000000 | bytes 2000000 | tf_op jit(solution)/shard_map/conv_first/pallas_call | solution.py:253
  57.6 0.1 collective-permute-start.10
  57.7 3.2 %collective-permute-start.11 = (bf16[288,512]{1,0:T(8,128)(2,1)}, bf16[288,512]{1,0:T(8,128)(2,1)S(1)}, u32[]{:S(2)}, u32[]{:S(2)}) collective-permute-start(bf16[288,512]{1,0:T(8,128)(2,1)} %get-tuple-element.73), channel_id=1, source_target_pairs={{0,12},{4,0},{8,4},{12,8},{1,13},{5,1},{9,5},{13,9},{2,14},{6,2},{... | collective-permute-start | bytes 884744 | tf_op jit(solution)/shard_map/ppermute | solution.py:316
  60.9 1.5 %collective-permute-start.3 = (bf16[288,512]{1,0:T(8,128)(2,1)}, bf16[288,512]{1,0:T(8,128)(2,1)S(1)}, u32[]{:S(2)}, u32[]{:S(2)}) collective-permute-start(bf16[288,512]{1,0:T(8,128)(2,1)} %get-tuple-element.61), channel_id=1, source_target_pairs={{0,32},{32,64},{64,96},{96,0},{1,33},{33,65},{65,97},{97,1},{2,34}... | collective-permute-start | bytes 884744 | tf_op jit(solution)/shard_map/ppermute | solution.py:315
  62.4 1.7 %collective-permute-start.4 = (bf16[288,512]{1,0:T(8,128)(2,1)}, bf16[288,512]{1,0:T(8,128)(2,1)S(1)}, u32[]{:S(2)}, u32[]{:S(2)}) collective-permute-start(bf16[288,512]{1,0:T(8,128)(2,1)} %get-tuple-element.62), channel_id=1, source_target_pairs={{0,96},{32,0},{64,32},{96,64},{1,97},{33,1},{65,33},{97,65},{2,98}... | collective-permute-start | bytes 884744 | tf_op jit(solution)/shard_map/ppermute | solution.py:316
  64.2 2.7 %proj_grad.1.through_in = bf16[4,144,1280]{2,1,0:T(8,128)(2,1)} custom-call(bf16[512,512]{1,0:T(8,128)(2,1)S(1)} %get-tuple-element.56.own, bf16[512,512]{1,0:T(8,128)(2,1)S(1)} %get-tuple-element.57.other, bf16[512,1280]{1,0:T(8,128)(2,1)S(1)} %get-tuple-element.47.grad_ref.gown, bf16[512,1280]{1,0:T(8,128)(2,1)S(1)} %collective-permute-done.1.gother, ...), custom_call_target="tpu_custom_call" | custom-call | flops 1400000000 | bytes 2000000 | tf_op jit(solution)/shard_map/proj_grad/pallas_call | solution.py:364
  66.9 5.2 %conv_second.1 = (bf16[576,512]{1,0:T(8,128)(2,1)}, bf16[576,512]{1,0:T(8,128)(2,1)}, bf16[576,512]{1,0:T(8,128)(2,1)}, bf16[576,512]{1,0:T(8,128)(2,1)}, bf16[5...) custom-call(s32[4]{0:T(128)S(1)} %copy-done, ...), custom_call_target="tpu_custom_call", output_to_operand_aliasing={{6}: (5, {})} | custom-call | flops 3700000000 | bytes 3000000 | tf_op jit(solution)/shard_map/conv_second/pallas_call | solution.py:279
  72.1 3.6 %all-to-all-start.1 = ((bf16[4,144,1280]{2,1,0:T(8,128)(2,1)}), bf16[4,144,1280]{2,1,0:T(8,128)(2,1)S(1)}, u32[]{:S(2)}, u32[]{:S(2)}) async-start(bf16[4,144,1280]{2,1,0:T(8,128)(2,1)} %get-tuple-element.76), calls=%async_computation.1 | async-start | bytes 2949120 | tf_op jit(solution)/shard_map/all_to_all | solution.py:474
  75.7 0.0 collective-permute-done.3.from_behind
  75.7 0.0 collective-permute-done.4.from_ahead
  75.7 1.9 %add_x.1 = (bf16[576,512]{1,0:T(8,128)(2,1)}, bf16[576,512]{1,0:T(8,128)(2,1)}) custom-call(bf16[576,512]{1,0:T(8,128)(2,1)} %get-tuple-element.59.ahead_in, bf16[576,512]{1,0:T(8,128)(2,1)} %get-tuple-element.60.behind_in, bf16[288,512]{1,0:T(8,128)(2,1)S(1)} %collective-permute-done.3.from_behind, ...), custom_call_target="tpu_custom_call", output_to_operand_aliasing={{0}: (0, {}), {1}: (1, {})} | custom-call | flops 20000000000 | bytes 3000000 | tf_op jit(solution)/shard_map/add_x/pallas_call | solution.py:319
  77.6 0.3 collective-permute-start.5
  78.0 3.0 %collective-permute-start.6 = (bf16[576,512]{1,0:T(8,128)(2,1)}, bf16[576,512]{1,0:T(8,128)(2,1)S(1)}, u32[]{:S(2)}, u32[]{:S(2)}) collective-permute-start(bf16[576,512]{1,0:T(8,128)(2,1)} %get-tuple-element.64), channel_id=1, source_target_pairs={{0,96},{32,0},{64,32},{96,64},{1,97},{33,1},{65,33},{97,65},{2,98}... | collective-permute-start | bytes 1769480 | tf_op jit(solution)/shard_map/ppermute | solution.py:330
  80.9 0.0 collective-permute-done.10.from_behind
  80.9 0.0 collective-permute-done.11.from_ahead
  81.0 2.0 %add_y.1 = (bf16[576,512]{1,0:T(8,128)(2,1)}, bf16[576,512]{1,0:T(8,128)(2,1)}) custom-call(bf16[576,512]{1,0:T(8,128)(2,1)} %get-tuple-element.70.ahead_in, bf16[576,512]{1,0:T(8,128)(2,1)} %get-tuple-element.71.behind_in, bf16[288,512]{1,0:T(8,128)(2,1)S(1)} %collective-permute-done.10.from_behind, ...), custom_call_target="tpu_custom_call", output_to_operand_aliasing={{0}: (0, {}), {1}: (1, {})} | custom-call | flops 20000000000 | bytes 3000000 | tf_op jit(solution)/shard_map/add_y/pallas_call | solution.py:319
  82.9 0.1 collective-permute-start.12
  83.0 3.2 %collective-permute-start.13 = (bf16[576,512]{1,0:T(8,128)(2,1)}, bf16[576,512]{1,0:T(8,128)(2,1)S(1)}, u32[]{:S(2)}, u32[]{:S(2)}) collective-permute-start(bf16[576,512]{1,0:T(8,128)(2,1)} %get-tuple-element.75), channel_id=1, source_target_pairs={{0,12},{4,0},{8,4},{12,8},{1,13},{5,1},{9,5},{13,9},{2,14},{6,2},{... | collective-permute-start | bytes 1769480 | tf_op jit(solution)/shard_map/ppermute | solution.py:330
  86.2 7.3 %collective-permute-done.5.b = bf16[576,512]{1,0:T(8,128)(2,1)S(1)} collective-permute-done((bf16[576,512]{1,0:T(8,128)(2,1)}, bf16[576,512]{1,0:T(8,128)(2,1)S(1)}, u32[]{:S(2)}, u32[]{:S(2)}) %collective-permute-start.5) | collective-permute-done | bytes 589856 | tf_op jit(solution)/shard_map/ppermute | solution.py:330
  93.5 0.0 collective-permute-done.6.c
  93.5 0.0 copy-done.3
  93.5 0.8 first_sum.1
  94.3 0.1 collective-permute-start.7
  94.4 5.4 %collective-permute-done.12.b = bf16[576,512]{1,0:T(8,128)(2,1)S(1)} collective-permute-done((bf16[576,512]{1,0:T(8,128)(2,1)}, bf16[576,512]{1,0:T(8,128)(2,1)S(1)}, u32[]{:S(2)}, u32[]{:S(2)}) %collective-permute-start.12) | collective-permute-done | bytes 589856 | tf_op jit(solution)/shard_map/ppermute | solution.py:330
  99.8 0.0 collective-permute-done.13.c
  99.8 0.0 all-to-all-done.1.proj_ref
  99.8 1.1 copy-done.2
  100.9 1.0 second_sum.1
  101.9 0.1 collective-permute-start.14
  101.9 0.3 collective-permute-start.15
  102.2 3.0 %collective-permute-start.16 = (bf16[288,512]{1,0:T(8,128)(2,1)S(1)}, bf16[288,512]{1,0:T(8,128)(2,1)S(1)}, u32[]{:S(2)}, u32[]{:S(2)}) collective-permute-start(bf16[288,512]{1,0:T(8,128)(2,1)S(1)} %get-tuple-element.80), channel_id=1, source_target_pairs={{0,96},{32,0},{64,32},{96,64},{1,97},{33,1},{65,33},{97,65},{2,98}... | collective-permute-start | bytes 884744 | tf_op jit(solution)/shard_map/ppermute | solution.py:455
  105.2 0.0 collective-permute-start.8
  105.2 0.0 collective-permute-done.7.a1
  105.2 1.7 %collective-permute-start.9 = (bf16[144,512]{1,0:T(8,128)(2,1)S(1)}, bf16[144,512]{1,0:T(8,128)(2,1)S(1)}, u32[]{:S(2)}, u32[]{:S(2)}) collective-permute-start(bf16[144,512]{1,0:T(8,128)(2,1)S(1)} %get-tuple-element.68), channel_id=1, source_target_pairs={{0,12},{4,0},{8,4},{12,8},{1,13},{5,1},{9,5},{13,9},{2,14},{6,2},{... | collective-permute-start | bytes 442376 | tf_op jit(solution)/shard_map/ppermute | solution.py:455
  106.9 4.9 %collective-permute-done.8.a2 = bf16[144,512]{1,0:T(8,128)(2,1)S(1)} collective-permute-done((bf16[144,512]{1,0:T(8,128)(2,1)S(1)}, bf16[144,512]{1,0:T(8,128)(2,1)S(1)}, u32[]{:S(2)}, u32[]{:S(2)}) %collective-permute-start.8) | collective-permute-done | bytes 147488 | tf_op jit(solution)/shard_map/ppermute | solution.py:455
  111.8 0.3 collective-permute-done.9.a3
  112.1 2.4 %collective-permute-done.14.b1.b = bf16[288,512]{1,0:T(8,128)(2,1)S(1)} collective-permute-done((bf16[288,512]{1,0:T(8,128)(2,1)S(1)}, bf16[288,512]{1,0:T(8,128)(2,1)S(1)}, u32[]{:S(2)}, u32[]{:S(2)}) %collective-permute-start.14) | collective-permute-done | bytes 294944 | tf_op jit(solution)/shard_map/ppermute | solution.py:455
  114.5 0.0 collective-permute-done.15.b2.c
  114.5 0.6 collective-permute-done.16.b3.d
  115.1 0.9 plane_sum.1
  116.0 1.5 %collective-permute-start.17 = (bf16[36,1024]{1,0:T(8,128)(2,1)S(1)}, bf16[36,1024]{1,0:T(8,128)(2,1)S(1)}, u32[]{:S(2)}, u32[]{:S(2)}) collective-permute-start(bf16[36,1024]{1,0:T(8,128)(2,1)S(1)} %get-tuple-element.82), channel_id=1, source_target_pairs={{0,1},{1,2},{2,3},{3,0},{4,5},{5,6},{6,7},{7,4},{8,9},{9,10},{10,1... | collective-permute-start | bytes 221192 | tf_op jit(solution)/shard_map/ppermute | solution.py:455
  117.5 2.7 %collective-permute-start.18 = (bf16[36,1024]{1,0:T(8,128)(2,1)S(1)}, bf16[36,1024]{1,0:T(8,128)(2,1)S(1)}, u32[]{:S(2)}, u32[]{:S(2)}) collective-permute-start(bf16[36,1024]{1,0:T(8,128)(2,1)S(1)} %get-tuple-element.83), channel_id=1, source_target_pairs={{0,2},{1,3},{2,0},{3,1},{4,6},{5,7},{6,4},{7,5},{8,10},{9,11},{10,... | collective-permute-start | bytes 221192 | tf_op jit(solution)/shard_map/ppermute | solution.py:455
  120.2 1.5 %collective-permute-start.19 = (bf16[36,1024]{1,0:T(8,128)(2,1)S(1)}, bf16[36,1024]{1,0:T(8,128)(2,1)S(1)}, u32[]{:S(2)}, u32[]{:S(2)}) collective-permute-start(bf16[36,1024]{1,0:T(8,128)(2,1)S(1)} %get-tuple-element.84), channel_id=1, source_target_pairs={{0,3},{1,0},{2,1},{3,2},{4,7},{5,4},{6,5},{7,6},{8,11},{9,8},{10,9... | collective-permute-start | bytes 221192 | tf_op jit(solution)/shard_map/ppermute | solution.py:455
  121.6 1.3 proj_plane.1
  122.9 3.9 %all-to-all-start.2 = ((bf16[4,16,1280]{2,1,0:T(8,128)(2,1)}), bf16[4,16,1280]{2,1,0:T(8,128)(2,1)S(1)}, u32[]{:S(2)}, u32[]{:S(2)}) async-start(bf16[4,16,1280]{2,1,0:T(8,128)(2,1)} %proj_plane.1), calls=%async_computation.2 | async-start | bytes 327680 | tf_op jit(solution)/shard_map/all_to_all | solution.py:489
  126.8 0.0 collective-permute-done.17.b
  126.8 0.0 collective-permute-done.18.c
  126.8 0.0 collective-permute-done.19.d
  126.8 1.2 conv_total.1
  128.1 4.9 %all-to-all-done.2.got_ref = bf16[4,16,1280]{2,1,0:T(8,128)(2,1)S(1)} async-done(((bf16[4,16,1280]{2,1,0:T(8,128)(2,1)}), bf16[4,16,1280]{2,1,0:T(8,128)(2,1)S(1)}, u32[]{:S(2)}, u32[]{:S(2)}) %all-to-all-start.2) | async-done | bytes 163872 | tf_op jit(solution)/shard_map/all_to_all | solution.py:489
  133.0 1.2 proj_total.1
  134.1 0.6 reduce
  (9 shorter events, 0.0 us)
Async XLA Ops:
  0.6 45.2 %all-to-all-start = ((bf16[16,64,1280]{2,1,0:T(8,128)(2,1)}), bf16[16,64,1280]{2,1,0:T(8,128)(2,1)S(1)}, u32[]{:S(2)}, u32[]{:S(2)}) async-start(bf16[16,64,1280]{2,1,0:T(8,128)(2,1)} %bitcast.9), calls=%async_computation | async-start | bytes 5242880 | tf_op jit(solution)/shard_map/all_to_all | solution.py:462
  10.0 18.6 %copy-start.4 = (f32[1280]{0:T(1024)S(1)}, f32[1280]{0:T(1024)}, u32[]{:S(2)}) copy-start(f32[1280]{0:T(1024)} %param.10) | copy-start | bytes 15364
  10.0 35.8 %copy-start.1 = (s32[8,1]{0,1:T(1,128)S(1)}, s32[8,1]{0,1:T(1,128)}, u32[]{:S(2)}) copy-start(s32[8,1]{0,1:T(1,128)} %param.13) | copy-start | bytes 100
  28.7 21.0 %collective-permute-start = (bf16[2816,512]{1,0:T(8,128)(2,1)}, bf16[2816,512]{1,0:T(8,128)(2,1)}, u32[]{:S(2)}, u32[]{:S(2)}) collective-permute-start(bf16[2816,512]{1,0:T(8,128)(2,1)} %get-tuple-element.50), channel_id=1, source_target_pairs={{0,16},{16,0},{1,17},{17,1},{2,18},{18,2},{3,19},{19,3},{4,20},{20... | collective-permute-start | bytes 8650760 | tf_op jit(solution)/shard_map/ppermute | solution.py:466
  49.0 4.4 %collective-permute-start.1 = (bf16[512,1280]{1,0:T(8,128)(2,1)S(1)}, bf16[512,1280]{1,0:T(8,128)(2,1)S(1)}, u32[]{:S(2)}, u32[]{:S(2)}) collective-permute-start(bf16[512,1280]{1,0:T(8,128)(2,1)S(1)} %get-tuple-element.47.grad_ref.gown), channel_id=1, source_target_pairs={{0,16},{16,0},{1,17},{17,1},{2,18},{18,2},{3,19},{19,3},{4,20},{20... | collective-permute-start | bytes 3932168 | tf_op jit(solution)/shard_map/ppermute | solution.py:468
  49.1 4.3 %collective-permute-start.2 = (f32[8,1280]{1,0:T(8,128)S(1)}, f32[8,1280]{1,0:T(8,128)S(1)}, u32[]{:S(2)}, u32[]{:S(2)}) collective-permute-start(f32[8,1280]{1,0:T(8,128)S(1)} %get-tuple-element.54.gain_own), channel_id=1, source_target_pairs={{0,16},{16,0},{1,17},{17,1},{2,18},{18,2},{3,19},{19,3},{4,20},{20... | collective-permute-start | bytes 122888 | tf_op jit(solution)/shard_map/ppermute | solution.py:468
  49.6 3.8 %copy-start = (s32[4]{0:T(128)S(1)}, s32[4]{0:T(128)}, u32[]{:S(2)}) copy-start(s32[4]{0:T(128)} %pad_add_fusion.core_ref.pos_ref) | copy-start | bytes 52
  57.6 23.3 %collective-permute-start.10 = (bf16[288,512]{1,0:T(8,128)(2,1)}, bf16[288,512]{1,0:T(8,128)(2,1)S(1)}, u32[]{:S(2)}, u32[]{:S(2)}) collective-permute-start(bf16[288,512]{1,0:T(8,128)(2,1)} %get-tuple-element.72), channel_id=1, source_target_pairs={{0,4},{4,8},{8,12},{12,0},{1,5},{5,9},{9,13},{13,1},{2,6},{6,10},{... | collective-permute-start | bytes 884744 | tf_op jit(solution)/shard_map/ppermute | solution.py:315
  57.7 23.3 %collective-permute-start.11 = (bf16[288,512]{1,0:T(8,128)(2,1)}, bf16[288,512]{1,0:T(8,128)(2,1)S(1)}, u32[]{:S(2)}, u32[]{:S(2)}) collective-permute-start(bf16[288,512]{1,0:T(8,128)(2,1)} %get-tuple-element.73), channel_id=1, source_target_pairs={{0,12},{4,0},{8,4},{12,8},{1,13},{5,1},{9,5},{13,9},{2,14},{6,2},{... | collective-permute-start | bytes 884744 | tf_op jit(solution)/shard_map/ppermute | solution.py:316
  60.9 14.8 %collective-permute-start.3 = (bf16[288,512]{1,0:T(8,128)(2,1)}, bf16[288,512]{1,0:T(8,128)(2,1)S(1)}, u32[]{:S(2)}, u32[]{:S(2)}) collective-permute-start(bf16[288,512]{1,0:T(8,128)(2,1)} %get-tuple-element.61), channel_id=1, source_target_pairs={{0,32},{32,64},{64,96},{96,0},{1,33},{33,65},{65,97},{97,1},{2,34}... | collective-permute-start | bytes 884744 | tf_op jit(solution)/shard_map/ppermute | solution.py:315
  62.4 13.3 %collective-permute-start.4 = (bf16[288,512]{1,0:T(8,128)(2,1)}, bf16[288,512]{1,0:T(8,128)(2,1)S(1)}, u32[]{:S(2)}, u32[]{:S(2)}) collective-permute-start(bf16[288,512]{1,0:T(8,128)(2,1)} %get-tuple-element.62), channel_id=1, source_target_pairs={{0,96},{32,0},{64,32},{96,64},{1,97},{33,1},{65,33},{97,65},{2,98}... | collective-permute-start | bytes 884744 | tf_op jit(solution)/shard_map/ppermute | solution.py:316
  72.1 27.7 %all-to-all-start.1 = ((bf16[4,144,1280]{2,1,0:T(8,128)(2,1)}), bf16[4,144,1280]{2,1,0:T(8,128)(2,1)S(1)}, u32[]{:S(2)}, u32[]{:S(2)}) async-start(bf16[4,144,1280]{2,1,0:T(8,128)(2,1)} %get-tuple-element.76), calls=%async_computation.1 | async-start | bytes 2949120 | tf_op jit(solution)/shard_map/all_to_all | solution.py:474
  77.6 15.9 %collective-permute-start.5 = (bf16[576,512]{1,0:T(8,128)(2,1)}, bf16[576,512]{1,0:T(8,128)(2,1)S(1)}, u32[]{:S(2)}, u32[]{:S(2)}) collective-permute-start(bf16[576,512]{1,0:T(8,128)(2,1)} %get-tuple-element.63), channel_id=1, source_target_pairs={{0,32},{32,64},{64,96},{96,0},{1,33},{33,65},{65,97},{97,1},{2,34}... | collective-permute-start | bytes 1769480 | tf_op jit(solution)/shard_map/ppermute | solution.py:330
  78.0 15.5 %collective-permute-start.6 = (bf16[576,512]{1,0:T(8,128)(2,1)}, bf16[576,512]{1,0:T(8,128)(2,1)S(1)}, u32[]{:S(2)}, u32[]{:S(2)}) collective-permute-start(bf16[576,512]{1,0:T(8,128)(2,1)} %get-tuple-element.64), channel_id=1, source_target_pairs={{0,96},{32,0},{64,32},{96,64},{1,97},{33,1},{65,33},{97,65},{2,98}... | collective-permute-start | bytes 1769480 | tf_op jit(solution)/shard_map/ppermute | solution.py:330
  80.9 12.6 %copy-start.3 = (bf16[576,512]{1,0:T(8,128)(2,1)S(1)}, bf16[576,512]{1,0:T(8,128)(2,1)}, u32[]{:S(2)}) copy-start(bf16[576,512]{1,0:T(8,128)(2,1)} %get-tuple-element.58.a) | copy-start | bytes 1769476
  82.9 16.9 %collective-permute-start.12 = (bf16[576,512]{1,0:T(8,128)(2,1)}, bf16[576,512]{1,0:T(8,128)(2,1)S(1)}, u32[]{:S(2)}, u32[]{:S(2)}) collective-permute-start(bf16[576,512]{1,0:T(8,128)(2,1)} %get-tuple-element.74), channel_id=1, source_target_pairs={{0,4},{4,8},{8,12},{12,0},{1,5},{5,9},{9,13},{13,1},{2,6},{6,10},{... | collective-permute-start | bytes 1769480 | tf_op jit(solution)/shard_map/ppermute | solution.py:330
  83.0 16.8 %collective-permute-start.13 = (bf16[576,512]{1,0:T(8,128)(2,1)}, bf16[576,512]{1,0:T(8,128)(2,1)S(1)}, u32[]{:S(2)}, u32[]{:S(2)}) collective-permute-start(bf16[576,512]{1,0:T(8,128)(2,1)} %get-tuple-element.75), channel_id=1, source_target_pairs={{0,12},{4,0},{8,4},{12,8},{1,13},{5,1},{9,5},{13,9},{2,14},{6,2},{... | collective-permute-start | bytes 1769480 | tf_op jit(solution)/shard_map/ppermute | solution.py:330
  94.3 10.9 %collective-permute-start.7 = (bf16[144,512]{1,0:T(8,128)(2,1)S(1)}, bf16[144,512]{1,0:T(8,128)(2,1)S(1)}, u32[]{:S(2)}, u32[]{:S(2)}) collective-permute-start(bf16[144,512]{1,0:T(8,128)(2,1)S(1)} %get-tuple-element.66), channel_id=1, source_target_pairs={{0,4},{4,8},{8,12},{12,0},{1,5},{5,9},{9,13},{13,1},{2,6},{6,10},{... | collective-permute-start | bytes 442376 | tf_op jit(solution)/shard_map/ppermute | solution.py:455
  99.8 1.1 copy-start.2
  101.9 12.6 %collective-permute-start.14 = (bf16[288,512]{1,0:T(8,128)(2,1)S(1)}, bf16[288,512]{1,0:T(8,128)(2,1)S(1)}, u32[]{:S(2)}, u32[]{:S(2)}) collective-permute-start(bf16[288,512]{1,0:T(8,128)(2,1)S(1)} %get-tuple-element.78), channel_id=1, source_target_pairs={{0,32},{32,64},{64,96},{96,0},{1,33},{33,65},{65,97},{97,1},{2,34}... | collective-permute-start | bytes 884744 | tf_op jit(solution)/shard_map/ppermute | solution.py:455
  101.9 12.6 %collective-permute-start.15 = (bf16[288,512]{1,0:T(8,128)(2,1)S(1)}, bf16[288,512]{1,0:T(8,128)(2,1)S(1)}, u32[]{:S(2)}, u32[]{:S(2)}) collective-permute-start(bf16[288,512]{1,0:T(8,128)(2,1)S(1)} %get-tuple-element.79), channel_id=1, source_target_pairs={{0,64},{32,96},{64,0},{96,32},{1,65},{33,97},{65,1},{97,33},{2,66}... | collective-permute-start | bytes 884744 | tf_op jit(solution)/shard_map/ppermute | solution.py:455
  102.2 12.9 %collective-permute-start.16 = (bf16[288,512]{1,0:T(8,128)(2,1)S(1)}, bf16[288,512]{1,0:T(8,128)(2,1)S(1)}, u32[]{:S(2)}, u32[]{:S(2)}) collective-permute-start(bf16[288,512]{1,0:T(8,128)(2,1)S(1)} %get-tuple-element.80), channel_id=1, source_target_pairs={{0,96},{32,0},{64,32},{96,64},{1,97},{33,1},{65,33},{97,65},{2,98}... | collective-permute-start | bytes 884744 | tf_op jit(solution)/shard_map/ppermute | solution.py:455
  105.2 6.6 %collective-permute-start.8 = (bf16[144,512]{1,0:T(8,128)(2,1)S(1)}, bf16[144,512]{1,0:T(8,128)(2,1)S(1)}, u32[]{:S(2)}, u32[]{:S(2)}) collective-permute-start(bf16[144,512]{1,0:T(8,128)(2,1)S(1)} %get-tuple-element.67), channel_id=1, source_target_pairs={{0,8},{4,12},{8,0},{12,4},{1,9},{5,13},{9,1},{13,5},{2,10},{6,14},... | collective-permute-start | bytes 442376 | tf_op jit(solution)/shard_map/ppermute | solution.py:455
  105.2 6.9 %collective-permute-start.9 = (bf16[144,512]{1,0:T(8,128)(2,1)S(1)}, bf16[144,512]{1,0:T(8,128)(2,1)S(1)}, u32[]{:S(2)}, u32[]{:S(2)}) collective-permute-start(bf16[144,512]{1,0:T(8,128)(2,1)S(1)} %get-tuple-element.68), channel_id=1, source_target_pairs={{0,12},{4,0},{8,4},{12,8},{1,13},{5,1},{9,5},{13,9},{2,14},{6,2},{... | collective-permute-start | bytes 442376 | tf_op jit(solution)/shard_map/ppermute | solution.py:455
  116.0 10.8 %collective-permute-start.17 = (bf16[36,1024]{1,0:T(8,128)(2,1)S(1)}, bf16[36,1024]{1,0:T(8,128)(2,1)S(1)}, u32[]{:S(2)}, u32[]{:S(2)}) collective-permute-start(bf16[36,1024]{1,0:T(8,128)(2,1)S(1)} %get-tuple-element.82), channel_id=1, source_target_pairs={{0,1},{1,2},{2,3},{3,0},{4,5},{5,6},{6,7},{7,4},{8,9},{9,10},{10,1... | collective-permute-start | bytes 221192 | tf_op jit(solution)/shard_map/ppermute | solution.py:455
  117.5 9.3 %collective-permute-start.18 = (bf16[36,1024]{1,0:T(8,128)(2,1)S(1)}, bf16[36,1024]{1,0:T(8,128)(2,1)S(1)}, u32[]{:S(2)}, u32[]{:S(2)}) collective-permute-start(bf16[36,1024]{1,0:T(8,128)(2,1)S(1)} %get-tuple-element.83), channel_id=1, source_target_pairs={{0,2},{1,3},{2,0},{3,1},{4,6},{5,7},{6,4},{7,5},{8,10},{9,11},{10,... | collective-permute-start | bytes 221192 | tf_op jit(solution)/shard_map/ppermute | solution.py:455
  120.2 6.7 %collective-permute-start.19 = (bf16[36,1024]{1,0:T(8,128)(2,1)S(1)}, bf16[36,1024]{1,0:T(8,128)(2,1)S(1)}, u32[]{:S(2)}, u32[]{:S(2)}) collective-permute-start(bf16[36,1024]{1,0:T(8,128)(2,1)S(1)} %get-tuple-element.84), channel_id=1, source_target_pairs={{0,3},{1,0},{2,1},{3,2},{4,7},{5,4},{6,5},{7,6},{8,11},{9,8},{10,9... | collective-permute-start | bytes 221192 | tf_op jit(solution)/shard_map/ppermute | solution.py:455
  122.9 10.0 %all-to-all-start.2 = ((bf16[4,16,1280]{2,1,0:T(8,128)(2,1)}), bf16[4,16,1280]{2,1,0:T(8,128)(2,1)S(1)}, u32[]{:S(2)}, u32[]{:S(2)}) async-start(bf16[4,16,1280]{2,1,0:T(8,128)(2,1)} %proj_plane.1), calls=%async_computation.2 | async-start | bytes 327680 | tf_op jit(solution)/shard_map/all_to_all | solution.py:489

commit v3 on v2

--- a/solution.py
+++ b/solution.py
@@ -29,7 +29,10 @@
 YROWS = XCONV // 4
 HROWS = XCONV // 2
 HALF = COUT // 2
-LONG = 20_000_000_000
+COST_ADD = 1
+COST_SUM = 1
+COST_PROJ = 20000000000
+COST_SECOND = 20000000000
 
 
 def dot(a, b, dims):
@@ -143,7 +146,7 @@
     dest_ref, cot_ref, values_hbm, gain_ref, proj_t_hbm, grad_ref, gain_out_ref, proj_t_ref, values, sems
 ):
     copies = [pltpu.make_async_copy(values_hbm.at[k], values.at[k], sems.at[k]) for k in range(8)]
-    copies.append(pltpu.make_async_copy(proj_t_hbm, proj_t_ref, sems.at[8]))
+    copies.append(pltpu.make_async_copy(proj_t_hbm.at[:, pl.ds(0, HALF)], proj_t_ref, sems.at[8]))
     for copy in copies:
         copy.start()
     total = jnp.zeros((8, DM), F32)
@@ -178,7 +181,7 @@
         out_shape=[
             jax.ShapeDtypeStruct((512, DM), BF),
             jax.ShapeDtypeStruct((8, DM), F32),
-            pltpu.VMEM((DM, COUT), BF),
+            pltpu.VMEM((DM, HALF), BF),
         ],
         scratch_shapes=[pltpu.VMEM((8, 64, DM), F32), pltpu.SemaphoreType.DMA((9,))],
         compiler_params=pltpu.CompilerParams(vmem_limit_bytes=16 << 20),
@@ -187,37 +190,41 @@
     )(dest, cot, in_hbm(values.reshape(8, 64, DM)), gain, in_hbm(proj_t))
 
 
-def token_kernel(
-    grad_ref, proj_t_ref, own_hbm, other_hbm, out_ref, own_ref, other_ref, own_tok_ref, other_tok_ref, sems
-):
-    copies = []
-    for x in range(4):
-        rows = pl.ds(x * XCONV, XCONV)
-        copies.append(pltpu.make_async_copy(own_hbm.at[rows], own_ref.at[x], sems.at[0, x]))
-        copies.append(pltpu.make_async_copy(other_hbm.at[rows], other_ref.at[x], sems.at[1, x]))
-    rows = pl.ds(NX * XCONV, NX * XPROJ)
-    copies.append(pltpu.make_async_copy(own_hbm.at[rows], own_tok_ref, sems.at[0, 4]))
-    copies.append(pltpu.make_async_copy(other_hbm.at[rows], other_tok_ref, sems.at[1, 4]))
-    for copy in copies:
+def token_kernel(pos_ref, grad_ref, left_ref, proj_t_hbm, own_hbm, other_hbm, *rest):
+    out_ref, right_ref, sems = rest[0], rest[1], rest[6]
+    right = pltpu.make_async_copy(proj_t_hbm.at[:, pl.ds(HALF, HALF)], right_ref, sems.at[0, 0])
+    right.start()
+    copies = [right]
+    for i, hbm in enumerate((own_hbm, other_hbm)):
+        x = (pos_ref[0] + 2) & 3
+        y = (pos_ref[2] + 2) & 3
+        rows = pl.ds(pl.multiple_of(x * XCONV, 64), XCONV)
+        copies.append(pltpu.make_async_copy(hbm.at[rows], rest[2 + i], sems.at[0, 1 + i]))
+        for k in range(NX):
+            rows = pl.ds(pl.multiple_of(k * XCONV + y * YROWS, 16), YROWS)
+            to = rest[4 + i].at[pl.ds(k * YROWS, YROWS)]
+            copies.append(pltpu.make_async_copy(hbm.at[rows], to, sems.at[1 + i, k]))
+    for copy in copies[1:]:
         copy.start()
-    out_ref[...] = dot(grad_ref[...], proj_t_ref[...], ((1,), (0,))).astype(BF)
-    for copy in copies:
+    out_ref[:, :HALF] = dot(grad_ref[...], left_ref[...], ((1,), (0,))).astype(BF)
+    right.wait()
+    out_ref[:, HALF:] = dot(grad_ref[...], right_ref[...], ((1,), (0,))).astype(BF)
+    for copy in copies[1:]:
         copy.wait()
 
 
-def token_grad(grads, proj_t, own, other):
+def token_grad(pos, grads, left, proj_t, own, other):
     return pl.pallas_call(
         token_kernel,
-        in_specs=[VMEM_SPEC, VMEM_SPEC, HBM_SPEC, HBM_SPEC],
-        out_specs=[VMEM_SPEC] * 5,
-        out_shape=[jax.ShapeDtypeStruct((512, COUT), BF)]
-        + [pltpu.VMEM((NX, XCONV, 512), BF)] * 2
-        + [pltpu.VMEM((NX * XPROJ, 512), BF)] * 2,
-        scratch_shapes=[pltpu.SemaphoreType.DMA((2, 5))],
+        in_specs=[SMEM_SPEC, VMEM_SPEC, VMEM_SPEC, HBM_SPEC, HBM_SPEC, HBM_SPEC],
+        out_specs=[VMEM_SPEC] * 6,
+        out_shape=[jax.ShapeDtypeStruct((512, COUT), BF), pltpu.VMEM((DM, HALF), BF)]
+        + [pltpu.VMEM((XCONV, 512), BF)] * 4,
+        scratch_shapes=[pltpu.SemaphoreType.DMA((3, 4))],
         compiler_params=pltpu.CompilerParams(vmem_limit_bytes=16 << 20),
         cost_estimate=pl.CostEstimate(flops=1_340_000_000, bytes_accessed=8_000_000, transcendentals=0),
         name="token_grad",
-    )(grads, proj_t, in_hbm(own), in_hbm(other))
+    )(pos, grads, left, in_hbm(proj_t), in_hbm(own), in_hbm(other))
 
 
 def by_turn(axis, pos_ref, s, rows_ref):
@@ -227,66 +234,115 @@
     return jnp.concatenate([rows_ref[x, rows, :] for x in range(NX)], axis=0)
 
 
-def conv_block(axis, pos_ref, s, own, other, gtok, gtok_other):
-    at = pl.ds(axis * HALF // 2, HALF)
-    return (
-        dot(by_turn(axis, pos_ref, s, own), gtok[:, at], ((1,), (0,)))
-        + dot(by_turn(axis, pos_ref, s, other), gtok_other[:, at], ((1,), (0,)))
-    ).astype(BF)
-
-
-def conv_first_kernel(pos_ref, own, other, gtok, gother, proj_t, after, *rest):
-    outs, gtok_other, part, sems = rest[:4], rest[4], rest[5], rest[6]
-    gtok_other[...] = dot(gother[...], proj_t[...], ((1,), (0,))).astype(BF)
-    sends = []
-    for slot, axis in enumerate((0, 2)):
-        part[slot] = conv_block(axis, pos_ref, 2, own, other, gtok, gtok_other)
+def conv_first_kernel(gtok, gother, left, right, own_x, other_x, own_y, other_y, own_hbm, other_hbm, after, *rest):
+    outs, gtok_other, brought, gtok_hbm, gtok_other_hbm = rest[:4], rest[4], rest[5:7], rest[7], rest[8]
+    part, sems, in_sems, g_sems = rest[9:]
+    moves = [
+        pltpu.make_async_copy(hbm.at[pl.ds(NX * XCONV, NX * XPROJ)], brought[i], in_sems.at[i])
+        for i, hbm in enumerate((own_hbm, other_hbm))
+    ]
+    moves.append(pltpu.make_async_copy(gtok, gtok_hbm, g_sems.at[0]))
+    for copy in moves:
+        copy.start()
+    for slot, (weights, mine, theirs) in enumerate(((left, own_x, other_x), (right, own_y, other_y))):
+        at = pl.ds(slot * HALF, HALF)
+        gtok_other[:, at] = dot(gother[...], weights[...], ((1,), (0,))).astype(BF)
+        moves.append(pltpu.make_async_copy(gtok_other.at[:, at], gtok_other_hbm.at[:, at], g_sems.at[1 + slot]))
+        moves[-1].start()
+        part[slot] = (
+            dot(mine[...], gtok[:, at], ((1,), (0,))) + dot(theirs[...], gtok_other[:, at], ((1,), (0,)))
+        ).astype(BF)
         for half in range(2):
             rows = part.at[slot, pl.ds(half * HROWS, HROWS)]
-            sends.append(pltpu.make_async_copy(rows, outs[2 * slot + half], sems.at[slot, half]))
-            sends[-1].start()
-    for copy in sends:
+            moves.append(pltpu.make_async_copy(rows, outs[2 * slot + half], sems.at[slot, half]))
+            moves[-1].start()
+    for copy in moves:
         copy.wait()
 
 
-def conv_first(pos, own, other, gtok, gother, proj_t, after):
+def conv_first(gtok, gother, left, right, blocks, own, other, after):
     return pl.pallas_call(
         conv_first_kernel,
-        in_specs=[SMEM_SPEC] + [VMEM_SPEC] * 5 + [ANY_SPEC],
-        out_specs=[HBM_SPEC] * 4 + [VMEM_SPEC],
-        out_shape=[pltpu.HBM((HROWS, HALF), BF)] * 4 + [jax.ShapeDtypeStruct((512, COUT), BF)],
-        scratch_shapes=[pltpu.VMEM((2, XCONV, HALF), BF), pltpu.SemaphoreType.DMA((2, 2))],
+        in_specs=[VMEM_SPEC] * 8 + [HBM_SPEC] * 2 + [ANY_SPEC],
+        out_specs=[HBM_SPEC] * 4 + [VMEM_SPEC] * 3 + [HBM_SPEC] * 2,
+        out_shape=[pltpu.HBM((HROWS, HALF), BF)] * 4
+        + [jax.ShapeDtypeStruct((512, COUT), BF)]
+        + [pltpu.VMEM((NX * XPROJ, 512), BF)] * 2
+        + [pltpu.HBM((512, COUT), BF)] * 2,
+        scratch_shapes=[
+            pltpu.VMEM((2, XCONV, HALF), BF),
+            pltpu.SemaphoreType.DMA((2, 2)),
+            pltpu.SemaphoreType.DMA((2,)),
+            pltpu.SemaphoreType.DMA((3,)),
+        ],
         compiler_params=pltpu.CompilerParams(vmem_limit_bytes=16 << 20),
-        cost_estimate=pl.CostEstimate(flops=2_500_000_000, bytes_accessed=2_000_000, transcendentals=0),
+        cost_estimate=pl.CostEstimate(flops=2_500_000_000, bytes_accessed=8_000_000, transcendentals=0),
         name="conv_first",
-    )(pos, own, other, gtok, gother, proj_t, after)
-
-
-def conv_second_kernel(pos_ref, own, other, gtok, gtok_other, through_in, *rest):
-    outs, through_out, part, sems = rest[:6], rest[6], rest[7], rest[8]
+    )(gtok, gother, left, right, *blocks, in_hbm(own), in_hbm(other), after)
+
+
+def conv_second_kernel(pos_ref, own_hbm, other_hbm, gtok_hbm, gtok_other_hbm, after, *rest):
+    outs, own, other, gtok, gtok_other, part, sems, in_sems, g_sems = rest[:6], *rest[6:]
+    grads = [
+        pltpu.make_async_copy(gtok_hbm, gtok, g_sems.at[0]),
+        pltpu.make_async_copy(gtok_other_hbm, gtok_other, g_sems.at[1]),
+    ]
+    blocks = []
+    for s in (1, 3, 0, 2):
+        x = (pos_ref[0] + s) & 3
+        rows = pl.ds(pl.multiple_of(x * XCONV, 64), XCONV)
+        blocks.append(
+            [
+                pltpu.make_async_copy(hbm.at[rows], vmem.at[x], in_sems.at[i, s])
+                for i, (hbm, vmem) in enumerate(((own_hbm, own), (other_hbm, other)))
+            ]
+        )
+    for copy in (blocks[0][0], grads[0], blocks[0][1], grads[1], *blocks[1]):
+        copy.start()
     sends = []
     for axis in (0, 2):
         for s in (1, 3, 0):
             slot = len(sends)
-            part[slot] = conv_block(axis, pos_ref, s, own, other, gtok, gtok_other)
+            if slot == 0:
+                for copy in grads:
+                    copy.wait()
+            if slot < 2:
+                for copy in blocks[slot + 2]:
+                    copy.start()
+            for block in {0: blocks[:1], 1: blocks[1:2], 2: blocks[2:3], 3: blocks[3:]}.get(slot, []):
+                for copy in block:
+                    copy.wait()
+            at = pl.ds(axis * HALF // 2, HALF)
+            part[slot] = (
+                dot(by_turn(axis, pos_ref, s, own), gtok[:, at], ((1,), (0,)))
+                + dot(by_turn(axis, pos_ref, s, other), gtok_other[:, at], ((1,), (0,)))
+            ).astype(BF)
             sends.append(pltpu.make_async_copy(part.at[slot], outs[slot], sems.at[slot]))
             sends[-1].start()
     for copy in sends:
         copy.wait()
 
 
-def conv_second(pos, own, other, gtok, gtok_other, through):
+def conv_second(pos, own, other, gtok, gtok_other, after):
     return pl.pallas_call(
         conv_second_kernel,
-        in_specs=[SMEM_SPEC] + [VMEM_SPEC] * 4 + [HBM_SPEC],
-        out_specs=[HBM_SPEC] * 7,
-        out_shape=[pltpu.HBM((XCONV, HALF), BF)] * 6 + [pltpu.HBM(through.shape, through.dtype)],
-        input_output_aliases={5: 6},
-        scratch_shapes=[pltpu.VMEM((6, XCONV, HALF), BF), pltpu.SemaphoreType.DMA((6,))],
-        compiler_params=pltpu.CompilerParams(vmem_limit_bytes=16 << 20),
-        cost_estimate=pl.CostEstimate(flops=3_700_000_000, bytes_accessed=3_000_000, transcendentals=0),
+        in_specs=[SMEM_SPEC] + [HBM_SPEC] * 5,
+        out_specs=[HBM_SPEC] * 6,
+        out_shape=[pltpu.HBM((XCONV, HALF), BF)] * 6,
+        scratch_shapes=[
+            pltpu.VMEM((NX, XCONV, 512), BF),
+            pltpu.VMEM((NX, XCONV, 512), BF),
+            pltpu.VMEM((512, COUT), BF),
+            pltpu.VMEM((512, COUT), BF),
+            pltpu.VMEM((6, XCONV, HALF), BF),
+            pltpu.SemaphoreType.DMA((6,)),
+            pltpu.SemaphoreType.DMA((2, 4)),
+            pltpu.SemaphoreType.DMA((2,)),
+        ],
+        compiler_params=pltpu.CompilerParams(vmem_limit_bytes=24 << 20),
+        cost_estimate=pl.CostEstimate(flops=COST_SECOND, bytes_accessed=3_000_000, transcendentals=0),
         name="conv_second",
-    )(pos, own, other, gtok, gtok_other, in_hbm(through))
+    )(pos, *[in_hbm(a) for a in (own, other, gtok, gtok_other, after)])
 
 
 def add_kernel(ahead_in, behind_in, from_behind, from_ahead, ahead, behind, part, sems):
@@ -324,7 +380,7 @@
             input_output_aliases={0: 0, 1: 1},
             scratch_shapes=[pltpu.VMEM((2, HROWS, HALF), BF), pltpu.SemaphoreType.DMA((2, 2))],
             compiler_params=pltpu.CompilerParams(vmem_limit_bytes=16 << 20),
-            cost_estimate=pl.CostEstimate(flops=LONG, bytes_accessed=3_000_000, transcendentals=0),
+            cost_estimate=pl.CostEstimate(flops=COST_ADD, bytes_accessed=3_000_000, transcendentals=0),
             name="add_" + axis,
         )(in_hbm(ahead), in_hbm(behind), from_behind, from_ahead)
         return [here, lax.ppermute(one, axis, forward), lax.ppermute(other, axis, back)]
@@ -345,16 +401,17 @@
     )
 
 
-def proj_kernel(own, other, gown, gother, gain_own, gain_other, after, out_hbm, part, out, sem):
+def proj_kernel(own, other, gown, gother, gain_own, gain_other, after, out_hbm, stage, out, sem):
     gain = split_gain(gain_own[0:1] + gain_other[0:1]).astype(BF)
-    for z in range(4):
-        out[z, 128:144, :] = gain
     for x in range(4):
         rows = slice(x * XPROJ, (x + 1) * XPROJ)
-        part[...] = dot(own[rows, :], gown[...], ((1,), (0,))) + dot(other[rows, :], gother[...], ((1,), (0,)))
-        for z in range(4):
-            pick = [part[y * 32 + z * 8 : y * 32 + z * 8 + 8, :] for y in range(4)]
-            out[z, x * 32 : x * 32 + 32, :] = jnp.concatenate(pick, axis=0).astype(BF)
+        part = dot(own[rows, :], gown[...], ((1,), (0,))) + dot(other[rows, :], gother[...], ((1,), (0,)))
+        for y in range(4):
+            for z in range(4):
+                stage[z, y * 32 + x * 8 : y * 32 + x * 8 + 8, :] = part[y * 32 + z * 8 : y * 32 + z * 8 + 8]
+    for z in range(4):
+        out[z, 0:128, :] = stage[z].astype(BF)
+        out[z, 128:144, :] = gain
     copy = pltpu.make_async_copy(out, out_hbm, sem)
     copy.start()
     copy.wait()
@@ -367,12 +424,12 @@
         out_specs=HBM_SPEC,
         out_shape=pltpu.HBM((4, 144, DM), BF),
         scratch_shapes=[
-            pltpu.VMEM((XPROJ, DM), F32),
+            pltpu.VMEM((4, XPROJ, DM), F32),
             pltpu.VMEM((4, 144, DM), BF),
             pltpu.SemaphoreType.DMA,
         ],
         compiler_params=pltpu.CompilerParams(vmem_limit_bytes=16 << 20),
-        cost_estimate=pl.CostEstimate(flops=1_400_000_000, bytes_accessed=2_000_000, transcendentals=0),
+        cost_estimate=pl.CostEstimate(flops=COST_PROJ, bytes_accessed=2_000_000, transcendentals=0),
         name="proj_grad",
     )(own, other, gown, gother, gain_own, gain_other, after)
 
@@ -397,57 +454,60 @@
         ref[...] = (a[at, :].astype(F32) + (b[at, :].astype(F32) + c[at, :].astype(F32))).astype(BF)
 
 
-def second_sum_kernel(pos_ref, a, b, c, proj_ref, *outs):
-    gains = [proj_ref[i, 128:136, :].astype(F32) + proj_ref[i, 136:144, :].astype(F32) for i in range(4)]
+def sum_four(ref, rows, gain_rows):
+    got = [ref[i, 0:rows, :].astype(F32) for i in range(4)]
+    high, low = pl.ds(gain_rows, 8), pl.ds(gain_rows + 8, 8)
+    gains = [ref[i, high, :].astype(F32) + ref[i, low, :].astype(F32) for i in range(4)]
     gain = split_gain(((gains[0] + gains[1]) + (gains[2] + gains[3]))[0:1])
-    for s, ref in enumerate(outs):
-        x = (pos_ref[0] + s) & 3
-        at = pl.ds(pl.multiple_of(x * YROWS, 16), YROWS)
-        ref[0:YROWS, :] = (a[at, :].astype(F32) + (b[at, :].astype(F32) + c[at, :].astype(F32))).astype(BF)
-        at = pl.ds(pl.multiple_of(x * 32, 32), 32)
-        rows = [proj_ref[i, at, :].astype(F32) for i in range(4)]
-        rows = (rows[0] + rows[1]) + (rows[2] + rows[3])
-        rows = jnp.concatenate([rows, gain], axis=0).astype(BF)
-        ref[144:192, :] = rows[:, :512]
-        ref[192:240, :] = rows[:, 512:1024]
-        ref[240:288, 0:256] = rows[:, 1024:]
-        ref[240:288, 256:512] = jnp.zeros((48, 256), BF)
-
-
-def plane_sum_kernel(pos_ref, a0, a1, a2, a3, b0, b1, b2, b3, o0, o1, o2, o3, part, by_z):
+    return (got[0] + got[1]) + (got[2] + got[3]), gain
+
+
+def proj_sum_kernel(pos_ref, got_ref, out_ref, gains):
+    total, gain = sum_four(got_ref, 128, 128)
+    gains[...] = jnp.zeros_like(gains)
+    for t in range(DM // 128):
+        piece = slice(128 * t, 128 * t + 128)
+        gains[t : t + 1, 0:128] = gain[0:1, piece]
+        gains[t : t + 1, 128:256] = gain[8:9, piece]
+    for k in range(16):
+        rows = total[8 * k : 8 * k + 8]
+        halves = jnp.concatenate([rows[:, : DM // 2], rows[:, DM // 2 :]], axis=0)
+        out_ref[k] = jnp.concatenate([halves, gains[...]], axis=1).astype(BF)
+
+
+def second_sum_kernel(pos_ref, a, b, c, o0, o1, o2, o3, part, by_z):
+    part[...] = a[...].astype(F32) + (b[...].astype(F32) + c[...].astype(F32))
+    for x in range(4):
+        for z in range(4):
+            at = x * YROWS + z * CONV_ROWS
+            by_z[z, x * CONV_ROWS : (x + 1) * CONV_ROWS, :] = part[at : at + CONV_ROWS, :]
+    for s, ref in enumerate((o0, o1, o2, o3)):
+        ref[...] = by_z[(pos_ref[3] + s) & 3].astype(BF)
+
+
+def plane_sum_kernel(along, pos_ref, a, b, c, d, o0, o1, o2, o3, part, split):
+    part[...] = (a[...].astype(F32) + b[...].astype(F32)) + (c[...].astype(F32) + d[...].astype(F32))
+    for i in range(4):
+        split[i, 0:CONV_ROWS, :] = part[CONV_ROWS * i : CONV_ROWS * (i + 1), :]
+    for s, ref in enumerate((o0, o1, o2, o3)):
+        ref[...] = split[(pos_ref[along] + s) & 3, 0:CONV_ROWS, :].astype(BF)
+
+
+def conv_total_kernel(pos_ref, a0, a1, a2, a3, b0, b1, b2, b3, after, out_ref):
     for at, refs in ((0, (a0, a1, a2, a3)), (HALF, (b0, b1, b2, b3))):
-        p, q, r, t = [ref[0:YROWS, :].astype(F32) for ref in refs]
-        part[:, at : at + HALF] = (p + q) + (r + t)
-    for z in range(4):
-        by_z[z, 0:36, :] = part[36 * z : 36 * z + 36, :]
-    for s, ref in enumerate((o0, o1, o2, o3)):
-        ref[...] = by_z[(pos_ref[3] + s) & 3, 0:36, :].astype(BF)
-
-
-def conv_total_kernel(pos_ref, a, b, c, d, out_ref):
-    out_ref[...] = (a[...].astype(F32) + b[...].astype(F32)) + (c[...].astype(F32) + d[...].astype(F32))
-
-
-def proj_plane_kernel(pos_ref, a, b, c, d, out_ref, gains, part):
-    rows = []
-    for s, ref in enumerate((a, b, c, d)):
-        got = jnp.concatenate(
-            [ref[144:192, :], ref[192:240, :], ref[240:288, 0:256]], axis=1
-        ).astype(F32)
-        rows.append(got[0:32])
-        gains[(pos_ref[0] - s) & 3] = got[32:40] + got[40:48]
-    part[...] = (rows[0] + rows[1]) + (rows[2] + rows[3])
-    gain = split_gain(((gains[0] + gains[1]) + (gains[2] + gains[3]))[0:1])
-    gain = jnp.concatenate([gain[0:4], gain[8:12]], axis=0)
-    for y in range(4):
-        out_ref[y] = jnp.concatenate([part[8 * y : 8 * y + 8, :], gain], axis=0).astype(BF)
+        p, q, r, t = [ref[...].astype(F32) for ref in refs]
+        out_ref[:, at : at + HALF] = (p + q) + (r + t)
 
 
 def proj_total_kernel(pos_ref, got_ref, out_ref, gain_ref):
-    got = [got_ref[i].astype(F32) for i in range(4)]
-    total = (got[0] + got[1]) + (got[2] + got[3])
-    out_ref[...] = total[0:8]
-    gain_ref[...] = total[8:9] + total[12:13]
+    total = got_ref[0].astype(F32)
+    for i in range(1, 16):
+        total = total + got_ref[i].astype(F32)
+    out_ref[:, : DM // 2] = total[0:8, : DM // 2]
+    out_ref[:, DM // 2 :] = total[8:16, : DM // 2]
+    gains = total[:, DM // 2 : DM // 2 + 128] + total[:, DM // 2 + 128 :]
+    for t in range(DM // 128):
+        gain_ref[:, 128 * t : 128 * t + 128] = gains[t : t + 1]
 
 
 def turn(axis, parts):
@@ -464,46 +524,50 @@
         pos, page_tiles, pre_conv.reshape(2048, CIN), conv_weight, proj_weight
     )
     other = swap(other)
-    grads, gain, proj_t = norm(block_dest[:, 0], cot, values, norm_gain.reshape(1, DM), proj_t)
+    grads, gain, left = norm(block_dest[:, 0], cot, values, norm_gain.reshape(1, DM), proj_t)
     gother, gain_other = swap(grads), swap(gain)
 
-    gtok, mine, theirs, my_tokens, their_tokens = token_grad(grads, proj_t, own, other)
-    *halves, gtok_other = conv_first(pos, mine, theirs, gtok, gother, proj_t, gain_other)
+    gtok, right, *blocks = token_grad(pos, grads, left, proj_t, own, other)
+    *halves, gtok_other, my_tokens, their_tokens, gtok, gtok_far = conv_first(
+        gtok, gother, left, right, blocks, own, other, gain_other
+    )
     proj = proj_grad(my_tokens, their_tokens, grads, gother, gain, gain_other, gtok_other)
-    *shares, proj = conv_second(pos, mine, theirs, gtok, gtok_other, proj)
+    shares = conv_second(pos, own, other, gtok, gtok_far, proj)
     proj = lax.all_to_all(proj, "z", 0, 0, tiled=True)
     first = relay("x", halves[:2], *shares[:3])
     second = relay("y", halves[2:], *shares[3:])
 
     plane = ((YROWS, HALF), BF)
-    wide = ((2 * YROWS, HALF), BF)
-    first = turn("y", small(first_sum_kernel, "first_sum", [plane] * 4, [pos, *first], flops=LONG))
-    second = turn("x", small(second_sum_kernel, "second_sum", [wide] * 4, [pos, *second, proj], flops=LONG))
-    (proj,) = small(
-        proj_plane_kernel,
-        "proj_plane",
-        [((4, 16, DM), BF)],
+    (proj,) = small(proj_sum_kernel, "proj_sum", [((16, 16, DM // 2 + 256), BF)], [pos, proj], [pltpu.VMEM((16, 256), F32)])
+    first = turn("y", small(first_sum_kernel, "first_sum", [plane] * 4, [pos, *first], flops=COST_SUM))
+    second = small(
+        second_sum_kernel,
+        "second_sum",
+        [plane] * 4,
         [pos, *second],
-        [pltpu.VMEM((4, 8, DM), F32), pltpu.VMEM((32, DM), F32)],
-    )
-    proj = lax.all_to_all(proj, "y", 0, 0, tiled=True)
+        [pltpu.VMEM((XCONV, HALF), F32), pltpu.VMEM((4, YROWS, HALF), F32)],
+        flops=COST_SUM,
+    )
+    second = turn("z", second)
+    proj = lax.all_to_all(proj, ("y", "x"), 0, 0, tiled=True)
     grad_proj, grad_gain = small(
         proj_total_kernel, "proj_total", [((PROJ_ROWS, DM), F32), ((1, DM), F32)], [pos, proj]
     )
-    both = small(
-        plane_sum_kernel,
-        "plane_sum",
-        [((CONV_ROWS, COUT), BF)] * 4,
-        [pos, *first, *second],
-        [pltpu.VMEM((YROWS, COUT), F32), pltpu.VMEM((4, 40, COUT), F32)],
-        flops=LONG,
+    lines = ((CONV_ROWS, HALF), BF)
+    scratch = [pltpu.VMEM((YROWS, HALF), F32), pltpu.VMEM((4, 40, HALF), F32)]
+    second = small(
+        functools.partial(plane_sum_kernel, 0), "plane_sum_x", [lines] * 4, [pos, *second], scratch, flops=COST_SUM
+    )
+    first = small(
+        functools.partial(plane_sum_kernel, 3), "plane_sum_z", [lines] * 4, [pos, *first], scratch, flops=COST_SUM
     )
     (grad_conv,) = small(
         conv_total_kernel,
         "conv_total",
         [((CONV_ROWS, COUT), F32)],
-        [pos, *turn("z", both)],
-        flops=LONG,
+        [pos, *turn("z", first), *turn("x", second)],
+        flops=COST_SUM,
+        after=[grad_gain],
     )
     return grad_conv, grad_proj, grad_gain.reshape(DM)
 

time: 135 us -> 127 us (0.941)
  waiting for transfers between devices: 43 us -> 20.4 us
  starting transfers between devices: 40.1 us -> 51.5 us
  Pallas kernels: 47.8 us -> 51.2 us
    ppermute x9 -> x12, starting transfers between devices: 10.7 us -> 22.3 us  [turn(): lax.ppermute(parts[s], axis, [(i, (i + s) % 4) for i in range(4)])]
    ppermute x2, waiting for transfers between devices: 12.7 us -> 2.5 us  [finish(): lax.ppermute(one, axis, forward)]
    ppermute x9 -> x12, waiting for transfers between devices: 8.21 us -> 0.72 us  [turn(): lax.ppermute(parts[s], axis, [(i, (i + s) % 4) for i in range(4)])]
    all_to_all x1, waiting for transfers between devices: 4.88 us -> 0.01 us  [per_device(): proj = lax.all_to_all(proj, ('y', 'x'), 0, 0, tiled=True)]
    pallas_call x6 -> x7, Pallas kernels: 6.31 us -> 8.55 us  [small(): pl.pallas_call(kernel, in_specs=[SMEM_SPEC] + [VMEM_SPEC] * (len(args) -...]
  transfers between devices with their start and end apart: 23 -> 26, of which waited for: 8 -> 4; matrix products, arithmetic and copies ran while one was open for 0% -> 1% of each run, Pallas kernels for 31% -> 34%
where the time goes in v3:
time: 127 us; the launch traced here: 126 us
  starting transfers between devices  51.5 us (41%)
  Pallas kernels  51.2 us (40%)
  waiting for transfers between devices  20.4 us (16%)
  between operations  1.56 us (1%)
  other arithmetic  1.27 us (1%)
    ppermute x12, starting transfers between devices, turn(): lax.ppermute(parts[s], axis, [(i, (i + s) % 4) for i in range(4)])  22.3 us
    pallas_call x1, Pallas kernels, forward(): pl.pallas_call(forward_kernel, grid=(9,), in_specs=[smem, smem, pl.BlockS...  18.5 us
    all_to_all x1, waiting for transfers between devices, per_device(): lax.all_to_all(slab_cotangent.reshape(16, 64, DM), ('y', 'z'), 0, 0, tile...  17.2 us
    pallas_call x7, Pallas kernels, small(): pl.pallas_call(kernel, in_specs=[SMEM_SPEC] + [VMEM_SPEC] * (len(args) -...  8.55 us
    all_to_all x1, starting transfers between devices, per_device(): lax.all_to_all(slab_cotangent.reshape(16, 64, DM), ('y', 'z'), 0, 0, tile...  8.14 us
    pallas_call x1, Pallas kernels, conv_second(): pl.pallas_call(conv_second_kernel, in_specs=[SMEM_SPEC] + [HBM_SPEC] * 5,...  7.76 us
    ppermute x2, starting transfers between devices, finish(): lax.ppermute(other, axis, back)  6.2 us
    ppermute x2, starting transfers between devices, relay(): from_ahead = lax.ppermute(halves[1], axis, back)  4.98 us
  transfers between devices with their start and end apart: 26, of which 4 were waited for; matrix products, arithmetic and copies ran while one was open for 1% of the time, Pallas kernels for 34%

profile of v3, /device:TPU:0, one launch (start us, length us, event | category | flops | bytes accessed | tf_op | source)
XLA Modules:
  0.0 126.0 jit_solution(14000817362553100535)
XLA Ops:
  0.6 8.1 %all-to-all-start = ((bf16[16,64,1280]{2,1,0:T(8,128)(2,1)}), bf16[16,64,1280]{2,1,0:T(8,128)(2,1)S(1)}, u32[]{:S(2)}, u32[]{:S(2)}) async-start(bf16[16,64,1280]{2,1,0:T(8,128)(2,1)} %bitcast.9), calls=%async_computation | async-start | bytes 5242880 | tf_op jit(solution)/shard_map/all_to_all | solution.py:522
  9.4 0.7 pad_add_fusion.core_ref.pos_ref
  10.1 18.5 %forward.1 = (bf16[2816,512]{1,0:T(8,128)(2,1)}, bf16[2816,512]{1,0:T(8,128)(2,1)}, f32[512,1280]{1,0:T(8,128)}, bf16[1280,1024]{1,0:T(8,128)(2,1)}) custom-call(s32[4]{0:T(128)} %pad_add_fusion.core_ref.pos_ref, s32[1]{0:T(128)S(6)} %copy.18.pages_ref, bf16[2048,512]{1,0:T(8,128)(2,1)} %bitcast.11, bf16[4608,1024]{1,0:T(8,128)(2,1)} %w_ref.1, ...), custom_call_target="tpu_custom_call" | custom-call | flops 6200000000 | bytes 24000000 | tf_op jit(solution)/shard_map/forward/pallas_call | solution.py:112
  28.6 0.0 collective-permute-start
  28.7 17.2 %all-to-all-done.cot_ref = bf16[16,64,1280]{2,1,0:T(8,128)(2,1)S(1)} async-done(((bf16[16,64,1280]{2,1,0:T(8,128)(2,1)}), bf16[16,64,1280]{2,1,0:T(8,128)(2,1)S(1)}, u32[]{:S(2)}, u32[]{:S(2)}) %all-to-all-start) | async-done | bytes 2621472 | tf_op jit(solution)/shard_map/all_to_all | solution.py:522
  45.9 3.1 %norm_backward.1 = (bf16[512,1280]{1,0:T(8,128)(2,1)S(1)}, f32[8,1280]{1,0:T(8,128)S(1)}, bf16[1280,512]{1,0:T(8,128)(2,1)S(1)}) custom-call(s32[8]{0:T(128)S(1)} %bitcast.8, bf16[16,64,1280]{2,1,0:T(8,128)(2,1)S(1)} %all-to-all-done.cot_ref, f32[8,64,1280]{2,1,0:T(8,128)} %bitcast.10, f32[1,1280]{1,0:T(1,128)S(1)} %reshape.24.gain_ref, ...), custom_call_target="tpu_custom_call" | custom-call | flops 8000000 | bytes 8000000 | tf_op jit(solution)/shard_map/norm_backward/pallas_call | solution.py:177
  48.9 0.1 collective-permute-start.1
  49.0 0.5 collective-permute-start.2
  49.5 0.0 collective-permute-done.other_hbm
  49.5 2.8 %token_grad.1 = (bf16[512,1024]{1,0:T(8,128)(2,1)S(1)}, bf16[1280,512]{1,0:T(8,128)(2,1)S(1)}, bf16[576,512]{1,0:T(8,128)(2,1)S(1)}, bf16[576,512]{1,0:T(8,128)(...) custom-call(s32[4]{0:T(128)S(1)} %copy-done.2, ...), custom_call_target="tpu_custom_call" | custom-call | flops 1340000000 | bytes 8000000 | tf_op jit(solution)/shard_map/token_grad/pallas_call | solution.py:217
  52.4 0.0 collective-permute-done.2.after.gain_other
  52.4 0.0 collective-permute-done.1.gother
  52.4 3.9 %conv_first.1 = (bf16[288,512]{1,0:T(8,128)(2,1)}, bf16[288,512]{1,0:T(8,128)(2,1)}, bf16[288,512]{1,0:T(8,128)(2,1)}, bf16[288,512]{1,0:T(8,128)(2,1)}, bf16[51...) custom-call(bf16[512,1024]{1,0:T(8,128)(2,1)S(1)} %get-tuple-element, ...), custom_call_target="tpu_custom_call" | custom-call | flops 2500000000 | bytes 8000000 | tf_op jit(solution)/shard_map/conv_first/pallas_call | solution.py:264
  56.3 2.7 %proj_grad.1.after = bf16[4,144,1280]{2,1,0:T(8,128)(2,1)} custom-call(bf16[512,512]{1,0:T(8,128)(2,1)S(1)} %get-tuple-element.68.own, bf16[512,512]{1,0:T(8,128)(2,1)S(1)} %get-tuple-element.69.other, bf16[512,1280]{1,0:T(8,128)(2,1)S(1)} %get-tuple-element.57.grad_ref.gown, bf16[512,1280]{1,0:T(8,128)(2,1)S(1)} %collective-permute-done.1.gother, ...), custom_call_target="tpu_custom_call" | custom-call | flops 20000000000 | bytes 2000000 | tf_op jit(solution)/shard_map/proj_grad/pallas_call | solution.py:421
  59.0 3.7 %all-to-all-start.1 = ((bf16[4,144,1280]{2,1,0:T(8,128)(2,1)}), bf16[4,144,1280]{2,1,0:T(8,128)(2,1)S(1)}, u32[]{:S(2)}, u32[]{:S(2)}) async-start(bf16[4,144,1280]{2,1,0:T(8,128)(2,1)} %proj_grad.1.after), calls=%async_computation.1 | async-start | bytes 2949120 | tf_op jit(solution)/shard_map/all_to_all | solution.py:536
  62.7 1.6 %collective-permute-start.3 = (bf16[288,512]{1,0:T(8,128)(2,1)S(1)}, bf16[288,512]{1,0:T(8,128)(2,1)S(1)}, u32[]{:S(2)}, u32[]{:S(2)}) collective-permute-start(bf16[288,512]{1,0:T(8,128)(2,1)S(1)} %copy-done.6), channel_id=1, source_target_pairs={{0,32},{32,64},{64,96},{96,0},{1,33},{33,65},{65,97},{97,1},{2,34}... | collective-permute-start | bytes 884744 | tf_op jit(solution)/shard_map/ppermute | solution.py:371
  64.3 1.7 %collective-permute-start.4 = (bf16[288,512]{1,0:T(8,128)(2,1)S(1)}, bf16[288,512]{1,0:T(8,128)(2,1)S(1)}, u32[]{:S(2)}, u32[]{:S(2)}) collective-permute-start(bf16[288,512]{1,0:T(8,128)(2,1)S(1)} %copy-done.5), channel_id=1, source_target_pairs={{0,96},{32,0},{64,32},{96,64},{1,97},{33,1},{65,33},{97,65},{2,98}... | collective-permute-start | bytes 884744 | tf_op jit(solution)/shard_map/ppermute | solution.py:372
  66.1 0.0 collective-permute-start.13
  66.1 3.2 %collective-permute-start.14 = (bf16[288,512]{1,0:T(8,128)(2,1)S(1)}, bf16[288,512]{1,0:T(8,128)(2,1)S(1)}, u32[]{:S(2)}, u32[]{:S(2)}) collective-permute-start(bf16[288,512]{1,0:T(8,128)(2,1)S(1)} %copy-done.7), channel_id=1, source_target_pairs={{0,12},{4,0},{8,4},{12,8},{1,13},{5,1},{9,5},{13,9},{2,14},{6,2},{... | collective-permute-start | bytes 884744 | tf_op jit(solution)/shard_map/ppermute | solution.py:372
  69.3 7.8 %conv_second.1 = (bf16[576,512]{1,0:T(8,128)(2,1)}, bf16[576,512]{1,0:T(8,128)(2,1)}, bf16[576,512]{1,0:T(8,128)(2,1)}, bf16[576,512]{1,0:T(8,128)(2,1)}, bf16[5...) custom-call(s32[4]{0:T(128)S(1)} %copy-done.2, bf16[2816,512]{1,0:T(8,128)(2,1)} %get-tuple-element.53.own_hbm, ...), custom_call_target="tpu_custom_call" | custom-call | flops 20000000000 | bytes 3000000 | tf_op jit(solution)/shard_map/conv_second/pallas_call | solution.py:327
  77.1 0.0 collective-permute-done.13.from_behind
  77.1 0.0 collective-permute-done.14.from_ahead
  77.1 1.9 %add_y.1 = (bf16[576,512]{1,0:T(8,128)(2,1)}, bf16[576,512]{1,0:T(8,128)(2,1)}) custom-call(bf16[576,512]{1,0:T(8,128)(2,1)} %get-tuple-element.87.ahead_in, bf16[576,512]{1,0:T(8,128)(2,1)} %get-tuple-element.88.behind_in, bf16[288,512]{1,0:T(8,128)(2,1)S(1)} %collective-permute-done.13.from_behind, ...), custom_call_target="tpu_custom_call", output_to_operand_aliasing={{0}: (0, {}), {1}: (1, {})} | custom-call | flops 1 | bytes 3000000 | tf_op jit(solution)/shard_map/add_y/pallas_call | solution.py:375
  79.0 0.1 collective-permute-start.15
  79.1 3.2 %collective-permute-start.16 = (bf16[576,512]{1,0:T(8,128)(2,1)}, bf16[576,512]{1,0:T(8,128)(2,1)}, u32[]{:S(2)}, u32[]{:S(2)}) collective-permute-start(bf16[576,512]{1,0:T(8,128)(2,1)} %get-tuple-element.92), channel_id=1, source_target_pairs={{0,12},{4,0},{8,4},{12,8},{1,13},{5,1},{9,5},{13,9},{2,14},{6,2},{... | collective-permute-start | bytes 1769480 | tf_op jit(solution)/shard_map/ppermute | solution.py:386
  82.4 0.0 collective-permute-done.3.from_behind
  82.4 0.0 collective-permute-done.4.from_ahead
  82.4 1.9 %add_x.1 = (bf16[576,512]{1,0:T(8,128)(2,1)}, bf16[576,512]{1,0:T(8,128)(2,1)}) custom-call(bf16[576,512]{1,0:T(8,128)(2,1)} %get-tuple-element.72.ahead_in, bf16[576,512]{1,0:T(8,128)(2,1)} %get-tuple-element.73.behind_in, bf16[288,512]{1,0:T(8,128)(2,1)S(1)} %collective-permute-done.3.from_behind, ...), custom_call_target="tpu_custom_call", output_to_operand_aliasing={{0}: (0, {}), {1}: (1, {})} | custom-call | flops 1 | bytes 3000000 | tf_op jit(solution)/shard_map/add_x/pallas_call | solution.py:375
  84.3 0.3 collective-permute-start.5
  84.6 3.0 %collective-permute-start.6 = (bf16[576,512]{1,0:T(8,128)(2,1)}, bf16[576,512]{1,0:T(8,128)(2,1)}, u32[]{:S(2)}, u32[]{:S(2)}) collective-permute-start(bf16[576,512]{1,0:T(8,128)(2,1)} %get-tuple-element.77), channel_id=1, source_target_pairs={{0,96},{32,0},{64,32},{96,64},{1,97},{33,1},{65,33},{97,65},{2,98}... | collective-permute-start | bytes 1769480 | tf_op jit(solution)/shard_map/ppermute | solution.py:386
  87.6 0.0 all-to-all-done.1.got_ref
  87.6 1.7 %proj_sum.1 = bf16[16,16,896]{2,1,0:T(8,128)(2,1)} custom-call(s32[4]{0:T(128)S(1)} %copy-done.2, bf16[4,144,1280]{2,1,0:T(8,128)(2,1)S(1)} %all-to-all-done.1.got_ref), custom_call_target="tpu_custom_call" | custom-call | flops 1000000 | bytes 1474576 | tf_op jit(solution)/shard_map/proj_sum/pallas_call | solution.py:439
  89.3 3.6 %all-to-all-start.2 = ((bf16[16,16,896]{2,1,0:T(8,128)(2,1)}), bf16[16,16,896]{2,1,0:T(8,128)(2,1)S(1)}, u32[]{:S(2)}, u32[]{:S(2)}) async-start(bf16[16,16,896]{2,1,0:T(8,128)(2,1)} %proj_sum.1), calls=%async_computation.2 | async-start | bytes 917504 | tf_op jit(solution)/shard_map/all_to_all | solution.py:552
  92.9 2.3 %collective-permute-done.15.b = bf16[576,512]{1,0:T(8,128)(2,1)} collective-permute-done((bf16[576,512]{1,0:T(8,128)(2,1)}, bf16[576,512]{1,0:T(8,128)(2,1)}, u32[]{:S(2)}, u32[]{:S(2)}) %collective-permute-start.15) | collective-permute-done | bytes 589856 | tf_op jit(solution)/shard_map/ppermute | solution.py:386
  95.1 0.0 collective-permute-done.16.c
  95.1 1.8 %second_sum.1 = (bf16[144,512]{1,0:T(8,128)(2,1)S(1)}, bf16[144,512]{1,0:T(8,128)(2,1)S(1)}, bf16[144,512]{1,0:T(8,128)(2,1)S(1)}, bf16[144,512]{1,0:T(8,128)(2,1)S(1)}) custom-call(s32[4]{0:T(128)S(1)} %copy-done.2, bf16[576,512]{1,0:T(8,128)(2,1)S(1)} %copy-done.1, bf16[576,512]{1,0:T(8,128)(2,1)} %collective-permute-done.15.b, ...), custom_call_target="tpu_custom_call" | custom-call | flops 1 | bytes 1769488 | tf_op jit(solution)/shard_map/second_sum/pallas_call | solution.py:439
  96.9 1.7 %collective-permute-start.17 = (bf16[144,512]{1,0:T(8,128)(2,1)S(1)}, bf16[144,512]{1,0:T(8,128)(2,1)S(1)}, u32[]{:S(2)}, u32[]{:S(2)}) collective-permute-start(bf16[144,512]{1,0:T(8,128)(2,1)S(1)} %get-tuple-element.94), channel_id=1, source_target_pairs={{0,1},{1,2},{2,3},{3,0},{4,5},{5,6},{6,7},{7,4},{8,9},{9,10},{10,1... | collective-permute-start | bytes 442376 | tf_op jit(solution)/shard_map/ppermute | solution.py:515
  98.6 2.7 %collective-permute-start.18 = (bf16[144,512]{1,0:T(8,128)(2,1)S(1)}, bf16[144,512]{1,0:T(8,128)(2,1)S(1)}, u32[]{:S(2)}, u32[]{:S(2)}) collective-permute-start(bf16[144,512]{1,0:T(8,128)(2,1)S(1)} %get-tuple-element.95), channel_id=1, source_target_pairs={{0,2},{1,3},{2,0},{3,1},{4,6},{5,7},{6,4},{7,5},{8,10},{9,11},{10,... | collective-permute-start | bytes 442376 | tf_op jit(solution)/shard_map/ppermute | solution.py:515
  101.3 1.5 %collective-permute-start.19 = (bf16[144,512]{1,0:T(8,128)(2,1)S(1)}, bf16[144,512]{1,0:T(8,128)(2,1)S(1)}, u32[]{:S(2)}, u32[]{:S(2)}) collective-permute-start(bf16[144,512]{1,0:T(8,128)(2,1)S(1)} %get-tuple-element.96), channel_id=1, source_target_pairs={{0,3},{1,0},{2,1},{3,2},{4,7},{5,4},{6,5},{7,6},{8,11},{9,8},{10,9... | collective-permute-start | bytes 442376 | tf_op jit(solution)/shard_map/ppermute | solution.py:515
  102.7 0.2 collective-permute-done.5.b
  103.0 0.0 collective-permute-done.6.c
  103.0 1.3 %first_sum.1 = (bf16[144,512]{1,0:T(8,128)(2,1)S(1)}, bf16[144,512]{1,0:T(8,128)(2,1)S(1)}, bf16[144,512]{1,0:T(8,128)(2,1)S(1)}, bf16[144,512]{1,0:T(8,128)(2,1)S(1)}) custom-call(s32[4]{0:T(128)S(1)} %copy-done.2, bf16[576,512]{1,0:T(8,128)(2,1)S(1)} %copy-done, bf16[576,512]{1,0:T(8,128)(2,1)S(1)} %collective-permute-done.5.b, ...), custom_call_target="tpu_custom_call" | custom-call | flops 1 | bytes 1769488 | tf_op jit(solution)/shard_map/first_sum/pallas_call | solution.py:439
  104.3 0.1 collective-permute-start.7
  104.4 4.7 %collective-permute-start.8 = (bf16[144,512]{1,0:T(8,128)(2,1)S(1)}, bf16[144,512]{1,0:T(8,128)(2,1)S(1)}, u32[]{:S(2)}, u32[]{:S(2)}) collective-permute-start(bf16[144,512]{1,0:T(8,128)(2,1)S(1)} %get-tuple-element.80), channel_id=1, source_target_pairs={{0,8},{4,12},{8,0},{12,4},{1,9},{5,13},{9,1},{13,5},{2,10},{6,14},... | collective-permute-start | bytes 442376 | tf_op jit(solution)/shard_map/ppermute | solution.py:515
  109.1 0.0 collective-permute-done.17.b
  109.1 0.0 collective-permute-start.9
  109.1 0.0 collective-permute-done.18.c
  109.1 0.0 collective-permute-done.19.d
  109.1 0.7 plane_sum_x.1
  109.8 0.6 collective-permute-start.20
  110.4 2.8 %collective-permute-start.21 = (bf16[36,512]{1,0:T(8,128)(2,1)S(1)}, bf16[36,512]{1,0:T(8,128)(2,1)S(1)}, u32[]{:S(2)}, u32[]{:S(2)}) collective-permute-start(bf16[36,512]{1,0:T(8,128)(2,1)S(1)} %get-tuple-element.99), channel_id=1, source_target_pairs={{0,64},{32,96},{64,0},{96,32},{1,65},{33,97},{65,1},{97,33},{2,66}... | collective-permute-start | bytes 110600 | tf_op jit(solution)/shard_map/ppermute | solution.py:515
  113.2 0.0 collective-permute-done.7.b
  113.2 2.5 %collective-permute-start.22 = (bf16[36,512]{1,0:T(8,128)(2,1)S(1)}, bf16[36,512]{1,0:T(8,128)(2,1)S(1)}, u32[]{:S(2)}, u32[]{:S(2)}) collective-permute-start(bf16[36,512]{1,0:T(8,128)(2,1)S(1)} %get-tuple-element.100), channel_id=1, source_target_pairs={{0,96},{32,0},{64,32},{96,64},{1,97},{33,1},{65,33},{97,65},{2,98}... | collective-permute-start | bytes 110600 | tf_op jit(solution)/shard_map/ppermute | solution.py:515
  115.7 0.7 plane_sum_z.1
  116.3 1.7 %collective-permute-start.10 = (bf16[36,512]{1,0:T(8,128)(2,1)S(1)}, bf16[36,512]{1,0:T(8,128)(2,1)S(1)}, u32[]{:S(2)}, u32[]{:S(2)}) collective-permute-start(bf16[36,512]{1,0:T(8,128)(2,1)S(1)} %get-tuple-element.83), channel_id=1, source_target_pairs={{0,1},{1,2},{2,3},{3,0},{4,5},{5,6},{6,7},{7,4},{8,9},{9,10},{10,1... | collective-permute-start | bytes 110600 | tf_op jit(solution)/shard_map/ppermute | solution.py:515
  118.0 2.7 %collective-permute-start.11 = (bf16[36,512]{1,0:T(8,128)(2,1)S(1)}, bf16[36,512]{1,0:T(8,128)(2,1)S(1)}, u32[]{:S(2)}, u32[]{:S(2)}) collective-permute-start(bf16[36,512]{1,0:T(8,128)(2,1)S(1)} %get-tuple-element.84), channel_id=1, source_target_pairs={{0,2},{1,3},{2,0},{3,1},{4,6},{5,7},{6,4},{7,5},{8,10},{9,11},{10,... | collective-permute-start | bytes 110600 | tf_op jit(solution)/shard_map/ppermute | solution.py:515
  120.7 1.5 %collective-permute-start.12 = (bf16[36,512]{1,0:T(8,128)(2,1)S(1)}, bf16[36,512]{1,0:T(8,128)(2,1)S(1)}, u32[]{:S(2)}, u32[]{:S(2)}) collective-permute-start(bf16[36,512]{1,0:T(8,128)(2,1)S(1)} %get-tuple-element.85), channel_id=1, source_target_pairs={{0,3},{1,0},{2,1},{3,2},{4,7},{5,4},{6,5},{7,6},{8,11},{9,8},{10,9... | collective-permute-start | bytes 110600 | tf_op jit(solution)/shard_map/ppermute | solution.py:515
  122.2 1.2 proj_total.1
  123.4 0.6 reduce
  124.0 0.0 collective-permute-done.21.b2
  124.0 0.0 collective-permute-done.22.b3
  124.0 0.0 collective-permute-done.10.a1
  124.0 0.7 collective-permute-done.12.a3
  124.7 1.2 conv_total.1
  (24 shorter events, 0.1 us)
Async XLA Ops:
  0.6 45.2 %all-to-all-start = ((bf16[16,64,1280]{2,1,0:T(8,128)(2,1)}), bf16[16,64,1280]{2,1,0:T(8,128)(2,1)S(1)}, u32[]{:S(2)}, u32[]{:S(2)}) async-start(bf16[16,64,1280]{2,1,0:T(8,128)(2,1)} %bitcast.9), calls=%async_computation | async-start | bytes 5242880 | tf_op jit(solution)/shard_map/all_to_all | solution.py:522
  10.1 18.6 %copy-start.4 = (f32[1280]{0:T(1024)S(1)}, f32[1280]{0:T(1024)}, u32[]{:S(2)}) copy-start(f32[1280]{0:T(1024)} %param.10) | copy-start | bytes 15364
  10.1 35.8 %copy-start.3 = (s32[8,1]{0,1:T(1,128)S(1)}, s32[8,1]{0,1:T(1,128)}, u32[]{:S(2)}) copy-start(s32[8,1]{0,1:T(1,128)} %param.13) | copy-start | bytes 100
  28.6 20.9 %collective-permute-start = (bf16[2816,512]{1,0:T(8,128)(2,1)}, bf16[2816,512]{1,0:T(8,128)(2,1)}, u32[]{:S(2)}, u32[]{:S(2)}) collective-permute-start(bf16[2816,512]{1,0:T(8,128)(2,1)} %get-tuple-element.54), channel_id=1, source_target_pairs={{0,16},{16,0},{1,17},{17,1},{2,18},{18,2},{3,19},{19,3},{4,20},{20... | collective-permute-start | bytes 8650760 | tf_op jit(solution)/shard_map/ppermute | solution.py:526
  45.9 3.7 %copy-start.2 = (s32[4]{0:T(128)S(1)}, s32[4]{0:T(128)}, u32[]{:S(2)}) copy-start(s32[4]{0:T(128)} %pad_add_fusion.core_ref.pos_ref) | copy-start | bytes 52
  48.9 3.5 %collective-permute-start.1 = (bf16[512,1280]{1,0:T(8,128)(2,1)S(1)}, bf16[512,1280]{1,0:T(8,128)(2,1)S(1)}, u32[]{:S(2)}, u32[]{:S(2)}) collective-permute-start(bf16[512,1280]{1,0:T(8,128)(2,1)S(1)} %get-tuple-element.57.grad_ref.gown), channel_id=1, source_target_pairs={{0,16},{16,0},{1,17},{17,1},{2,18},{18,2},{3,19},{19,3},{4,20},{20... | collective-permute-start | bytes 3932168 | tf_op jit(solution)/shard_map/ppermute | solution.py:528
  49.0 3.4 %collective-permute-start.2 = (f32[8,1280]{1,0:T(8,128)S(1)}, f32[8,1280]{1,0:T(8,128)S(1)}, u32[]{:S(2)}, u32[]{:S(2)}) collective-permute-start(f32[8,1280]{1,0:T(8,128)S(1)} %get-tuple-element.65.gain_own), channel_id=1, source_target_pairs={{0,16},{16,0},{1,17},{17,1},{2,18},{18,2},{3,19},{19,3},{4,20},{20... | collective-permute-start | bytes 122888 | tf_op jit(solution)/shard_map/ppermute | solution.py:528
  59.0 3.7 %copy-start.6 = (bf16[288,512]{1,0:T(8,128)(2,1)S(1)}, bf16[288,512]{1,0:T(8,128)(2,1)}, u32[]{:S(2)}) copy-start(bf16[288,512]{1,0:T(8,128)(2,1)} %get-tuple-element.74) | copy-start | bytes 884740
  59.0 5.3 %copy-start.5 = (bf16[288,512]{1,0:T(8,128)(2,1)S(1)}, bf16[288,512]{1,0:T(8,128)(2,1)}, u32[]{:S(2)}) copy-start(bf16[288,512]{1,0:T(8,128)(2,1)} %get-tuple-element.75) | copy-start | bytes 884740
  59.0 7.0 %copy-start.8 = (bf16[288,512]{1,0:T(8,128)(2,1)S(1)}, bf16[288,512]{1,0:T(8,128)(2,1)}, u32[]{:S(2)}) copy-start(bf16[288,512]{1,0:T(8,128)(2,1)} %get-tuple-element.89) | copy-start | bytes 884740
  59.0 7.0 %copy-start.7 = (bf16[288,512]{1,0:T(8,128)(2,1)S(1)}, bf16[288,512]{1,0:T(8,128)(2,1)}, u32[]{:S(2)}) copy-start(bf16[288,512]{1,0:T(8,128)(2,1)} %get-tuple-element.90) | copy-start | bytes 884740
  59.0 28.6 %all-to-all-start.1 = ((bf16[4,144,1280]{2,1,0:T(8,128)(2,1)}), bf16[4,144,1280]{2,1,0:T(8,128)(2,1)S(1)}, u32[]{:S(2)}, u32[]{:S(2)}) async-start(bf16[4,144,1280]{2,1,0:T(8,128)(2,1)} %proj_grad.1.after), calls=%async_computation.1 | async-start | bytes 2949120 | tf_op jit(solution)/shard_map/all_to_all | solution.py:536
  62.7 19.6 %collective-permute-start.3 = (bf16[288,512]{1,0:T(8,128)(2,1)S(1)}, bf16[288,512]{1,0:T(8,128)(2,1)S(1)}, u32[]{:S(2)}, u32[]{:S(2)}) collective-permute-start(bf16[288,512]{1,0:T(8,128)(2,1)S(1)} %copy-done.6), channel_id=1, source_target_pairs={{0,32},{32,64},{64,96},{96,0},{1,33},{33,65},{65,97},{97,1},{2,34}... | collective-permute-start | bytes 884744 | tf_op jit(solution)/shard_map/ppermute | solution.py:371
  64.3 18.0 %collective-permute-start.4 = (bf16[288,512]{1,0:T(8,128)(2,1)S(1)}, bf16[288,512]{1,0:T(8,128)(2,1)S(1)}, u32[]{:S(2)}, u32[]{:S(2)}) collective-permute-start(bf16[288,512]{1,0:T(8,128)(2,1)S(1)} %copy-done.5), channel_id=1, source_target_pairs={{0,96},{32,0},{64,32},{96,64},{1,97},{33,1},{65,33},{97,65},{2,98}... | collective-permute-start | bytes 884744 | tf_op jit(solution)/shard_map/ppermute | solution.py:372
  66.1 11.0 %collective-permute-start.13 = (bf16[288,512]{1,0:T(8,128)(2,1)S(1)}, bf16[288,512]{1,0:T(8,128)(2,1)S(1)}, u32[]{:S(2)}, u32[]{:S(2)}) collective-permute-start(bf16[288,512]{1,0:T(8,128)(2,1)S(1)} %copy-done.8), channel_id=1, source_target_pairs={{0,4},{4,8},{8,12},{12,0},{1,5},{5,9},{9,13},{13,1},{2,6},{6,10},{... | collective-permute-start | bytes 884744 | tf_op jit(solution)/shard_map/ppermute | solution.py:371
  66.1 11.0 %collective-permute-start.14 = (bf16[288,512]{1,0:T(8,128)(2,1)S(1)}, bf16[288,512]{1,0:T(8,128)(2,1)S(1)}, u32[]{:S(2)}, u32[]{:S(2)}) collective-permute-start(bf16[288,512]{1,0:T(8,128)(2,1)S(1)} %copy-done.7), channel_id=1, source_target_pairs={{0,12},{4,0},{8,4},{12,8},{1,13},{5,1},{9,5},{13,9},{2,14},{6,2},{... | collective-permute-start | bytes 884744 | tf_op jit(solution)/shard_map/ppermute | solution.py:372
  79.0 16.1 %copy-start.1 = (bf16[576,512]{1,0:T(8,128)(2,1)S(1)}, bf16[576,512]{1,0:T(8,128)(2,1)}, u32[]{:S(2)}) copy-start(bf16[576,512]{1,0:T(8,128)(2,1)} %get-tuple-element.86.a) | copy-start | bytes 1769476
  79.0 16.1 %collective-permute-start.15 = (bf16[576,512]{1,0:T(8,128)(2,1)}, bf16[576,512]{1,0:T(8,128)(2,1)}, u32[]{:S(2)}, u32[]{:S(2)}) collective-permute-start(bf16[576,512]{1,0:T(8,128)(2,1)} %get-tuple-element.91), channel_id=1, source_target_pairs={{0,4},{4,8},{8,12},{12,0},{1,5},{5,9},{9,13},{13,1},{2,6},{6,10},{... | collective-permute-start | bytes 1769480 | tf_op jit(solution)/shard_map/ppermute | solution.py:386
  79.1 16.0 %collective-permute-start.16 = (bf16[576,512]{1,0:T(8,128)(2,1)}, bf16[576,512]{1,0:T(8,128)(2,1)}, u32[]{:S(2)}, u32[]{:S(2)}) collective-permute-start(bf16[576,512]{1,0:T(8,128)(2,1)} %get-tuple-element.92), channel_id=1, source_target_pairs={{0,12},{4,0},{8,4},{12,8},{1,13},{5,1},{9,5},{13,9},{2,14},{6,2},{... | collective-permute-start | bytes 1769480 | tf_op jit(solution)/shard_map/ppermute | solution.py:386
  84.3 18.7 %copy-start = (bf16[576,512]{1,0:T(8,128)(2,1)S(1)}, bf16[576,512]{1,0:T(8,128)(2,1)}, u32[]{:S(2)}) copy-start(bf16[576,512]{1,0:T(8,128)(2,1)} %get-tuple-element.71.a) | copy-start | bytes 1769476
  84.3 18.7 %collective-permute-start.5 = (bf16[576,512]{1,0:T(8,128)(2,1)}, bf16[576,512]{1,0:T(8,128)(2,1)S(1)}, u32[]{:S(2)}, u32[]{:S(2)}) collective-permute-start(bf16[576,512]{1,0:T(8,128)(2,1)} %get-tuple-element.76), channel_id=1, source_target_pairs={{0,32},{32,64},{64,96},{96,0},{1,33},{33,65},{65,97},{97,1},{2,34}... | collective-permute-start | bytes 1769480 | tf_op jit(solution)/shard_map/ppermute | solution.py:386
  84.6 18.4 %collective-permute-start.6 = (bf16[576,512]{1,0:T(8,128)(2,1)}, bf16[576,512]{1,0:T(8,128)(2,1)}, u32[]{:S(2)}, u32[]{:S(2)}) collective-permute-start(bf16[576,512]{1,0:T(8,128)(2,1)} %get-tuple-element.77), channel_id=1, source_target_pairs={{0,96},{32,0},{64,32},{96,64},{1,97},{33,1},{65,33},{97,65},{2,98}... | collective-permute-start | bytes 1769480 | tf_op jit(solution)/shard_map/ppermute | solution.py:386
  89.3 32.9 %all-to-all-start.2 = ((bf16[16,16,896]{2,1,0:T(8,128)(2,1)}), bf16[16,16,896]{2,1,0:T(8,128)(2,1)S(1)}, u32[]{:S(2)}, u32[]{:S(2)}) async-start(bf16[16,16,896]{2,1,0:T(8,128)(2,1)} %proj_sum.1), calls=%async_computation.2 | async-start | bytes 917504 | tf_op jit(solution)/shard_map/all_to_all | solution.py:552
  96.9 12.1 %collective-permute-start.17 = (bf16[144,512]{1,0:T(8,128)(2,1)S(1)}, bf16[144,512]{1,0:T(8,128)(2,1)S(1)}, u32[]{:S(2)}, u32[]{:S(2)}) collective-permute-start(bf16[144,512]{1,0:T(8,128)(2,1)S(1)} %get-tuple-element.94), channel_id=1, source_target_pairs={{0,1},{1,2},{2,3},{3,0},{4,5},{5,6},{6,7},{7,4},{8,9},{9,10},{10,1... | collective-permute-start | bytes 442376 | tf_op jit(solution)/shard_map/ppermute | solution.py:515
  98.6 10.5 %collective-permute-start.18 = (bf16[144,512]{1,0:T(8,128)(2,1)S(1)}, bf16[144,512]{1,0:T(8,128)(2,1)S(1)}, u32[]{:S(2)}, u32[]{:S(2)}) collective-permute-start(bf16[144,512]{1,0:T(8,128)(2,1)S(1)} %get-tuple-element.95), channel_id=1, source_target_pairs={{0,2},{1,3},{2,0},{3,1},{4,6},{5,7},{6,4},{7,5},{8,10},{9,11},{10,... | collective-permute-start | bytes 442376 | tf_op jit(solution)/shard_map/ppermute | solution.py:515
  101.3 7.8 %collective-permute-start.19 = (bf16[144,512]{1,0:T(8,128)(2,1)S(1)}, bf16[144,512]{1,0:T(8,128)(2,1)S(1)}, u32[]{:S(2)}, u32[]{:S(2)}) collective-permute-start(bf16[144,512]{1,0:T(8,128)(2,1)S(1)} %get-tuple-element.96), channel_id=1, source_target_pairs={{0,3},{1,0},{2,1},{3,2},{4,7},{5,4},{6,5},{7,6},{8,11},{9,8},{10,9... | collective-permute-start | bytes 442376 | tf_op jit(solution)/shard_map/ppermute | solution.py:515
  104.3 8.9 %collective-permute-start.7 = (bf16[144,512]{1,0:T(8,128)(2,1)S(1)}, bf16[144,512]{1,0:T(8,128)(2,1)S(1)}, u32[]{:S(2)}, u32[]{:S(2)}) collective-permute-start(bf16[144,512]{1,0:T(8,128)(2,1)S(1)} %get-tuple-element.79), channel_id=1, source_target_pairs={{0,4},{4,8},{8,12},{12,0},{1,5},{5,9},{9,13},{13,1},{2,6},{6,10},{... | collective-permute-start | bytes 442376 | tf_op jit(solution)/shard_map/ppermute | solution.py:515
  104.4 11.3 %collective-permute-start.8 = (bf16[144,512]{1,0:T(8,128)(2,1)S(1)}, bf16[144,512]{1,0:T(8,128)(2,1)S(1)}, u32[]{:S(2)}, u32[]{:S(2)}) collective-permute-start(bf16[144,512]{1,0:T(8,128)(2,1)S(1)} %get-tuple-element.80), channel_id=1, source_target_pairs={{0,8},{4,12},{8,0},{12,4},{1,9},{5,13},{9,1},{13,5},{2,10},{6,14},... | collective-permute-start | bytes 442376 | tf_op jit(solution)/shard_map/ppermute | solution.py:515
  109.1 6.6 %collective-permute-start.9 = (bf16[144,512]{1,0:T(8,128)(2,1)S(1)}, bf16[144,512]{1,0:T(8,128)(2,1)S(1)}, u32[]{:S(2)}, u32[]{:S(2)}) collective-permute-start(bf16[144,512]{1,0:T(8,128)(2,1)S(1)} %get-tuple-element.81), channel_id=1, source_target_pairs={{0,12},{4,0},{8,4},{12,8},{1,13},{5,1},{9,5},{13,9},{2,14},{6,2},{... | collective-permute-start | bytes 442376 | tf_op jit(solution)/shard_map/ppermute | solution.py:515
  109.8 10.9 %collective-permute-start.20 = (bf16[36,512]{1,0:T(8,128)(2,1)S(1)}, bf16[36,512]{1,0:T(8,128)(2,1)S(1)}, u32[]{:S(2)}, u32[]{:S(2)}) collective-permute-start(bf16[36,512]{1,0:T(8,128)(2,1)S(1)} %get-tuple-element.98), channel_id=1, source_target_pairs={{0,32},{32,64},{64,96},{96,0},{1,33},{33,65},{65,97},{97,1},{2,34}... | collective-permute-start | bytes 110600 | tf_op jit(solution)/shard_map/ppermute | solution.py:515
  110.4 13.6 %collective-permute-start.21 = (bf16[36,512]{1,0:T(8,128)(2,1)S(1)}, bf16[36,512]{1,0:T(8,128)(2,1)S(1)}, u32[]{:S(2)}, u32[]{:S(2)}) collective-permute-start(bf16[36,512]{1,0:T(8,128)(2,1)S(1)} %get-tuple-element.99), channel_id=1, source_target_pairs={{0,64},{32,96},{64,0},{96,32},{1,65},{33,97},{65,1},{97,33},{2,66}... | collective-permute-start | bytes 110600 | tf_op jit(solution)/shard_map/ppermute | solution.py:515
  113.2 10.8 %collective-permute-start.22 = (bf16[36,512]{1,0:T(8,128)(2,1)S(1)}, bf16[36,512]{1,0:T(8,128)(2,1)S(1)}, u32[]{:S(2)}, u32[]{:S(2)}) collective-permute-start(bf16[36,512]{1,0:T(8,128)(2,1)S(1)} %get-tuple-element.100), channel_id=1, source_target_pairs={{0,96},{32,0},{64,32},{96,64},{1,97},{33,1},{65,33},{97,65},{2,98}... | collective-permute-start | bytes 110600 | tf_op jit(solution)/shard_map/ppermute | solution.py:515
  116.3 7.7 %collective-permute-start.10 = (bf16[36,512]{1,0:T(8,128)(2,1)S(1)}, bf16[36,512]{1,0:T(8,128)(2,1)S(1)}, u32[]{:S(2)}, u32[]{:S(2)}) collective-permute-start(bf16[36,512]{1,0:T(8,128)(2,1)S(1)} %get-tuple-element.83), channel_id=1, source_target_pairs={{0,1},{1,2},{2,3},{3,0},{4,5},{5,6},{6,7},{7,4},{8,9},{9,10},{10,1... | collective-permute-start | bytes 110600 | tf_op jit(solution)/shard_map/ppermute | solution.py:515
  118.0 6.0 %collective-permute-start.11 = (bf16[36,512]{1,0:T(8,128)(2,1)S(1)}, bf16[36,512]{1,0:T(8,128)(2,1)S(1)}, u32[]{:S(2)}, u32[]{:S(2)}) collective-permute-start(bf16[36,512]{1,0:T(8,128)(2,1)S(1)} %get-tuple-element.84), channel_id=1, source_target_pairs={{0,2},{1,3},{2,0},{3,1},{4,6},{5,7},{6,4},{7,5},{8,10},{9,11},{10,... | collective-permute-start | bytes 110600 | tf_op jit(solution)/shard_map/ppermute | solution.py:515
  120.7 4.0 %collective-permute-start.12 = (bf16[36,512]{1,0:T(8,128)(2,1)S(1)}, bf16[36,512]{1,0:T(8,128)(2,1)S(1)}, u32[]{:S(2)}, u32[]{:S(2)}) collective-permute-start(bf16[36,512]{1,0:T(8,128)(2,1)S(1)} %get-tuple-element.85), channel_id=1, source_target_pairs={{0,3},{1,0},{2,1},{3,2},{4,7},{5,4},{6,5},{7,6},{8,11},{9,8},{10,9... | collective-permute-start | bytes 110600 | tf_op jit(solution)/shard_map/ppermute | solution.py:515

commit v4 on v3

--- a/solution.py
+++ b/solution.py
@@ -191,7 +191,7 @@
 
 
 def token_kernel(pos_ref, grad_ref, left_ref, proj_t_hbm, own_hbm, other_hbm, *rest):
-    out_ref, right_ref, sems = rest[0], rest[1], rest[6]
+    out_ref, right_ref, sems = rest[0], rest[1], rest[8]
     right = pltpu.make_async_copy(proj_t_hbm.at[:, pl.ds(HALF, HALF)], right_ref, sems.at[0, 0])
     right.start()
     copies = [right]
@@ -204,6 +204,8 @@
             rows = pl.ds(pl.multiple_of(k * XCONV + y * YROWS, 16), YROWS)
             to = rest[4 + i].at[pl.ds(k * YROWS, YROWS)]
             copies.append(pltpu.make_async_copy(hbm.at[rows], to, sems.at[1 + i, k]))
+        rows = pl.ds(NX * XCONV, NX * XPROJ)
+        copies.append(pltpu.make_async_copy(hbm.at[rows], rest[6 + i], sems.at[3, i]))
     for copy in copies[1:]:
         copy.start()
     out_ref[:, :HALF] = dot(grad_ref[...], left_ref[...], ((1,), (0,))).astype(BF)
@@ -217,10 +219,11 @@
     return pl.pallas_call(
         token_kernel,
         in_specs=[SMEM_SPEC, VMEM_SPEC, VMEM_SPEC, HBM_SPEC, HBM_SPEC, HBM_SPEC],
-        out_specs=[VMEM_SPEC] * 6,
+        out_specs=[VMEM_SPEC] * 8,
         out_shape=[jax.ShapeDtypeStruct((512, COUT), BF), pltpu.VMEM((DM, HALF), BF)]
-        + [pltpu.VMEM((XCONV, 512), BF)] * 4,
-        scratch_shapes=[pltpu.SemaphoreType.DMA((3, 4))],
+        + [pltpu.VMEM((XCONV, 512), BF)] * 4
+        + [pltpu.VMEM((NX * XPROJ, 512), BF)] * 2,
+        scratch_shapes=[pltpu.SemaphoreType.DMA((4, 4))],
         compiler_params=pltpu.CompilerParams(vmem_limit_bytes=16 << 20),
         cost_estimate=pl.CostEstimate(flops=1_340_000_000, bytes_accessed=8_000_000, transcendentals=0),
         name="token_grad",
@@ -234,16 +237,13 @@
     return jnp.concatenate([rows_ref[x, rows, :] for x in range(NX)], axis=0)
 
 
-def conv_first_kernel(gtok, gother, left, right, own_x, other_x, own_y, other_y, own_hbm, other_hbm, after, *rest):
-    outs, gtok_other, brought, gtok_hbm, gtok_other_hbm = rest[:4], rest[4], rest[5:7], rest[7], rest[8]
-    part, sems, in_sems, g_sems = rest[9:]
-    moves = [
-        pltpu.make_async_copy(hbm.at[pl.ds(NX * XCONV, NX * XPROJ)], brought[i], in_sems.at[i])
-        for i, hbm in enumerate((own_hbm, other_hbm))
-    ]
-    moves.append(pltpu.make_async_copy(gtok, gtok_hbm, g_sems.at[0]))
-    for copy in moves:
-        copy.start()
+def conv_first_kernel(
+    gtok, gother, left, right, own_x, other_x, own_y, other_y, own_tok, other_tok, gown, gain_own, gain_other, *rest
+):
+    outs, gtok_hbm, gtok_other_hbm, proj_hbm = rest[:4], *rest[4:7]
+    gtok_other, part, stage, out, sems, g_sems = rest[7:]
+    moves = [pltpu.make_async_copy(gtok, gtok_hbm, g_sems.at[0])]
+    moves[0].start()
     for slot, (weights, mine, theirs) in enumerate(((left, own_x, other_x), (right, own_y, other_y))):
         at = pl.ds(slot * HALF, HALF)
         gtok_other[:, at] = dot(gother[...], weights[...], ((1,), (0,))).astype(BF)
@@ -256,29 +256,42 @@
             rows = part.at[slot, pl.ds(half * HROWS, HROWS)]
             moves.append(pltpu.make_async_copy(rows, outs[2 * slot + half], sems.at[slot, half]))
             moves[-1].start()
+    gain = split_gain(gain_own[0:1] + gain_other[0:1]).astype(BF)
+    for x in range(4):
+        rows = slice(x * XPROJ, (x + 1) * XPROJ)
+        share = dot(own_tok[rows, :], gown[...], ((1,), (0,))) + dot(other_tok[rows, :], gother[...], ((1,), (0,)))
+        for y in range(4):
+            for z in range(4):
+                stage[z, y * 32 + x * 8 : y * 32 + x * 8 + 8, :] = share[y * 32 + z * 8 : y * 32 + z * 8 + 8]
+    for z in range(4):
+        out[z, 0:128, :] = stage[z].astype(BF)
+        out[z, 128:144, :] = gain
+        moves.append(pltpu.make_async_copy(out.at[z], proj_hbm.at[z], g_sems.at[3 + z]))
+        moves[-1].start()
     for copy in moves:
         copy.wait()
 
 
-def conv_first(gtok, gother, left, right, blocks, own, other, after):
+def conv_first(gtok, gother, left, right, blocks, grads, gain, gain_other):
     return pl.pallas_call(
         conv_first_kernel,
-        in_specs=[VMEM_SPEC] * 8 + [HBM_SPEC] * 2 + [ANY_SPEC],
-        out_specs=[HBM_SPEC] * 4 + [VMEM_SPEC] * 3 + [HBM_SPEC] * 2,
+        in_specs=[VMEM_SPEC] * 13,
+        out_specs=[HBM_SPEC] * 7,
         out_shape=[pltpu.HBM((HROWS, HALF), BF)] * 4
-        + [jax.ShapeDtypeStruct((512, COUT), BF)]
-        + [pltpu.VMEM((NX * XPROJ, 512), BF)] * 2
-        + [pltpu.HBM((512, COUT), BF)] * 2,
+        + [pltpu.HBM((512, COUT), BF)] * 2
+        + [pltpu.HBM((4, 144, DM), BF)],
         scratch_shapes=[
+            pltpu.VMEM((512, COUT), BF),
             pltpu.VMEM((2, XCONV, HALF), BF),
+            pltpu.VMEM((4, XPROJ, DM), F32),
+            pltpu.VMEM((4, 144, DM), BF),
             pltpu.SemaphoreType.DMA((2, 2)),
-            pltpu.SemaphoreType.DMA((2,)),
-            pltpu.SemaphoreType.DMA((3,)),
-        ],
-        compiler_params=pltpu.CompilerParams(vmem_limit_bytes=16 << 20),
-        cost_estimate=pl.CostEstimate(flops=2_500_000_000, bytes_accessed=8_000_000, transcendentals=0),
+            pltpu.SemaphoreType.DMA((7,)),
+        ],
+        compiler_params=pltpu.CompilerParams(vmem_limit_bytes=24 << 20),
+        cost_estimate=pl.CostEstimate(flops=4_000_000_000, bytes_accessed=8_000_000, transcendentals=0),
         name="conv_first",
-    )(gtok, gother, left, right, *blocks, in_hbm(own), in_hbm(other), after)
+    )(gtok, gother, left, right, *blocks, grads, gain, gain_other)
 
 
 def conv_second_kernel(pos_ref, own_hbm, other_hbm, gtok_hbm, gtok_other_hbm, after, *rest):
@@ -297,7 +310,7 @@
                 for i, (hbm, vmem) in enumerate(((own_hbm, own), (other_hbm, other)))
             ]
         )
-    for copy in (blocks[0][0], grads[0], blocks[0][1], grads[1], *blocks[1]):
+    for copy in (grads[0], blocks[0][0], grads[1], blocks[0][1], *blocks[1], *blocks[2], *blocks[3]):
         copy.start()
     sends = []
     for axis in (0, 2):
@@ -306,9 +319,6 @@
             if slot == 0:
                 for copy in grads:
                     copy.wait()
-            if slot < 2:
-                for copy in blocks[slot + 2]:
-                    copy.start()
             for block in {0: blocks[:1], 1: blocks[1:2], 2: blocks[2:3], 3: blocks[3:]}.get(slot, []):
                 for copy in block:
                     copy.wait()
@@ -401,39 +411,6 @@
     )
 
 
-def proj_kernel(own, other, gown, gother, gain_own, gain_other, after, out_hbm, stage, out, sem):
-    gain = split_gain(gain_own[0:1] + gain_other[0:1]).astype(BF)
-    for x in range(4):
-        rows = slice(x * XPROJ, (x + 1) * XPROJ)
-        part = dot(own[rows, :], gown[...], ((1,), (0,))) + dot(other[rows, :], gother[...], ((1,), (0,)))
-        for y in range(4):
-            for z in range(4):
-                stage[z, y * 32 + x * 8 : y * 32 + x * 8 + 8, :] = part[y * 32 + z * 8 : y * 32 + z * 8 + 8]
-    for z in range(4):
-        out[z, 0:128, :] = stage[z].astype(BF)
-        out[z, 128:144, :] = gain
-    copy = pltpu.make_async_copy(out, out_hbm, sem)
-    copy.start()
-    copy.wait()
-
-
-def proj_grad(own, other, gown, gother, gain_own, gain_other, after):
-    return pl.pallas_call(
-        proj_kernel,
-        in_specs=[VMEM_SPEC] * 6 + [ANY_SPEC],
-        out_specs=HBM_SPEC,
-        out_shape=pltpu.HBM((4, 144, DM), BF),
-        scratch_shapes=[
-            pltpu.VMEM((4, XPROJ, DM), F32),
-            pltpu.VMEM((4, 144, DM), BF),
-            pltpu.SemaphoreType.DMA,
-        ],
-        compiler_params=pltpu.CompilerParams(vmem_limit_bytes=16 << 20),
-        cost_estimate=pl.CostEstimate(flops=COST_PROJ, bytes_accessed=2_000_000, transcendentals=0),
-        name="proj_grad",
-    )(own, other, gown, gother, gain_own, gain_other, after)
-
-
 def small(kernel, name, outs, args, scratch=(), mib=16, flops=1_000_000, after=()):
     bytes_in = sum(a.size * a.dtype.itemsize for a in args)
     return pl.pallas_call(
@@ -528,10 +505,7 @@
     gother, gain_other = swap(grads), swap(gain)
 
     gtok, right, *blocks = token_grad(pos, grads, left, proj_t, own, other)
-    *halves, gtok_other, my_tokens, their_tokens, gtok, gtok_far = conv_first(
-        gtok, gother, left, right, blocks, own, other, gain_other
-    )
-    proj = proj_grad(my_tokens, their_tokens, grads, gother, gain, gain_other, gtok_other)
+    *halves, gtok, gtok_far, proj = conv_first(gtok, gother, left, right, blocks, grads, gain, gain_other)
     shares = conv_second(pos, own, other, gtok, gtok_far, proj)
     proj = lax.all_to_all(proj, "z", 0, 0, tiled=True)
     first = relay("x", halves[:2], *shares[:3])

time: 127 us -> 126 us (level)
    pallas_call x2 -> x1, Pallas kernels: 6.57 us -> 5.48 us  [conv_first(): pl.pallas_call(conv_first_kernel, in_specs=[VMEM_SPEC] * 13, out_specs=[H...]
  transfers between devices with their start and end apart: 26 -> 26, of which waited for: 4 -> 4; matrix products, arithmetic and copies ran while one was open for 1% -> 1% of each run, Pallas kernels for 34% -> 35%
where the time goes in v4:
time: 126 us; the launch traced here: 125 us
  starting transfers between devices  51.5 us (41%)
  Pallas kernels  50.4 us (40%)
  waiting for transfers between devices  20.4 us (16%)
  between operations  1.55 us (1%)
  other arithmetic  1.27 us (1%)
    ppermute x12, starting transfers between devices, turn(): lax.ppermute(parts[s], axis, [(i, (i + s) % 4) for i in range(4)])  22.3 us
    pallas_call x1, Pallas kernels, forward(): pl.pallas_call(forward_kernel, grid=(9,), in_specs=[smem, smem, pl.BlockS...  18.5 us
    all_to_all x1, waiting for transfers between devices, per_device(): lax.all_to_all(slab_cotangent.reshape(16, 64, DM), ('y', 'z'), 0, 0, tile...  17.2 us
    pallas_call x7, Pallas kernels, small(): pl.pallas_call(kernel, in_specs=[SMEM_SPEC] + [VMEM_SPEC] * (len(args) -...  8.55 us
    all_to_all x1, starting transfers between devices, per_device(): lax.all_to_all(slab_cotangent.reshape(16, 64, DM), ('y', 'z'), 0, 0, tile...  8.14 us
    pallas_call x1, Pallas kernels, conv_second(): pl.pallas_call(conv_second_kernel, in_specs=[SMEM_SPEC] + [HBM_SPEC] * 5,...  7.75 us
    ppermute x2, starting transfers between devices, finish(): lax.ppermute(other, axis, back)  6.19 us
    pallas_call x1, Pallas kernels, conv_first(): pl.pallas_call(conv_first_kernel, in_specs=[VMEM_SPEC] * 13, out_specs=[H...  5.48 us
  transfers between devices with their start and end apart: 26, of which 4 were waited for; matrix products, arithmetic and copies ran while one was open for 1% of the time, Pallas kernels for 35%

profile of v4, /device:TPU:0, one launch (start us, length us, event | category | flops | bytes accessed | tf_op | source)
XLA Modules:
  0.0 125.1 jit_solution(6865319480169699763)
XLA Ops:
  0.6 8.1 %all-to-all-start = ((bf16[16,64,1280]{2,1,0:T(8,128)(2,1)}), bf16[16,64,1280]{2,1,0:T(8,128)(2,1)S(1)}, u32[]{:S(2)}, u32[]{:S(2)}) async-start(bf16[16,64,1280]{2,1,0:T(8,128)(2,1)} %bitcast.9), calls=%async_computation | async-start | bytes 5242880 | tf_op jit(solution)/shard_map/all_to_all | solution.py:499
  9.4 0.7 pad_add_fusion.core_ref.pos_ref
  10.1 18.5 %forward.1 = (bf16[2816,512]{1,0:T(8,128)(2,1)}, bf16[2816,512]{1,0:T(8,128)(2,1)}, f32[512,1280]{1,0:T(8,128)}, bf16[1280,1024]{1,0:T(8,128)(2,1)}) custom-call(s32[4]{0:T(128)} %pad_add_fusion.core_ref.pos_ref, s32[1]{0:T(128)S(6)} %copy.18.pages_ref, bf16[2048,512]{1,0:T(8,128)(2,1)} %bitcast.11, bf16[4608,1024]{1,0:T(8,128)(2,1)} %w_ref.1, ...), custom_call_target="tpu_custom_call" | custom-call | flops 6200000000 | bytes 24000000 | tf_op jit(solution)/shard_map/forward/pallas_call | solution.py:112
  28.6 0.0 collective-permute-start
  28.7 17.2 %all-to-all-done.cot_ref = bf16[16,64,1280]{2,1,0:T(8,128)(2,1)S(1)} async-done(((bf16[16,64,1280]{2,1,0:T(8,128)(2,1)}), bf16[16,64,1280]{2,1,0:T(8,128)(2,1)S(1)}, u32[]{:S(2)}, u32[]{:S(2)}) %all-to-all-start) | async-done | bytes 2621472 | tf_op jit(solution)/shard_map/all_to_all | solution.py:499
  45.9 3.1 %norm_backward.1 = (bf16[512,1280]{1,0:T(8,128)(2,1)S(1)}, f32[8,1280]{1,0:T(8,128)S(1)}, bf16[1280,512]{1,0:T(8,128)(2,1)S(1)}) custom-call(s32[8]{0:T(128)S(1)} %bitcast.8, bf16[16,64,1280]{2,1,0:T(8,128)(2,1)S(1)} %all-to-all-done.cot_ref, f32[8,64,1280]{2,1,0:T(8,128)} %bitcast.10, f32[1,1280]{1,0:T(1,128)S(1)} %reshape.24.gain_ref, ...), custom_call_target="tpu_custom_call" | custom-call | flops 8000000 | bytes 8000000 | tf_op jit(solution)/shard_map/norm_backward/pallas_call | solution.py:177
  48.9 0.1 collective-permute-start.1
  49.0 0.5 collective-permute-start.2
  49.5 0.0 collective-permute-done.other_hbm
  49.5 3.1 %token_grad.1 = (bf16[512,1024]{1,0:T(8,128)(2,1)S(1)}, bf16[1280,512]{1,0:T(8,128)(2,1)S(1)}, bf16[576,512]{1,0:T(8,128)(2,1)S(1)}, bf16[576,512]{1,0:T(8,128)(...) custom-call(s32[4]{0:T(128)S(1)} %copy-done.2, ...), custom_call_target="tpu_custom_call" | custom-call | flops 1340000000 | bytes 8000000 | tf_op jit(solution)/shard_map/token_grad/pallas_call | solution.py:219
  52.7 0.0 collective-permute-done.2.gain_other
  52.7 0.0 collective-permute-done.1.gother
  52.7 5.5 %conv_first.1 = (bf16[288,512]{1,0:T(8,128)(2,1)}, bf16[288,512]{1,0:T(8,128)(2,1)}, bf16[288,512]{1,0:T(8,128)(2,1)}, bf16[288,512]{1,0:T(8,128)(2,1)}, bf16[51...) custom-call(bf16[512,1024]{1,0:T(8,128)(2,1)S(1)} %get-tuple-element.59.gtok, ...), custom_call_target="tpu_custom_call" | custom-call | flops 4000000000 | bytes 8000000 | tf_op jit(solution)/shard_map/conv_first/pallas_call | solution.py:276
  58.2 3.7 %all-to-all-start.1 = ((bf16[4,144,1280]{2,1,0:T(8,128)(2,1)}), bf16[4,144,1280]{2,1,0:T(8,128)(2,1)S(1)}, u32[]{:S(2)}, u32[]{:S(2)}) async-start(bf16[4,144,1280]{2,1,0:T(8,128)(2,1)} %get-tuple-element.70.after), calls=%async_computation.1 | async-start | bytes 2949120 | tf_op jit(solution)/shard_map/all_to_all | solution.py:510
  61.9 1.6 %collective-permute-start.3 = (bf16[288,512]{1,0:T(8,128)(2,1)S(1)}, bf16[288,512]{1,0:T(8,128)(2,1)S(1)}, u32[]{:S(2)}, u32[]{:S(2)}) collective-permute-start(bf16[288,512]{1,0:T(8,128)(2,1)S(1)} %copy-done.6), channel_id=1, source_target_pairs={{0,32},{32,64},{64,96},{96,0},{1,33},{33,65},{65,97},{97,1},{2,34}... | collective-permute-start | bytes 884744 | tf_op jit(solution)/shard_map/ppermute | solution.py:381
  63.5 1.7 %collective-permute-start.4 = (bf16[288,512]{1,0:T(8,128)(2,1)S(1)}, bf16[288,512]{1,0:T(8,128)(2,1)S(1)}, u32[]{:S(2)}, u32[]{:S(2)}) collective-permute-start(bf16[288,512]{1,0:T(8,128)(2,1)S(1)} %copy-done.5), channel_id=1, source_target_pairs={{0,96},{32,0},{64,32},{96,64},{1,97},{33,1},{65,33},{97,65},{2,98}... | collective-permute-start | bytes 884744 | tf_op jit(solution)/shard_map/ppermute | solution.py:382
  65.2 0.0 collective-permute-start.13
  65.2 3.2 %collective-permute-start.14 = (bf16[288,512]{1,0:T(8,128)(2,1)S(1)}, bf16[288,512]{1,0:T(8,128)(2,1)S(1)}, u32[]{:S(2)}, u32[]{:S(2)}) collective-permute-start(bf16[288,512]{1,0:T(8,128)(2,1)S(1)} %copy-done.7), channel_id=1, source_target_pairs={{0,12},{4,0},{8,4},{12,8},{1,13},{5,1},{9,5},{13,9},{2,14},{6,2},{... | collective-permute-start | bytes 884744 | tf_op jit(solution)/shard_map/ppermute | solution.py:382
  68.5 7.8 %conv_second.1 = (bf16[576,512]{1,0:T(8,128)(2,1)}, bf16[576,512]{1,0:T(8,128)(2,1)}, bf16[576,512]{1,0:T(8,128)(2,1)}, bf16[576,512]{1,0:T(8,128)(2,1)}, bf16[5...) custom-call(s32[4]{0:T(128)S(1)} %copy-done.2, bf16[2816,512]{1,0:T(8,128)(2,1)} %get-tuple-element.53.own_hbm, ...), custom_call_target="tpu_custom_call" | custom-call | flops 20000000000 | bytes 3000000 | tf_op jit(solution)/shard_map/conv_second/pallas_call | solution.py:337
  76.2 0.0 collective-permute-done.13.from_behind
  76.3 0.0 collective-permute-done.14.from_ahead
  76.3 1.9 %add_y.1 = (bf16[576,512]{1,0:T(8,128)(2,1)}, bf16[576,512]{1,0:T(8,128)(2,1)}) custom-call(bf16[576,512]{1,0:T(8,128)(2,1)} %get-tuple-element.87.ahead_in, bf16[576,512]{1,0:T(8,128)(2,1)} %get-tuple-element.88.behind_in, bf16[288,512]{1,0:T(8,128)(2,1)S(1)} %collective-permute-done.13.from_behind, ...), custom_call_target="tpu_custom_call", output_to_operand_aliasing={{0}: (0, {}), {1}: (1, {})} | custom-call | flops 1 | bytes 3000000 | tf_op jit(solution)/shard_map/add_y/pallas_call | solution.py:385
  78.2 0.1 collective-permute-start.15
  78.3 3.2 %collective-permute-start.16 = (bf16[576,512]{1,0:T(8,128)(2,1)}, bf16[576,512]{1,0:T(8,128)(2,1)}, u32[]{:S(2)}, u32[]{:S(2)}) collective-permute-start(bf16[576,512]{1,0:T(8,128)(2,1)} %get-tuple-element.92), channel_id=1, source_target_pairs={{0,12},{4,0},{8,4},{12,8},{1,13},{5,1},{9,5},{13,9},{2,14},{6,2},{... | collective-permute-start | bytes 1769480 | tf_op jit(solution)/shard_map/ppermute | solution.py:396
  81.5 0.0 collective-permute-done.3.from_behind
  81.5 0.0 collective-permute-done.4.from_ahead
  81.5 1.9 %add_x.1 = (bf16[576,512]{1,0:T(8,128)(2,1)}, bf16[576,512]{1,0:T(8,128)(2,1)}) custom-call(bf16[576,512]{1,0:T(8,128)(2,1)} %get-tuple-element.72.ahead_in, bf16[576,512]{1,0:T(8,128)(2,1)} %get-tuple-element.73.behind_in, bf16[288,512]{1,0:T(8,128)(2,1)S(1)} %collective-permute-done.3.from_behind, ...), custom_call_target="tpu_custom_call", output_to_operand_aliasing={{0}: (0, {}), {1}: (1, {})} | custom-call | flops 1 | bytes 3000000 | tf_op jit(solution)/shard_map/add_x/pallas_call | solution.py:385
  83.5 0.3 collective-permute-start.5
  83.8 3.0 %collective-permute-start.6 = (bf16[576,512]{1,0:T(8,128)(2,1)}, bf16[576,512]{1,0:T(8,128)(2,1)}, u32[]{:S(2)}, u32[]{:S(2)}) collective-permute-start(bf16[576,512]{1,0:T(8,128)(2,1)} %get-tuple-element.77), channel_id=1, source_target_pairs={{0,96},{32,0},{64,32},{96,64},{1,97},{33,1},{65,33},{97,65},{2,98}... | collective-permute-start | bytes 1769480 | tf_op jit(solution)/shard_map/ppermute | solution.py:396
  86.8 0.0 all-to-all-done.1.got_ref
  86.8 1.7 %proj_sum.1 = bf16[16,16,896]{2,1,0:T(8,128)(2,1)} custom-call(s32[4]{0:T(128)S(1)} %copy-done.2, bf16[4,144,1280]{2,1,0:T(8,128)(2,1)S(1)} %all-to-all-done.1.got_ref), custom_call_target="tpu_custom_call" | custom-call | flops 1000000 | bytes 1474576 | tf_op jit(solution)/shard_map/proj_sum/pallas_call | solution.py:416
  88.5 3.6 %all-to-all-start.2 = ((bf16[16,16,896]{2,1,0:T(8,128)(2,1)}), bf16[16,16,896]{2,1,0:T(8,128)(2,1)S(1)}, u32[]{:S(2)}, u32[]{:S(2)}) async-start(bf16[16,16,896]{2,1,0:T(8,128)(2,1)} %proj_sum.1), calls=%async_computation.2 | async-start | bytes 917504 | tf_op jit(solution)/shard_map/all_to_all | solution.py:526
  92.0 2.3 %collective-permute-done.15.b = bf16[576,512]{1,0:T(8,128)(2,1)} collective-permute-done((bf16[576,512]{1,0:T(8,128)(2,1)}, bf16[576,512]{1,0:T(8,128)(2,1)}, u32[]{:S(2)}, u32[]{:S(2)}) %collective-permute-start.15) | collective-permute-done | bytes 589856 | tf_op jit(solution)/shard_map/ppermute | solution.py:396
  94.3 1.8 %second_sum.1 = (bf16[144,512]{1,0:T(8,128)(2,1)S(1)}, bf16[144,512]{1,0:T(8,128)(2,1)S(1)}, bf16[144,512]{1,0:T(8,128)(2,1)S(1)}, bf16[144,512]{1,0:T(8,128)(2,1)S(1)}) custom-call(s32[4]{0:T(128)S(1)} %copy-done.2, bf16[576,512]{1,0:T(8,128)(2,1)S(1)} %copy-done.1, bf16[576,512]{1,0:T(8,128)(2,1)} %collective-permute-done.15.b, ...), custom_call_target="tpu_custom_call" | custom-call | flops 1 | bytes 1769488 | tf_op jit(solution)/shard_map/second_sum/pallas_call | solution.py:416
  96.1 1.7 %collective-permute-start.17 = (bf16[144,512]{1,0:T(8,128)(2,1)S(1)}, bf16[144,512]{1,0:T(8,128)(2,1)S(1)}, u32[]{:S(2)}, u32[]{:S(2)}) collective-permute-start(bf16[144,512]{1,0:T(8,128)(2,1)S(1)} %get-tuple-element.94), channel_id=1, source_target_pairs={{0,1},{1,2},{2,3},{3,0},{4,5},{5,6},{6,7},{7,4},{8,9},{9,10},{10,1... | collective-permute-start | bytes 442376 | tf_op jit(solution)/shard_map/ppermute | solution.py:492
  97.8 2.7 %collective-permute-start.18 = (bf16[144,512]{1,0:T(8,128)(2,1)S(1)}, bf16[144,512]{1,0:T(8,128)(2,1)S(1)}, u32[]{:S(2)}, u32[]{:S(2)}) collective-permute-start(bf16[144,512]{1,0:T(8,128)(2,1)S(1)} %get-tuple-element.95), channel_id=1, source_target_pairs={{0,2},{1,3},{2,0},{3,1},{4,6},{5,7},{6,4},{7,5},{8,10},{9,11},{10,... | collective-permute-start | bytes 442376 | tf_op jit(solution)/shard_map/ppermute | solution.py:492
  100.5 1.5 %collective-permute-start.19 = (bf16[144,512]{1,0:T(8,128)(2,1)S(1)}, bf16[144,512]{1,0:T(8,128)(2,1)S(1)}, u32[]{:S(2)}, u32[]{:S(2)}) collective-permute-start(bf16[144,512]{1,0:T(8,128)(2,1)S(1)} %get-tuple-element.96), channel_id=1, source_target_pairs={{0,3},{1,0},{2,1},{3,2},{4,7},{5,4},{6,5},{7,6},{8,11},{9,8},{10,9... | collective-permute-start | bytes 442376 | tf_op jit(solution)/shard_map/ppermute | solution.py:492
  101.9 0.2 collective-permute-done.5.b
  102.1 0.0 collective-permute-done.6.c
  102.2 1.3 %first_sum.1 = (bf16[144,512]{1,0:T(8,128)(2,1)S(1)}, bf16[144,512]{1,0:T(8,128)(2,1)S(1)}, bf16[144,512]{1,0:T(8,128)(2,1)S(1)}, bf16[144,512]{1,0:T(8,128)(2,1)S(1)}) custom-call(s32[4]{0:T(128)S(1)} %copy-done.2, bf16[576,512]{1,0:T(8,128)(2,1)S(1)} %copy-done, bf16[576,512]{1,0:T(8,128)(2,1)S(1)} %collective-permute-done.5.b, ...), custom_call_target="tpu_custom_call" | custom-call | flops 1 | bytes 1769488 | tf_op jit(solution)/shard_map/first_sum/pallas_call | solution.py:416
  103.5 0.1 collective-permute-start.7
  103.5 4.7 %collective-permute-start.8 = (bf16[144,512]{1,0:T(8,128)(2,1)S(1)}, bf16[144,512]{1,0:T(8,128)(2,1)S(1)}, u32[]{:S(2)}, u32[]{:S(2)}) collective-permute-start(bf16[144,512]{1,0:T(8,128)(2,1)S(1)} %get-tuple-element.80), channel_id=1, source_target_pairs={{0,8},{4,12},{8,0},{12,4},{1,9},{5,13},{9,1},{13,5},{2,10},{6,14},... | collective-permute-start | bytes 442376 | tf_op jit(solution)/shard_map/ppermute | solution.py:492
  108.2 0.0 collective-permute-start.9
  108.2 0.0 collective-permute-done.18.c
  108.3 0.7 plane_sum_x.1
  108.9 0.6 collective-permute-start.20
  109.5 2.8 %collective-permute-start.21 = (bf16[36,512]{1,0:T(8,128)(2,1)S(1)}, bf16[36,512]{1,0:T(8,128)(2,1)S(1)}, u32[]{:S(2)}, u32[]{:S(2)}) collective-permute-start(bf16[36,512]{1,0:T(8,128)(2,1)S(1)} %get-tuple-element.99), channel_id=1, source_target_pairs={{0,64},{32,96},{64,0},{96,32},{1,65},{33,97},{65,1},{97,33},{2,66}... | collective-permute-start | bytes 110600 | tf_op jit(solution)/shard_map/ppermute | solution.py:492
  112.3 0.0 collective-permute-done.7.b
  112.3 2.5 %collective-permute-start.22 = (bf16[36,512]{1,0:T(8,128)(2,1)S(1)}, bf16[36,512]{1,0:T(8,128)(2,1)S(1)}, u32[]{:S(2)}, u32[]{:S(2)}) collective-permute-start(bf16[36,512]{1,0:T(8,128)(2,1)S(1)} %get-tuple-element.100), channel_id=1, source_target_pairs={{0,96},{32,0},{64,32},{96,64},{1,97},{33,1},{65,33},{97,65},{2,98}... | collective-permute-start | bytes 110600 | tf_op jit(solution)/shard_map/ppermute | solution.py:492
  114.8 0.0 collective-permute-done.8.c
  114.8 0.0 collective-permute-done.9.d
  114.8 0.7 plane_sum_z.1
  115.5 1.7 %collective-permute-start.10 = (bf16[36,512]{1,0:T(8,128)(2,1)S(1)}, bf16[36,512]{1,0:T(8,128)(2,1)S(1)}, u32[]{:S(2)}, u32[]{:S(2)}) collective-permute-start(bf16[36,512]{1,0:T(8,128)(2,1)S(1)} %get-tuple-element.83), channel_id=1, source_target_pairs={{0,1},{1,2},{2,3},{3,0},{4,5},{5,6},{6,7},{7,4},{8,9},{9,10},{10,1... | collective-permute-start | bytes 110600 | tf_op jit(solution)/shard_map/ppermute | solution.py:492
  117.2 2.7 %collective-permute-start.11 = (bf16[36,512]{1,0:T(8,128)(2,1)S(1)}, bf16[36,512]{1,0:T(8,128)(2,1)S(1)}, u32[]{:S(2)}, u32[]{:S(2)}) collective-permute-start(bf16[36,512]{1,0:T(8,128)(2,1)S(1)} %get-tuple-element.84), channel_id=1, source_target_pairs={{0,2},{1,3},{2,0},{3,1},{4,6},{5,7},{6,4},{7,5},{8,10},{9,11},{10,... | collective-permute-start | bytes 110600 | tf_op jit(solution)/shard_map/ppermute | solution.py:492
  119.9 0.0 collective-permute-done.20.b1
  119.9 1.5 %collective-permute-start.12 = (bf16[36,512]{1,0:T(8,128)(2,1)S(1)}, bf16[36,512]{1,0:T(8,128)(2,1)S(1)}, u32[]{:S(2)}, u32[]{:S(2)}) collective-permute-start(bf16[36,512]{1,0:T(8,128)(2,1)S(1)} %get-tuple-element.85), channel_id=1, source_target_pairs={{0,3},{1,0},{2,1},{3,2},{4,7},{5,4},{6,5},{7,6},{8,11},{9,8},{10,9... | collective-permute-start | bytes 110600 | tf_op jit(solution)/shard_map/ppermute | solution.py:492
  121.3 0.0 all-to-all-done.2.got_ref
  121.3 1.2 proj_total.1
  122.6 0.6 reduce
  123.2 0.0 collective-permute-done.21.b2
  123.2 0.0 collective-permute-done.22.b3
  123.2 0.0 collective-permute-done.11.a2
  123.2 0.7 collective-permute-done.12.a3
  123.9 1.2 conv_total.1
  (23 shorter events, 0.1 us)
Async XLA Ops:
  0.6 45.2 %all-to-all-start = ((bf16[16,64,1280]{2,1,0:T(8,128)(2,1)}), bf16[16,64,1280]{2,1,0:T(8,128)(2,1)S(1)}, u32[]{:S(2)}, u32[]{:S(2)}) async-start(bf16[16,64,1280]{2,1,0:T(8,128)(2,1)} %bitcast.9), calls=%async_computation | async-start | bytes 5242880 | tf_op jit(solution)/shard_map/all_to_all | solution.py:499
  10.1 18.6 %copy-start.4 = (f32[1280]{0:T(1024)S(1)}, f32[1280]{0:T(1024)}, u32[]{:S(2)}) copy-start(f32[1280]{0:T(1024)} %param.10) | copy-start | bytes 15364
  10.1 35.8 %copy-start.3 = (s32[8,1]{0,1:T(1,128)S(1)}, s32[8,1]{0,1:T(1,128)}, u32[]{:S(2)}) copy-start(s32[8,1]{0,1:T(1,128)} %param.13) | copy-start | bytes 100
  28.6 20.9 %collective-permute-start = (bf16[2816,512]{1,0:T(8,128)(2,1)}, bf16[2816,512]{1,0:T(8,128)(2,1)}, u32[]{:S(2)}, u32[]{:S(2)}) collective-permute-start(bf16[2816,512]{1,0:T(8,128)(2,1)} %get-tuple-element.54), channel_id=1, source_target_pairs={{0,16},{16,0},{1,17},{17,1},{2,18},{18,2},{3,19},{19,3},{4,20},{20... | collective-permute-start | bytes 8650760 | tf_op jit(solution)/shard_map/ppermute | solution.py:503
  45.9 3.7 %copy-start.2 = (s32[4]{0:T(128)S(1)}, s32[4]{0:T(128)}, u32[]{:S(2)}) copy-start(s32[4]{0:T(128)} %pad_add_fusion.core_ref.pos_ref) | copy-start | bytes 52
  48.9 3.7 %collective-permute-start.1 = (bf16[512,1280]{1,0:T(8,128)(2,1)S(1)}, bf16[512,1280]{1,0:T(8,128)(2,1)S(1)}, u32[]{:S(2)}, u32[]{:S(2)}) collective-permute-start(bf16[512,1280]{1,0:T(8,128)(2,1)S(1)} %get-tuple-element.57.grad_ref.gown), channel_id=1, source_target_pairs={{0,16},{16,0},{1,17},{17,1},{2,18},{18,2},{3,19},{19,3},{4,20},{20... | collective-permute-start | bytes 3932168 | tf_op jit(solution)/shard_map/ppermute | solution.py:505
  49.0 3.6 %collective-permute-start.2 = (f32[8,1280]{1,0:T(8,128)S(1)}, f32[8,1280]{1,0:T(8,128)S(1)}, u32[]{:S(2)}, u32[]{:S(2)}) collective-permute-start(f32[8,1280]{1,0:T(8,128)S(1)} %get-tuple-element.67.gain_own), channel_id=1, source_target_pairs={{0,16},{16,0},{1,17},{17,1},{2,18},{18,2},{3,19},{19,3},{4,20},{20... | collective-permute-start | bytes 122888 | tf_op jit(solution)/shard_map/ppermute | solution.py:505
  58.2 3.7 %copy-start.6 = (bf16[288,512]{1,0:T(8,128)(2,1)S(1)}, bf16[288,512]{1,0:T(8,128)(2,1)}, u32[]{:S(2)}) copy-start(bf16[288,512]{1,0:T(8,128)(2,1)} %get-tuple-element.74) | copy-start | bytes 884740
  58.2 5.3 %copy-start.5 = (bf16[288,512]{1,0:T(8,128)(2,1)S(1)}, bf16[288,512]{1,0:T(8,128)(2,1)}, u32[]{:S(2)}) copy-start(bf16[288,512]{1,0:T(8,128)(2,1)} %get-tuple-element.75) | copy-start | bytes 884740
  58.2 7.0 %copy-start.8 = (bf16[288,512]{1,0:T(8,128)(2,1)S(1)}, bf16[288,512]{1,0:T(8,128)(2,1)}, u32[]{:S(2)}) copy-start(bf16[288,512]{1,0:T(8,128)(2,1)} %get-tuple-element.89) | copy-start | bytes 884740
  58.2 7.0 %copy-start.7 = (bf16[288,512]{1,0:T(8,128)(2,1)S(1)}, bf16[288,512]{1,0:T(8,128)(2,1)}, u32[]{:S(2)}) copy-start(bf16[288,512]{1,0:T(8,128)(2,1)} %get-tuple-element.90) | copy-start | bytes 884740
  58.2 28.5 %all-to-all-start.1 = ((bf16[4,144,1280]{2,1,0:T(8,128)(2,1)}), bf16[4,144,1280]{2,1,0:T(8,128)(2,1)S(1)}, u32[]{:S(2)}, u32[]{:S(2)}) async-start(bf16[4,144,1280]{2,1,0:T(8,128)(2,1)} %get-tuple-element.70.after), calls=%async_computation.1 | async-start | bytes 2949120 | tf_op jit(solution)/shard_map/all_to_all | solution.py:510
  61.9 19.6 %collective-permute-start.3 = (bf16[288,512]{1,0:T(8,128)(2,1)S(1)}, bf16[288,512]{1,0:T(8,128)(2,1)S(1)}, u32[]{:S(2)}, u32[]{:S(2)}) collective-permute-start(bf16[288,512]{1,0:T(8,128)(2,1)S(1)} %copy-done.6), channel_id=1, source_target_pairs={{0,32},{32,64},{64,96},{96,0},{1,33},{33,65},{65,97},{97,1},{2,34}... | collective-permute-start | bytes 884744 | tf_op jit(solution)/shard_map/ppermute | solution.py:381
  63.5 18.0 %collective-permute-start.4 = (bf16[288,512]{1,0:T(8,128)(2,1)S(1)}, bf16[288,512]{1,0:T(8,128)(2,1)S(1)}, u32[]{:S(2)}, u32[]{:S(2)}) collective-permute-start(bf16[288,512]{1,0:T(8,128)(2,1)S(1)} %copy-done.5), channel_id=1, source_target_pairs={{0,96},{32,0},{64,32},{96,64},{1,97},{33,1},{65,33},{97,65},{2,98}... | collective-permute-start | bytes 884744 | tf_op jit(solution)/shard_map/ppermute | solution.py:382
  65.2 11.0 %collective-permute-start.13 = (bf16[288,512]{1,0:T(8,128)(2,1)S(1)}, bf16[288,512]{1,0:T(8,128)(2,1)S(1)}, u32[]{:S(2)}, u32[]{:S(2)}) collective-permute-start(bf16[288,512]{1,0:T(8,128)(2,1)S(1)} %copy-done.8), channel_id=1, source_target_pairs={{0,4},{4,8},{8,12},{12,0},{1,5},{5,9},{9,13},{13,1},{2,6},{6,10},{... | collective-permute-start | bytes 884744 | tf_op jit(solution)/shard_map/ppermute | solution.py:381
  65.2 11.0 %collective-permute-start.14 = (bf16[288,512]{1,0:T(8,128)(2,1)S(1)}, bf16[288,512]{1,0:T(8,128)(2,1)S(1)}, u32[]{:S(2)}, u32[]{:S(2)}) collective-permute-start(bf16[288,512]{1,0:T(8,128)(2,1)S(1)} %copy-done.7), channel_id=1, source_target_pairs={{0,12},{4,0},{8,4},{12,8},{1,13},{5,1},{9,5},{13,9},{2,14},{6,2},{... | collective-permute-start | bytes 884744 | tf_op jit(solution)/shard_map/ppermute | solution.py:382
  78.2 16.1 %copy-start.1 = (bf16[576,512]{1,0:T(8,128)(2,1)S(1)}, bf16[576,512]{1,0:T(8,128)(2,1)}, u32[]{:S(2)}) copy-start(bf16[576,512]{1,0:T(8,128)(2,1)} %get-tuple-element.86.a) | copy-start | bytes 1769476
  78.2 16.1 %collective-permute-start.15 = (bf16[576,512]{1,0:T(8,128)(2,1)}, bf16[576,512]{1,0:T(8,128)(2,1)}, u32[]{:S(2)}, u32[]{:S(2)}) collective-permute-start(bf16[576,512]{1,0:T(8,128)(2,1)} %get-tuple-element.91), channel_id=1, source_target_pairs={{0,4},{4,8},{8,12},{12,0},{1,5},{5,9},{9,13},{13,1},{2,6},{6,10},{... | collective-permute-start | bytes 1769480 | tf_op jit(solution)/shard_map/ppermute | solution.py:396
  78.3 16.0 %collective-permute-start.16 = (bf16[576,512]{1,0:T(8,128)(2,1)}, bf16[576,512]{1,0:T(8,128)(2,1)}, u32[]{:S(2)}, u32[]{:S(2)}) collective-permute-start(bf16[576,512]{1,0:T(8,128)(2,1)} %get-tuple-element.92), channel_id=1, source_target_pairs={{0,12},{4,0},{8,4},{12,8},{1,13},{5,1},{9,5},{13,9},{2,14},{6,2},{... | collective-permute-start | bytes 1769480 | tf_op jit(solution)/shard_map/ppermute | solution.py:396
  83.4 18.7 %copy-start = (bf16[576,512]{1,0:T(8,128)(2,1)S(1)}, bf16[576,512]{1,0:T(8,128)(2,1)}, u32[]{:S(2)}) copy-start(bf16[576,512]{1,0:T(8,128)(2,1)} %get-tuple-element.71.a) | copy-start | bytes 1769476
  83.5 18.7 %collective-permute-start.5 = (bf16[576,512]{1,0:T(8,128)(2,1)}, bf16[576,512]{1,0:T(8,128)(2,1)S(1)}, u32[]{:S(2)}, u32[]{:S(2)}) collective-permute-start(bf16[576,512]{1,0:T(8,128)(2,1)} %get-tuple-element.76), channel_id=1, source_target_pairs={{0,32},{32,64},{64,96},{96,0},{1,33},{33,65},{65,97},{97,1},{2,34}... | collective-permute-start | bytes 1769480 | tf_op jit(solution)/shard_map/ppermute | solution.py:396
  83.8 18.4 %collective-permute-start.6 = (bf16[576,512]{1,0:T(8,128)(2,1)}, bf16[576,512]{1,0:T(8,128)(2,1)}, u32[]{:S(2)}, u32[]{:S(2)}) collective-permute-start(bf16[576,512]{1,0:T(8,128)(2,1)} %get-tuple-element.77), channel_id=1, source_target_pairs={{0,96},{32,0},{64,32},{96,64},{1,97},{33,1},{65,33},{97,65},{2,98}... | collective-permute-start | bytes 1769480 | tf_op jit(solution)/shard_map/ppermute | solution.py:396
  88.5 32.9 %all-to-all-start.2 = ((bf16[16,16,896]{2,1,0:T(8,128)(2,1)}), bf16[16,16,896]{2,1,0:T(8,128)(2,1)S(1)}, u32[]{:S(2)}, u32[]{:S(2)}) async-start(bf16[16,16,896]{2,1,0:T(8,128)(2,1)} %proj_sum.1), calls=%async_computation.2 | async-start | bytes 917504 | tf_op jit(solution)/shard_map/all_to_all | solution.py:526
  96.1 12.1 %collective-permute-start.17 = (bf16[144,512]{1,0:T(8,128)(2,1)S(1)}, bf16[144,512]{1,0:T(8,128)(2,1)S(1)}, u32[]{:S(2)}, u32[]{:S(2)}) collective-permute-start(bf16[144,512]{1,0:T(8,128)(2,1)S(1)} %get-tuple-element.94), channel_id=1, source_target_pairs={{0,1},{1,2},{2,3},{3,0},{4,5},{5,6},{6,7},{7,4},{8,9},{9,10},{10,1... | collective-permute-start | bytes 442376 | tf_op jit(solution)/shard_map/ppermute | solution.py:492
  97.8 10.5 %collective-permute-start.18 = (bf16[144,512]{1,0:T(8,128)(2,1)S(1)}, bf16[144,512]{1,0:T(8,128)(2,1)S(1)}, u32[]{:S(2)}, u32[]{:S(2)}) collective-permute-start(bf16[144,512]{1,0:T(8,128)(2,1)S(1)} %get-tuple-element.95), channel_id=1, source_target_pairs={{0,2},{1,3},{2,0},{3,1},{4,6},{5,7},{6,4},{7,5},{8,10},{9,11},{10,... | collective-permute-start | bytes 442376 | tf_op jit(solution)/shard_map/ppermute | solution.py:492
  100.5 7.8 %collective-permute-start.19 = (bf16[144,512]{1,0:T(8,128)(2,1)S(1)}, bf16[144,512]{1,0:T(8,128)(2,1)S(1)}, u32[]{:S(2)}, u32[]{:S(2)}) collective-permute-start(bf16[144,512]{1,0:T(8,128)(2,1)S(1)} %get-tuple-element.96), channel_id=1, source_target_pairs={{0,3},{1,0},{2,1},{3,2},{4,7},{5,4},{6,5},{7,6},{8,11},{9,8},{10,9... | collective-permute-start | bytes 442376 | tf_op jit(solution)/shard_map/ppermute | solution.py:492
  103.5 8.9 %collective-permute-start.7 = (bf16[144,512]{1,0:T(8,128)(2,1)S(1)}, bf16[144,512]{1,0:T(8,128)(2,1)S(1)}, u32[]{:S(2)}, u32[]{:S(2)}) collective-permute-start(bf16[144,512]{1,0:T(8,128)(2,1)S(1)} %get-tuple-element.79), channel_id=1, source_target_pairs={{0,4},{4,8},{8,12},{12,0},{1,5},{5,9},{9,13},{13,1},{2,6},{6,10},{... | collective-permute-start | bytes 442376 | tf_op jit(solution)/shard_map/ppermute | solution.py:492
  103.5 11.3 %collective-permute-start.8 = (bf16[144,512]{1,0:T(8,128)(2,1)S(1)}, bf16[144,512]{1,0:T(8,128)(2,1)S(1)}, u32[]{:S(2)}, u32[]{:S(2)}) collective-permute-start(bf16[144,512]{1,0:T(8,128)(2,1)S(1)} %get-tuple-element.80), channel_id=1, source_target_pairs={{0,8},{4,12},{8,0},{12,4},{1,9},{5,13},{9,1},{13,5},{2,10},{6,14},... | collective-permute-start | bytes 442376 | tf_op jit(solution)/shard_map/ppermute | solution.py:492
  108.2 6.6 %collective-permute-start.9 = (bf16[144,512]{1,0:T(8,128)(2,1)S(1)}, bf16[144,512]{1,0:T(8,128)(2,1)S(1)}, u32[]{:S(2)}, u32[]{:S(2)}) collective-permute-start(bf16[144,512]{1,0:T(8,128)(2,1)S(1)} %get-tuple-element.81), channel_id=1, source_target_pairs={{0,12},{4,0},{8,4},{12,8},{1,13},{5,1},{9,5},{13,9},{2,14},{6,2},{... | collective-permute-start | bytes 442376 | tf_op jit(solution)/shard_map/ppermute | solution.py:492
  108.9 11.0 %collective-permute-start.20 = (bf16[36,512]{1,0:T(8,128)(2,1)S(1)}, bf16[36,512]{1,0:T(8,128)(2,1)S(1)}, u32[]{:S(2)}, u32[]{:S(2)}) collective-permute-start(bf16[36,512]{1,0:T(8,128)(2,1)S(1)} %get-tuple-element.98), channel_id=1, source_target_pairs={{0,32},{32,64},{64,96},{96,0},{1,33},{33,65},{65,97},{97,1},{2,34}... | collective-permute-start | bytes 110600 | tf_op jit(solution)/shard_map/ppermute | solution.py:492
  109.5 13.6 %collective-permute-start.21 = (bf16[36,512]{1,0:T(8,128)(2,1)S(1)}, bf16[36,512]{1,0:T(8,128)(2,1)S(1)}, u32[]{:S(2)}, u32[]{:S(2)}) collective-permute-start(bf16[36,512]{1,0:T(8,128)(2,1)S(1)} %get-tuple-element.99), channel_id=1, source_target_pairs={{0,64},{32,96},{64,0},{96,32},{1,65},{33,97},{65,1},{97,33},{2,66}... | collective-permute-start | bytes 110600 | tf_op jit(solution)/shard_map/ppermute | solution.py:492
  112.3 10.8 %collective-permute-start.22 = (bf16[36,512]{1,0:T(8,128)(2,1)S(1)}, bf16[36,512]{1,0:T(8,128)(2,1)S(1)}, u32[]{:S(2)}, u32[]{:S(2)}) collective-permute-start(bf16[36,512]{1,0:T(8,128)(2,1)S(1)} %get-tuple-element.100), channel_id=1, source_target_pairs={{0,96},{32,0},{64,32},{96,64},{1,97},{33,1},{65,33},{97,65},{2,98}... | collective-permute-start | bytes 110600 | tf_op jit(solution)/shard_map/ppermute | solution.py:492
  115.5 7.7 %collective-permute-start.10 = (bf16[36,512]{1,0:T(8,128)(2,1)S(1)}, bf16[36,512]{1,0:T(8,128)(2,1)S(1)}, u32[]{:S(2)}, u32[]{:S(2)}) collective-permute-start(bf16[36,512]{1,0:T(8,128)(2,1)S(1)} %get-tuple-element.83), channel_id=1, source_target_pairs={{0,1},{1,2},{2,3},{3,0},{4,5},{5,6},{6,7},{7,4},{8,9},{9,10},{10,1... | collective-permute-start | bytes 110600 | tf_op jit(solution)/shard_map/ppermute | solution.py:492
  117.2 6.0 %collective-permute-start.11 = (bf16[36,512]{1,0:T(8,128)(2,1)S(1)}, bf16[36,512]{1,0:T(8,128)(2,1)S(1)}, u32[]{:S(2)}, u32[]{:S(2)}) collective-permute-start(bf16[36,512]{1,0:T(8,128)(2,1)S(1)} %get-tuple-element.84), channel_id=1, source_target_pairs={{0,2},{1,3},{2,0},{3,1},{4,6},{5,7},{6,4},{7,5},{8,10},{9,11},{10,... | collective-permute-start | bytes 110600 | tf_op jit(solution)/shard_map/ppermute | solution.py:492
  119.9 4.0 %collective-permute-start.12 = (bf16[36,512]{1,0:T(8,128)(2,1)S(1)}, bf16[36,512]{1,0:T(8,128)(2,1)S(1)}, u32[]{:S(2)}, u32[]{:S(2)}) collective-permute-start(bf16[36,512]{1,0:T(8,128)(2,1)S(1)} %get-tuple-element.85), channel_id=1, source_target_pairs={{0,3},{1,0},{2,1},{3,2},{4,7},{5,4},{6,5},{7,6},{8,11},{9,8},{10,9... | collective-permute-start | bytes 110600 | tf_op jit(solution)/shard_map/ppermute | solution.py:492

commit v5 on v4

--- a/solution.py
+++ b/solution.py
@@ -30,7 +30,7 @@
 HROWS = XCONV // 2
 HALF = COUT // 2
 COST_ADD = 1
-COST_SUM = 1
+COST_SUM = 1000000000
 COST_PROJ = 20000000000
 COST_SECOND = 20000000000
 

time: 126 us -> 125 us (level)
  transfers between devices with their start and end apart: 26 -> 26, of which waited for: 4 -> 3; matrix products, arithmetic and copies ran while one was open for 1% -> 1% of each run, Pallas kernels for 35% -> 35%
where the time goes in v5:
time: 125 us; the launch traced here: 124 us
  starting transfers between devices  50.5 us (40%)
  Pallas kernels  49.9 us (40%)
  waiting for transfers between devices  20.2 us (16%)
  between operations  1.55 us (1%)
  other arithmetic  1.27 us (1%)
    ppermute x12, starting transfers between devices, turn(): lax.ppermute(parts[s], axis, [(i, (i + s) % 4) for i in range(4)])  21.4 us
    pallas_call x1, Pallas kernels, forward(): pl.pallas_call(forward_kernel, grid=(9,), in_specs=[smem, smem, pl.BlockS...  18.5 us
    all_to_all x1, waiting for transfers between devices, per_device(): lax.all_to_all(slab_cotangent.reshape(16, 64, DM), ('y', 'z'), 0, 0, tile...  17.2 us
    all_to_all x1, starting transfers between devices, per_device(): lax.all_to_all(slab_cotangent.reshape(16, 64, DM), ('y', 'z'), 0, 0, tile...  8.14 us
    pallas_call x7, Pallas kernels, small(): pl.pallas_call(kernel, in_specs=[SMEM_SPEC] + [VMEM_SPEC] * (len(args) -...  8.06 us
    pallas_call x1, Pallas kernels, conv_second(): pl.pallas_call(conv_second_kernel, in_specs=[SMEM_SPEC] + [HBM_SPEC] * 5,...  7.75 us
    ppermute x2, starting transfers between devices, finish(): lax.ppermute(other, axis, back)  6.19 us
    pallas_call x1, Pallas kernels, conv_first(): pl.pallas_call(conv_first_kernel, in_specs=[VMEM_SPEC] * 13, out_specs=[H...  5.48 us
  transfers between devices with their start and end apart: 26, of which 3 were waited for; matrix products, arithmetic and copies ran while one was open for 1% of the time, Pallas kernels for 35%

profile of v5, /device:TPU:0, one launch (start us, length us, event | category | flops | bytes accessed | tf_op | source)
XLA Modules:
  0.0 124.5 jit_solution(3269403584264980524)
XLA Ops:
  0.6 8.1 %all-to-all-start = ((bf16[16,64,1280]{2,1,0:T(8,128)(2,1)}), bf16[16,64,1280]{2,1,0:T(8,128)(2,1)S(1)}, u32[]{:S(2)}, u32[]{:S(2)}) async-start(bf16[16,64,1280]{2,1,0:T(8,128)(2,1)} %bitcast.9), calls=%async_computation | async-start | bytes 5242880 | tf_op jit(solution)/shard_map/all_to_all | solution.py:499
  9.4 0.7 pad_add_fusion.core_ref.pos_ref
  10.1 18.5 %forward.1 = (bf16[2816,512]{1,0:T(8,128)(2,1)}, bf16[2816,512]{1,0:T(8,128)(2,1)}, f32[512,1280]{1,0:T(8,128)}, bf16[1280,1024]{1,0:T(8,128)(2,1)}) custom-call(s32[4]{0:T(128)} %pad_add_fusion.core_ref.pos_ref, s32[1]{0:T(128)S(6)} %copy.18.pages_ref, bf16[2048,512]{1,0:T(8,128)(2,1)} %bitcast.11, bf16[4608,1024]{1,0:T(8,128)(2,1)} %w_ref.1, ...), custom_call_target="tpu_custom_call" | custom-call | flops 6200000000 | bytes 24000000 | tf_op jit(solution)/shard_map/forward/pallas_call | solution.py:112
  28.6 0.0 collective-permute-start
  28.7 17.2 %all-to-all-done.cot_ref = bf16[16,64,1280]{2,1,0:T(8,128)(2,1)S(1)} async-done(((bf16[16,64,1280]{2,1,0:T(8,128)(2,1)}), bf16[16,64,1280]{2,1,0:T(8,128)(2,1)S(1)}, u32[]{:S(2)}, u32[]{:S(2)}) %all-to-all-start) | async-done | bytes 2621472 | tf_op jit(solution)/shard_map/all_to_all | solution.py:499
  45.9 3.1 %norm_backward.1 = (bf16[512,1280]{1,0:T(8,128)(2,1)S(1)}, f32[8,1280]{1,0:T(8,128)S(1)}, bf16[1280,512]{1,0:T(8,128)(2,1)S(1)}) custom-call(s32[8]{0:T(128)S(1)} %bitcast.8, bf16[16,64,1280]{2,1,0:T(8,128)(2,1)S(1)} %all-to-all-done.cot_ref, f32[8,64,1280]{2,1,0:T(8,128)} %bitcast.10, f32[1,1280]{1,0:T(1,128)S(1)} %reshape.24.gain_ref, ...), custom_call_target="tpu_custom_call" | custom-call | flops 8000000 | bytes 8000000 | tf_op jit(solution)/shard_map/norm_backward/pallas_call | solution.py:177
  48.9 0.1 collective-permute-start.1
  49.0 0.5 collective-permute-start.2
  49.5 0.0 collective-permute-done.other_hbm
  49.5 3.1 %token_grad.1 = (bf16[512,1024]{1,0:T(8,128)(2,1)S(1)}, bf16[1280,512]{1,0:T(8,128)(2,1)S(1)}, bf16[576,512]{1,0:T(8,128)(2,1)S(1)}, bf16[576,512]{1,0:T(8,128)(...) custom-call(s32[4]{0:T(128)S(1)} %copy-done, ...), custom_call_target="tpu_custom_call" | custom-call | flops 1340000000 | bytes 8000000 | tf_op jit(solution)/shard_map/token_grad/pallas_call | solution.py:219
  52.7 0.0 collective-permute-done.2.gain_other
  52.7 0.0 collective-permute-done.1.gother
  52.7 5.5 %conv_first.1 = (bf16[288,512]{1,0:T(8,128)(2,1)}, bf16[288,512]{1,0:T(8,128)(2,1)}, bf16[288,512]{1,0:T(8,128)(2,1)}, bf16[288,512]{1,0:T(8,128)(2,1)}, bf16[51...) custom-call(bf16[512,1024]{1,0:T(8,128)(2,1)S(1)} %get-tuple-element.59.gtok, ...), custom_call_target="tpu_custom_call" | custom-call | flops 4000000000 | bytes 8000000 | tf_op jit(solution)/shard_map/conv_first/pallas_call | solution.py:276
  58.2 3.7 %all-to-all-start.1 = ((bf16[4,144,1280]{2,1,0:T(8,128)(2,1)}), bf16[4,144,1280]{2,1,0:T(8,128)(2,1)S(1)}, u32[]{:S(2)}, u32[]{:S(2)}) async-start(bf16[4,144,1280]{2,1,0:T(8,128)(2,1)} %get-tuple-element.70.after), calls=%async_computation.1 | async-start | bytes 2949120 | tf_op jit(solution)/shard_map/all_to_all | solution.py:510
  61.9 1.6 %collective-permute-start.3 = (bf16[288,512]{1,0:T(8,128)(2,1)S(1)}, bf16[288,512]{1,0:T(8,128)(2,1)S(1)}, u32[]{:S(2)}, u32[]{:S(2)}) collective-permute-start(bf16[288,512]{1,0:T(8,128)(2,1)S(1)} %copy-done.6), channel_id=1, source_target_pairs={{0,32},{32,64},{64,96},{96,0},{1,33},{33,65},{65,97},{97,1},{2,34}... | collective-permute-start | bytes 884744 | tf_op jit(solution)/shard_map/ppermute | solution.py:381
  63.5 1.7 %collective-permute-start.4 = (bf16[288,512]{1,0:T(8,128)(2,1)S(1)}, bf16[288,512]{1,0:T(8,128)(2,1)S(1)}, u32[]{:S(2)}, u32[]{:S(2)}) collective-permute-start(bf16[288,512]{1,0:T(8,128)(2,1)S(1)} %copy-done.5), channel_id=1, source_target_pairs={{0,96},{32,0},{64,32},{96,64},{1,97},{33,1},{65,33},{97,65},{2,98}... | collective-permute-start | bytes 884744 | tf_op jit(solution)/shard_map/ppermute | solution.py:382
  65.2 0.0 collective-permute-start.13
  65.2 3.2 %collective-permute-start.14 = (bf16[288,512]{1,0:T(8,128)(2,1)S(1)}, bf16[288,512]{1,0:T(8,128)(2,1)S(1)}, u32[]{:S(2)}, u32[]{:S(2)}) collective-permute-start(bf16[288,512]{1,0:T(8,128)(2,1)S(1)} %copy-done.7), channel_id=1, source_target_pairs={{0,12},{4,0},{8,4},{12,8},{1,13},{5,1},{9,5},{13,9},{2,14},{6,2},{... | collective-permute-start | bytes 884744 | tf_op jit(solution)/shard_map/ppermute | solution.py:382
  68.5 7.8 %conv_second.1 = (bf16[576,512]{1,0:T(8,128)(2,1)}, bf16[576,512]{1,0:T(8,128)(2,1)}, bf16[576,512]{1,0:T(8,128)(2,1)}, bf16[576,512]{1,0:T(8,128)(2,1)}, bf16[5...) custom-call(s32[4]{0:T(128)S(1)} %copy-done, bf16[2816,512]{1,0:T(8,128)(2,1)} %get-tuple-element.53.own_hbm, ...), custom_call_target="tpu_custom_call" | custom-call | flops 20000000000 | bytes 3000000 | tf_op jit(solution)/shard_map/conv_second/pallas_call | solution.py:337
  76.2 0.0 collective-permute-done.13.from_behind
  76.3 0.0 collective-permute-done.14.from_ahead
  76.3 1.9 %add_y.1 = (bf16[576,512]{1,0:T(8,128)(2,1)}, bf16[576,512]{1,0:T(8,128)(2,1)}) custom-call(bf16[576,512]{1,0:T(8,128)(2,1)} %get-tuple-element.87.ahead_in, bf16[576,512]{1,0:T(8,128)(2,1)} %get-tuple-element.88.behind_in, bf16[288,512]{1,0:T(8,128)(2,1)S(1)} %collective-permute-done.13.from_behind, ...), custom_call_target="tpu_custom_call", output_to_operand_aliasing={{0}: (0, {}), {1}: (1, {})} | custom-call | flops 1 | bytes 3000000 | tf_op jit(solution)/shard_map/add_y/pallas_call | solution.py:385
  78.2 0.1 collective-permute-start.15
  78.3 3.2 %collective-permute-start.16 = (bf16[576,512]{1,0:T(8,128)(2,1)}, bf16[576,512]{1,0:T(8,128)(2,1)}, u32[]{:S(2)}, u32[]{:S(2)}) collective-permute-start(bf16[576,512]{1,0:T(8,128)(2,1)} %get-tuple-element.92), channel_id=1, source_target_pairs={{0,12},{4,0},{8,4},{12,8},{1,13},{5,1},{9,5},{13,9},{2,14},{6,2},{... | collective-permute-start | bytes 1769480 | tf_op jit(solution)/shard_map/ppermute | solution.py:396
  81.5 0.0 collective-permute-done.3.from_behind
  81.5 0.0 collective-permute-done.4.from_ahead
  81.5 1.9 %add_x.1 = (bf16[576,512]{1,0:T(8,128)(2,1)}, bf16[576,512]{1,0:T(8,128)(2,1)}) custom-call(bf16[576,512]{1,0:T(8,128)(2,1)} %get-tuple-element.72.ahead_in, bf16[576,512]{1,0:T(8,128)(2,1)} %get-tuple-element.73.behind_in, bf16[288,512]{1,0:T(8,128)(2,1)S(1)} %collective-permute-done.3.from_behind, ...), custom_call_target="tpu_custom_call", output_to_operand_aliasing={{0}: (0, {}), {1}: (1, {})} | custom-call | flops 1 | bytes 3000000 | tf_op jit(solution)/shard_map/add_x/pallas_call | solution.py:385
  83.4 0.3 collective-permute-start.5
  83.8 3.0 %collective-permute-start.6 = (bf16[576,512]{1,0:T(8,128)(2,1)}, bf16[576,512]{1,0:T(8,128)(2,1)S(1)}, u32[]{:S(2)}, u32[]{:S(2)}) collective-permute-start(bf16[576,512]{1,0:T(8,128)(2,1)} %get-tuple-element.77), channel_id=1, source_target_pairs={{0,96},{32,0},{64,32},{96,64},{1,97},{33,1},{65,33},{97,65},{2,98}... | collective-permute-start | bytes 1769480 | tf_op jit(solution)/shard_map/ppermute | solution.py:396
  86.7 0.0 all-to-all-done.1.got_ref
  86.7 1.7 %proj_sum.1 = bf16[16,16,896]{2,1,0:T(8,128)(2,1)} custom-call(s32[4]{0:T(128)S(1)} %copy-done, bf16[4,144,1280]{2,1,0:T(8,128)(2,1)S(1)} %all-to-all-done.1.got_ref), custom_call_target="tpu_custom_call" | custom-call | flops 1000000 | bytes 1474576 | tf_op jit(solution)/shard_map/proj_sum/pallas_call | solution.py:416
  88.5 3.6 %all-to-all-start.2 = ((bf16[16,16,896]{2,1,0:T(8,128)(2,1)}), bf16[16,16,896]{2,1,0:T(8,128)(2,1)S(1)}, u32[]{:S(2)}, u32[]{:S(2)}) async-start(bf16[16,16,896]{2,1,0:T(8,128)(2,1)} %proj_sum.1), calls=%async_computation.2 | async-start | bytes 917504 | tf_op jit(solution)/shard_map/all_to_all | solution.py:526
  92.1 2.2 %collective-permute-done.15.b = bf16[576,512]{1,0:T(8,128)(2,1)} collective-permute-done((bf16[576,512]{1,0:T(8,128)(2,1)}, bf16[576,512]{1,0:T(8,128)(2,1)}, u32[]{:S(2)}, u32[]{:S(2)}) %collective-permute-start.15) | collective-permute-done | bytes 589856 | tf_op jit(solution)/shard_map/ppermute | solution.py:396
  94.3 0.0 collective-permute-done.16.c
  94.3 1.1 copy-done.3
  95.3 1.8 %second_sum.1 = (bf16[144,512]{1,0:T(8,128)(2,1)S(1)}, bf16[144,512]{1,0:T(8,128)(2,1)S(1)}, bf16[144,512]{1,0:T(8,128)(2,1)S(1)}, bf16[144,512]{1,0:T(8,128)(2,1)S(1)}) custom-call(s32[4]{0:T(128)S(1)} %copy-done, bf16[576,512]{1,0:T(8,128)(2,1)S(1)} %copy-done.3, bf16[576,512]{1,0:T(8,128)(2,1)} %collective-permute-done.15.b, ...), custom_call_target="tpu_custom_call" | custom-call | flops 1000000000 | bytes 1769488 | tf_op jit(solution)/shard_map/second_sum/pallas_call | solution.py:416
  97.1 1.7 %collective-permute-start.17 = (bf16[144,512]{1,0:T(8,128)(2,1)S(1)}, bf16[144,512]{1,0:T(8,128)(2,1)S(1)}, u32[]{:S(2)}, u32[]{:S(2)}) collective-permute-start(bf16[144,512]{1,0:T(8,128)(2,1)S(1)} %get-tuple-element.94), channel_id=1, source_target_pairs={{0,1},{1,2},{2,3},{3,0},{4,5},{5,6},{6,7},{7,4},{8,9},{9,10},{10,1... | collective-permute-start | bytes 442376 | tf_op jit(solution)/shard_map/ppermute | solution.py:492
  98.8 2.7 %collective-permute-start.18 = (bf16[144,512]{1,0:T(8,128)(2,1)S(1)}, bf16[144,512]{1,0:T(8,128)(2,1)S(1)}, u32[]{:S(2)}, u32[]{:S(2)}) collective-permute-start(bf16[144,512]{1,0:T(8,128)(2,1)S(1)} %get-tuple-element.95), channel_id=1, source_target_pairs={{0,2},{1,3},{2,0},{3,1},{4,6},{5,7},{6,4},{7,5},{8,10},{9,11},{10,... | collective-permute-start | bytes 442376 | tf_op jit(solution)/shard_map/ppermute | solution.py:492
  101.5 1.5 %collective-permute-start.19 = (bf16[144,512]{1,0:T(8,128)(2,1)S(1)}, bf16[144,512]{1,0:T(8,128)(2,1)S(1)}, u32[]{:S(2)}, u32[]{:S(2)}) collective-permute-start(bf16[144,512]{1,0:T(8,128)(2,1)S(1)} %get-tuple-element.96), channel_id=1, source_target_pairs={{0,3},{1,0},{2,1},{3,2},{4,7},{5,4},{6,5},{7,6},{8,11},{9,8},{10,9... | collective-permute-start | bytes 442376 | tf_op jit(solution)/shard_map/ppermute | solution.py:492
  103.0 0.0 collective-permute-done.6.c
  103.0 0.8 first_sum.1
  103.7 0.1 collective-permute-start.7
  103.8 4.9 %collective-permute-start.8 = (bf16[144,512]{1,0:T(8,128)(2,1)S(1)}, bf16[144,512]{1,0:T(8,128)(2,1)S(1)}, u32[]{:S(2)}, u32[]{:S(2)}) collective-permute-start(bf16[144,512]{1,0:T(8,128)(2,1)S(1)} %get-tuple-element.80), channel_id=1, source_target_pairs={{0,8},{4,12},{8,0},{12,4},{1,9},{5,13},{9,1},{13,5},{2,10},{6,14},... | collective-permute-start | bytes 442376 | tf_op jit(solution)/shard_map/ppermute | solution.py:492
  108.8 0.0 collective-permute-done.17.b
  108.8 0.0 collective-permute-start.9
  108.8 0.0 collective-permute-done.18.c
  108.8 0.7 plane_sum_x.1
  109.5 0.7 collective-permute-start.20
  110.2 2.7 %collective-permute-start.21 = (bf16[36,512]{1,0:T(8,128)(2,1)S(1)}, bf16[36,512]{1,0:T(8,128)(2,1)S(1)}, u32[]{:S(2)}, u32[]{:S(2)}) collective-permute-start(bf16[36,512]{1,0:T(8,128)(2,1)S(1)} %get-tuple-element.99), channel_id=1, source_target_pairs={{0,64},{32,96},{64,0},{96,32},{1,65},{33,97},{65,1},{97,33},{2,66}... | collective-permute-start | bytes 110600 | tf_op jit(solution)/shard_map/ppermute | solution.py:492
  112.8 0.0 collective-permute-done.7.b
  112.8 1.5 %collective-permute-start.22 = (bf16[36,512]{1,0:T(8,128)(2,1)S(1)}, bf16[36,512]{1,0:T(8,128)(2,1)S(1)}, u32[]{:S(2)}, u32[]{:S(2)}) collective-permute-start(bf16[36,512]{1,0:T(8,128)(2,1)S(1)} %get-tuple-element.100), channel_id=1, source_target_pairs={{0,96},{32,0},{64,32},{96,64},{1,97},{33,1},{65,33},{97,65},{2,98}... | collective-permute-start | bytes 110600 | tf_op jit(solution)/shard_map/ppermute | solution.py:492
  114.3 0.0 collective-permute-done.8.c
  114.3 0.0 collective-permute-done.9.d
  114.3 0.7 plane_sum_z.1
  115.0 1.6 %collective-permute-start.10 = (bf16[36,512]{1,0:T(8,128)(2,1)S(1)}, bf16[36,512]{1,0:T(8,128)(2,1)S(1)}, u32[]{:S(2)}, u32[]{:S(2)}) collective-permute-start(bf16[36,512]{1,0:T(8,128)(2,1)S(1)} %get-tuple-element.83), channel_id=1, source_target_pairs={{0,1},{1,2},{2,3},{3,0},{4,5},{5,6},{6,7},{7,4},{8,9},{9,10},{10,1... | collective-permute-start | bytes 110600 | tf_op jit(solution)/shard_map/ppermute | solution.py:492
  116.5 2.7 %collective-permute-start.11 = (bf16[36,512]{1,0:T(8,128)(2,1)S(1)}, bf16[36,512]{1,0:T(8,128)(2,1)S(1)}, u32[]{:S(2)}, u32[]{:S(2)}) collective-permute-start(bf16[36,512]{1,0:T(8,128)(2,1)S(1)} %get-tuple-element.84), channel_id=1, source_target_pairs={{0,2},{1,3},{2,0},{3,1},{4,6},{5,7},{6,4},{7,5},{8,10},{9,11},{10,... | collective-permute-start | bytes 110600 | tf_op jit(solution)/shard_map/ppermute | solution.py:492
  119.2 1.5 %collective-permute-start.12 = (bf16[36,512]{1,0:T(8,128)(2,1)S(1)}, bf16[36,512]{1,0:T(8,128)(2,1)S(1)}, u32[]{:S(2)}, u32[]{:S(2)}) collective-permute-start(bf16[36,512]{1,0:T(8,128)(2,1)S(1)} %get-tuple-element.85), channel_id=1, source_target_pairs={{0,3},{1,0},{2,1},{3,2},{4,7},{5,4},{6,5},{7,6},{8,11},{9,8},{10,9... | collective-permute-start | bytes 110600 | tf_op jit(solution)/shard_map/ppermute | solution.py:492
  120.7 1.2 proj_total.1
  121.9 0.6 reduce
  122.5 0.0 collective-permute-done.21.b2
  122.5 0.0 collective-permute-done.22.b3
  122.5 0.0 collective-permute-done.10.a1
  122.5 0.7 collective-permute-done.12.a3
  123.2 1.2 %conv_total.1 = f32[36,1024]{1,0:T(8,128)} custom-call(s32[4]{0:T(128)S(1)} %copy-done, bf16[36,512]{1,0:T(8,128)(2,1)S(1)} %get-tuple-element.82.a0, bf16[36,512]{1,0:T(8,128)(2,1)S(1)} %collective-permute-done.10.a1, bf16[36,512]{1,0:T(8,128)(2,1)S(1)} %collective-permute-done.11.a2, bf16[36,512]{1,0:T(8,128)(2,1)S(1)} %collective-permute-done.12.a3, ...), custom_call_target="tpu_custom_call" | custom-call | flops 1000000000 | bytes 294928 | tf_op jit(solution)/shard_map/conv_total/pallas_call | solution.py:416
  (23 shorter events, 0.1 us)
Async XLA Ops:
  0.6 45.2 %all-to-all-start = ((bf16[16,64,1280]{2,1,0:T(8,128)(2,1)}), bf16[16,64,1280]{2,1,0:T(8,128)(2,1)S(1)}, u32[]{:S(2)}, u32[]{:S(2)}) async-start(bf16[16,64,1280]{2,1,0:T(8,128)(2,1)} %bitcast.9), calls=%async_computation | async-start | bytes 5242880 | tf_op jit(solution)/shard_map/all_to_all | solution.py:499
  10.1 18.6 %copy-start.4 = (f32[1280]{0:T(1024)S(1)}, f32[1280]{0:T(1024)}, u32[]{:S(2)}) copy-start(f32[1280]{0:T(1024)} %param.10) | copy-start | bytes 15364
  10.1 35.8 %copy-start.1 = (s32[8,1]{0,1:T(1,128)S(1)}, s32[8,1]{0,1:T(1,128)}, u32[]{:S(2)}) copy-start(s32[8,1]{0,1:T(1,128)} %param.13) | copy-start | bytes 100
  28.6 20.9 %collective-permute-start = (bf16[2816,512]{1,0:T(8,128)(2,1)}, bf16[2816,512]{1,0:T(8,128)(2,1)}, u32[]{:S(2)}, u32[]{:S(2)}) collective-permute-start(bf16[2816,512]{1,0:T(8,128)(2,1)} %get-tuple-element.54), channel_id=1, source_target_pairs={{0,16},{16,0},{1,17},{17,1},{2,18},{18,2},{3,19},{19,3},{4,20},{20... | collective-permute-start | bytes 8650760 | tf_op jit(solution)/shard_map/ppermute | solution.py:503
  45.9 3.7 %copy-start = (s32[4]{0:T(128)S(1)}, s32[4]{0:T(128)}, u32[]{:S(2)}) copy-start(s32[4]{0:T(128)} %pad_add_fusion.core_ref.pos_ref) | copy-start | bytes 52
  48.9 3.7 %collective-permute-start.1 = (bf16[512,1280]{1,0:T(8,128)(2,1)S(1)}, bf16[512,1280]{1,0:T(8,128)(2,1)S(1)}, u32[]{:S(2)}, u32[]{:S(2)}) collective-permute-start(bf16[512,1280]{1,0:T(8,128)(2,1)S(1)} %get-tuple-element.57.grad_ref.gown), channel_id=1, source_target_pairs={{0,16},{16,0},{1,17},{17,1},{2,18},{18,2},{3,19},{19,3},{4,20},{20... | collective-permute-start | bytes 3932168 | tf_op jit(solution)/shard_map/ppermute | solution.py:505
  49.0 3.6 %collective-permute-start.2 = (f32[8,1280]{1,0:T(8,128)S(1)}, f32[8,1280]{1,0:T(8,128)S(1)}, u32[]{:S(2)}, u32[]{:S(2)}) collective-permute-start(f32[8,1280]{1,0:T(8,128)S(1)} %get-tuple-element.67.gain_own), channel_id=1, source_target_pairs={{0,16},{16,0},{1,17},{17,1},{2,18},{18,2},{3,19},{19,3},{4,20},{20... | collective-permute-start | bytes 122888 | tf_op jit(solution)/shard_map/ppermute | solution.py:505
  58.2 3.7 %copy-start.6 = (bf16[288,512]{1,0:T(8,128)(2,1)S(1)}, bf16[288,512]{1,0:T(8,128)(2,1)}, u32[]{:S(2)}) copy-start(bf16[288,512]{1,0:T(8,128)(2,1)} %get-tuple-element.74) | copy-start | bytes 884740
  58.2 5.3 %copy-start.5 = (bf16[288,512]{1,0:T(8,128)(2,1)S(1)}, bf16[288,512]{1,0:T(8,128)(2,1)}, u32[]{:S(2)}) copy-start(bf16[288,512]{1,0:T(8,128)(2,1)} %get-tuple-element.75) | copy-start | bytes 884740
  58.2 7.0 %copy-start.8 = (bf16[288,512]{1,0:T(8,128)(2,1)S(1)}, bf16[288,512]{1,0:T(8,128)(2,1)}, u32[]{:S(2)}) copy-start(bf16[288,512]{1,0:T(8,128)(2,1)} %get-tuple-element.89) | copy-start | bytes 884740
  58.2 7.0 %copy-start.7 = (bf16[288,512]{1,0:T(8,128)(2,1)S(1)}, bf16[288,512]{1,0:T(8,128)(2,1)}, u32[]{:S(2)}) copy-start(bf16[288,512]{1,0:T(8,128)(2,1)} %get-tuple-element.90) | copy-start | bytes 884740
  58.2 28.5 %all-to-all-start.1 = ((bf16[4,144,1280]{2,1,0:T(8,128)(2,1)}), bf16[4,144,1280]{2,1,0:T(8,128)(2,1)S(1)}, u32[]{:S(2)}, u32[]{:S(2)}) async-start(bf16[4,144,1280]{2,1,0:T(8,128)(2,1)} %get-tuple-element.70.after), calls=%async_computation.1 | async-start | bytes 2949120 | tf_op jit(solution)/shard_map/all_to_all | solution.py:510
  61.9 19.6 %collective-permute-start.3 = (bf16[288,512]{1,0:T(8,128)(2,1)S(1)}, bf16[288,512]{1,0:T(8,128)(2,1)S(1)}, u32[]{:S(2)}, u32[]{:S(2)}) collective-permute-start(bf16[288,512]{1,0:T(8,128)(2,1)S(1)} %copy-done.6), channel_id=1, source_target_pairs={{0,32},{32,64},{64,96},{96,0},{1,33},{33,65},{65,97},{97,1},{2,34}... | collective-permute-start | bytes 884744 | tf_op jit(solution)/shard_map/ppermute | solution.py:381
  63.5 18.0 %collective-permute-start.4 = (bf16[288,512]{1,0:T(8,128)(2,1)S(1)}, bf16[288,512]{1,0:T(8,128)(2,1)S(1)}, u32[]{:S(2)}, u32[]{:S(2)}) collective-permute-start(bf16[288,512]{1,0:T(8,128)(2,1)S(1)} %copy-done.5), channel_id=1, source_target_pairs={{0,96},{32,0},{64,32},{96,64},{1,97},{33,1},{65,33},{97,65},{2,98}... | collective-permute-start | bytes 884744 | tf_op jit(solution)/shard_map/ppermute | solution.py:382
  65.2 11.0 %collective-permute-start.13 = (bf16[288,512]{1,0:T(8,128)(2,1)S(1)}, bf16[288,512]{1,0:T(8,128)(2,1)S(1)}, u32[]{:S(2)}, u32[]{:S(2)}) collective-permute-start(bf16[288,512]{1,0:T(8,128)(2,1)S(1)} %copy-done.8), channel_id=1, source_target_pairs={{0,4},{4,8},{8,12},{12,0},{1,5},{5,9},{9,13},{13,1},{2,6},{6,10},{... | collective-permute-start | bytes 884744 | tf_op jit(solution)/shard_map/ppermute | solution.py:381
  65.2 11.0 %collective-permute-start.14 = (bf16[288,512]{1,0:T(8,128)(2,1)S(1)}, bf16[288,512]{1,0:T(8,128)(2,1)S(1)}, u32[]{:S(2)}, u32[]{:S(2)}) collective-permute-start(bf16[288,512]{1,0:T(8,128)(2,1)S(1)} %copy-done.7), channel_id=1, source_target_pairs={{0,12},{4,0},{8,4},{12,8},{1,13},{5,1},{9,5},{13,9},{2,14},{6,2},{... | collective-permute-start | bytes 884744 | tf_op jit(solution)/shard_map/ppermute | solution.py:382
  78.2 16.1 %collective-permute-start.15 = (bf16[576,512]{1,0:T(8,128)(2,1)}, bf16[576,512]{1,0:T(8,128)(2,1)}, u32[]{:S(2)}, u32[]{:S(2)}) collective-permute-start(bf16[576,512]{1,0:T(8,128)(2,1)} %get-tuple-element.91), channel_id=1, source_target_pairs={{0,4},{4,8},{8,12},{12,0},{1,5},{5,9},{9,13},{13,1},{2,6},{6,10},{... | collective-permute-start | bytes 1769480 | tf_op jit(solution)/shard_map/ppermute | solution.py:396
  78.3 16.0 %collective-permute-start.16 = (bf16[576,512]{1,0:T(8,128)(2,1)}, bf16[576,512]{1,0:T(8,128)(2,1)}, u32[]{:S(2)}, u32[]{:S(2)}) collective-permute-start(bf16[576,512]{1,0:T(8,128)(2,1)} %get-tuple-element.92), channel_id=1, source_target_pairs={{0,12},{4,0},{8,4},{12,8},{1,13},{5,1},{9,5},{13,9},{2,14},{6,2},{... | collective-permute-start | bytes 1769480 | tf_op jit(solution)/shard_map/ppermute | solution.py:396
  83.4 19.5 %collective-permute-start.5 = (bf16[576,512]{1,0:T(8,128)(2,1)}, bf16[576,512]{1,0:T(8,128)(2,1)S(1)}, u32[]{:S(2)}, u32[]{:S(2)}) collective-permute-start(bf16[576,512]{1,0:T(8,128)(2,1)} %get-tuple-element.76), channel_id=1, source_target_pairs={{0,32},{32,64},{64,96},{96,0},{1,33},{33,65},{65,97},{97,1},{2,34}... | collective-permute-start | bytes 1769480 | tf_op jit(solution)/shard_map/ppermute | solution.py:396
  83.8 19.2 %collective-permute-start.6 = (bf16[576,512]{1,0:T(8,128)(2,1)}, bf16[576,512]{1,0:T(8,128)(2,1)S(1)}, u32[]{:S(2)}, u32[]{:S(2)}) collective-permute-start(bf16[576,512]{1,0:T(8,128)(2,1)} %get-tuple-element.77), channel_id=1, source_target_pairs={{0,96},{32,0},{64,32},{96,64},{1,97},{33,1},{65,33},{97,65},{2,98}... | collective-permute-start | bytes 1769480 | tf_op jit(solution)/shard_map/ppermute | solution.py:396
  88.5 32.2 %all-to-all-start.2 = ((bf16[16,16,896]{2,1,0:T(8,128)(2,1)}), bf16[16,16,896]{2,1,0:T(8,128)(2,1)S(1)}, u32[]{:S(2)}, u32[]{:S(2)}) async-start(bf16[16,16,896]{2,1,0:T(8,128)(2,1)} %proj_sum.1), calls=%async_computation.2 | async-start | bytes 917504 | tf_op jit(solution)/shard_map/all_to_all | solution.py:526
  92.1 10.9 %copy-start.2 = (bf16[576,512]{1,0:T(8,128)(2,1)S(1)}, bf16[576,512]{1,0:T(8,128)(2,1)}, u32[]{:S(2)}) copy-start(bf16[576,512]{1,0:T(8,128)(2,1)} %get-tuple-element.71.a) | copy-start | bytes 1769476
  94.3 1.1 copy-start.3
  97.1 11.6 %collective-permute-start.17 = (bf16[144,512]{1,0:T(8,128)(2,1)S(1)}, bf16[144,512]{1,0:T(8,128)(2,1)S(1)}, u32[]{:S(2)}, u32[]{:S(2)}) collective-permute-start(bf16[144,512]{1,0:T(8,128)(2,1)S(1)} %get-tuple-element.94), channel_id=1, source_target_pairs={{0,1},{1,2},{2,3},{3,0},{4,5},{5,6},{6,7},{7,4},{8,9},{9,10},{10,1... | collective-permute-start | bytes 442376 | tf_op jit(solution)/shard_map/ppermute | solution.py:492
  98.8 9.9 %collective-permute-start.18 = (bf16[144,512]{1,0:T(8,128)(2,1)S(1)}, bf16[144,512]{1,0:T(8,128)(2,1)S(1)}, u32[]{:S(2)}, u32[]{:S(2)}) collective-permute-start(bf16[144,512]{1,0:T(8,128)(2,1)S(1)} %get-tuple-element.95), channel_id=1, source_target_pairs={{0,2},{1,3},{2,0},{3,1},{4,6},{5,7},{6,4},{7,5},{8,10},{9,11},{10,... | collective-permute-start | bytes 442376 | tf_op jit(solution)/shard_map/ppermute | solution.py:492
  101.5 7.3 %collective-permute-start.19 = (bf16[144,512]{1,0:T(8,128)(2,1)S(1)}, bf16[144,512]{1,0:T(8,128)(2,1)S(1)}, u32[]{:S(2)}, u32[]{:S(2)}) collective-permute-start(bf16[144,512]{1,0:T(8,128)(2,1)S(1)} %get-tuple-element.96), channel_id=1, source_target_pairs={{0,3},{1,0},{2,1},{3,2},{4,7},{5,4},{6,5},{7,6},{8,11},{9,8},{10,9... | collective-permute-start | bytes 442376 | tf_op jit(solution)/shard_map/ppermute | solution.py:492
  103.7 9.1 %collective-permute-start.7 = (bf16[144,512]{1,0:T(8,128)(2,1)S(1)}, bf16[144,512]{1,0:T(8,128)(2,1)S(1)}, u32[]{:S(2)}, u32[]{:S(2)}) collective-permute-start(bf16[144,512]{1,0:T(8,128)(2,1)S(1)} %get-tuple-element.79), channel_id=1, source_target_pairs={{0,4},{4,8},{8,12},{12,0},{1,5},{5,9},{9,13},{13,1},{2,6},{6,10},{... | collective-permute-start | bytes 442376 | tf_op jit(solution)/shard_map/ppermute | solution.py:492
  103.8 10.5 %collective-permute-start.8 = (bf16[144,512]{1,0:T(8,128)(2,1)S(1)}, bf16[144,512]{1,0:T(8,128)(2,1)S(1)}, u32[]{:S(2)}, u32[]{:S(2)}) collective-permute-start(bf16[144,512]{1,0:T(8,128)(2,1)S(1)} %get-tuple-element.80), channel_id=1, source_target_pairs={{0,8},{4,12},{8,0},{12,4},{1,9},{5,13},{9,1},{13,5},{2,10},{6,14},... | collective-permute-start | bytes 442376 | tf_op jit(solution)/shard_map/ppermute | solution.py:492
  108.8 5.6 %collective-permute-start.9 = (bf16[144,512]{1,0:T(8,128)(2,1)S(1)}, bf16[144,512]{1,0:T(8,128)(2,1)S(1)}, u32[]{:S(2)}, u32[]{:S(2)}) collective-permute-start(bf16[144,512]{1,0:T(8,128)(2,1)S(1)} %get-tuple-element.81), channel_id=1, source_target_pairs={{0,12},{4,0},{8,4},{12,8},{1,13},{5,1},{9,5},{13,9},{2,14},{6,2},{... | collective-permute-start | bytes 442376 | tf_op jit(solution)/shard_map/ppermute | solution.py:492
  109.5 9.8 %collective-permute-start.20 = (bf16[36,512]{1,0:T(8,128)(2,1)S(1)}, bf16[36,512]{1,0:T(8,128)(2,1)S(1)}, u32[]{:S(2)}, u32[]{:S(2)}) collective-permute-start(bf16[36,512]{1,0:T(8,128)(2,1)S(1)} %get-tuple-element.98), channel_id=1, source_target_pairs={{0,32},{32,64},{64,96},{96,0},{1,33},{33,65},{65,97},{97,1},{2,34}... | collective-permute-start | bytes 110600 | tf_op jit(solution)/shard_map/ppermute | solution.py:492
  110.2 12.4 %collective-permute-start.21 = (bf16[36,512]{1,0:T(8,128)(2,1)S(1)}, bf16[36,512]{1,0:T(8,128)(2,1)S(1)}, u32[]{:S(2)}, u32[]{:S(2)}) collective-permute-start(bf16[36,512]{1,0:T(8,128)(2,1)S(1)} %get-tuple-element.99), channel_id=1, source_target_pairs={{0,64},{32,96},{64,0},{96,32},{1,65},{33,97},{65,1},{97,33},{2,66}... | collective-permute-start | bytes 110600 | tf_op jit(solution)/shard_map/ppermute | solution.py:492
  112.8 9.7 %collective-permute-start.22 = (bf16[36,512]{1,0:T(8,128)(2,1)S(1)}, bf16[36,512]{1,0:T(8,128)(2,1)S(1)}, u32[]{:S(2)}, u32[]{:S(2)}) collective-permute-start(bf16[36,512]{1,0:T(8,128)(2,1)S(1)} %get-tuple-element.100), channel_id=1, source_target_pairs={{0,96},{32,0},{64,32},{96,64},{1,97},{33,1},{65,33},{97,65},{2,98}... | collective-permute-start | bytes 110600 | tf_op jit(solution)/shard_map/ppermute | solution.py:492
  115.0 7.5 %collective-permute-start.10 = (bf16[36,512]{1,0:T(8,128)(2,1)S(1)}, bf16[36,512]{1,0:T(8,128)(2,1)S(1)}, u32[]{:S(2)}, u32[]{:S(2)}) collective-permute-start(bf16[36,512]{1,0:T(8,128)(2,1)S(1)} %get-tuple-element.83), channel_id=1, source_target_pairs={{0,1},{1,2},{2,3},{3,0},{4,5},{5,6},{6,7},{7,4},{8,9},{9,10},{10,1... | collective-permute-start | bytes 110600 | tf_op jit(solution)/shard_map/ppermute | solution.py:492
  116.5 6.0 %collective-permute-start.11 = (bf16[36,512]{1,0:T(8,128)(2,1)S(1)}, bf16[36,512]{1,0:T(8,128)(2,1)S(1)}, u32[]{:S(2)}, u32[]{:S(2)}) collective-permute-start(bf16[36,512]{1,0:T(8,128)(2,1)S(1)} %get-tuple-element.84), channel_id=1, source_target_pairs={{0,2},{1,3},{2,0},{3,1},{4,6},{5,7},{6,4},{7,5},{8,10},{9,11},{10,... | collective-permute-start | bytes 110600 | tf_op jit(solution)/shard_map/ppermute | solution.py:492
  119.2 4.0 %collective-permute-start.12 = (bf16[36,512]{1,0:T(8,128)(2,1)S(1)}, bf16[36,512]{1,0:T(8,128)(2,1)S(1)}, u32[]{:S(2)}, u32[]{:S(2)}) collective-permute-start(bf16[36,512]{1,0:T(8,128)(2,1)S(1)} %get-tuple-element.85), channel_id=1, source_target_pairs={{0,3},{1,0},{2,1},{3,2},{4,7},{5,4},{6,5},{7,6},{8,11},{9,8},{10,9... | collective-permute-start | bytes 110600 | tf_op jit(solution)/shard_map/ppermute | solution.py:492
